TPU v7x, 32 devices: a whole 2x2x4 slice. The times are simulated.
32 devices in a mesh: dp: 8 (over z, y), seq: 4 (over x, core).
Axes of the slice: x: 2, y: 2, z: 4, core: 2. Of those that a mesh axis runs over, the one named last changes fastest.
Arguments:
- tokens: bfloat16 [8, 1024, 1152], P('dp', 'seq'), may hold values from -6 to 6
- condition: bfloat16 [8, 1024, 1152], P('dp', 'seq'), may hold values from -6 to 6
- cotangent: bfloat16 [8, 1024, 1152], P('dp', 'seq'), may hold values from -6 to 6
- w_qkv: bfloat16 [1152, 3456], P('seq'), may hold values from -0.1875 to 0.1875
- w_out: bfloat16 [1152, 1152], P('seq'), may hold values from -3 to 3
- w_gate: bfloat16 [1152, 3072], P('seq'), may hold values from -0.1875 to 0.1875
- w_up: bfloat16 [1152, 3072], P('seq'), may hold values from -0.1875 to 0.1875
- w_down: bfloat16 [3072, 1152], P('seq'), may hold values from -0.109375 to 0.109375
- w_mod: bfloat16 [1152, 6912], P('seq'), may hold values from -0.1875 to 0.1875
- b_mod: float32 [6912], replicated, may hold values from -3 to 3
- q_gain: float32 [72], replicated, may hold values from 0.25 to 1.75
- k_gain: float32 [72], replicated, may hold values from 0.25 to 1.75
- noise_counts: int32 [4], replicated, may hold values from 1 to 4, 8 in all
- time_steps: int32 [8], P('dp'), may hold values from 0 to 999
- positions: int32 [2, 8, 1024], P(None, 'dp', 'seq'), may hold values from 0 to 62, as said below
Outputs:
- block_out: bfloat16 [8, 1024, 1152], P('dp', 'seq')
- grad_tokens: float32 [8, 1024, 1152], P('dp', 'seq')
- grad_condition: float32 [8, 1024, 1152], P('dp', 'seq')
- grad_w_qkv: float32 [1152, 3456], P(('dp', 'seq'))
- grad_w_out: float32 [1152, 1152], P(('dp', 'seq'))
- grad_w_gate: float32 [1152, 3072], P(('dp', 'seq'))
- grad_w_up: float32 [1152, 3072], P(('dp', 'seq'))
- grad_w_down: float32 [3072, 1152], P(('dp', 'seq'))
- grad_w_mod: float32 [1152, 6912], P(('dp', 'seq'))
- grad_b_mod: float32 [6912], P(('dp', 'seq'))
- grad_q_gain: float32 [72], replicated
- grad_k_gain: float32 [72], replicated
Inputs may be any that keep to these rules, and one draw needn't show every extreme that they name: Image m owns the next noise_counts[m] items in order, so the counts sum to 8. `positions`: each item's rows hold every cell of its 32 x 32 patch grid once, in an order of that item, rows and columns both shifted by an offset of that item of 0 to 31; some item has offset 0 and another offset 32 - 1.
All inputs are finite; a program needn't handle non-finite values.
Results may differ from a plain program's by a relative error of at most 0.014.
Values may be sent and summed in bfloat16 or wider, within the bound.
A program may use at most 448 MiB of HBM per device.

v0:
```python
import math

import jax
import jax.numpy as jnp
from jax import lax
from jax.sharding import PartitionSpec as P

HEADS = 16
HD = 72


EPSILON = 1e-06


def inverse_rms(values):
    return lax.rsqrt(jnp.mean(values * values, axis=-1, keepdims=True) + EPSILON)


def rms_back(grad_in, normed, inverse):
    return inverse * (grad_in - normed * jnp.mean(grad_in * normed, axis=-1, keepdims=True))


def silu_slope(values):
    logistic = jax.nn.sigmoid(values)
    return logistic * (1.0 + values * (1.0 - logistic))


def time_embed(steps, width):
    half_width = width // 2
    frequency = jnp.exp(-math.log(10000.0) * jnp.arange(half_width, dtype=jnp.float32) / half_width)
    angles = steps.astype(jnp.float32)[:, None] * frequency[None, :]
    return jnp.concatenate([jnp.cos(angles), jnp.sin(angles)], axis=-1)


def rope_tables(positions, head_size):
    quarter = head_size // 4
    frequency = jnp.exp(-math.log(10000.0) * jnp.arange(quarter, dtype=jnp.float32) / quarter)
    along_rows = positions[0].astype(jnp.float32)[..., None] * frequency
    along_cols = positions[1].astype(jnp.float32)[..., None] * frequency
    angles = jnp.concatenate([along_rows, along_rows, along_cols, along_cols], axis=-1)
    return (jnp.cos(angles)[..., None, :], jnp.sin(angles)[..., None, :])


def quarter_turn(values):
    first, second, third, fourth = jnp.split(values, 4, axis=-1)
    return jnp.concatenate([-second, first, -fourth, third], axis=-1)


def rotate_heads(values, cosine, sine):
    return values * cosine + quarter_turn(values) * sine


def unrotate(grad_in, cosine, sine):
    return grad_in * cosine - quarter_turn(grad_in * sine)


def matmul(left, right):
    return jnp.dot(left, right, preferred_element_type=jnp.float32)


def outer_sum(left, right):
    return jnp.einsum("ra,rb->ab", left, right, preferred_element_type=jnp.float32)


def times_transpose(left, right):
    return jnp.einsum("rb,ab->ra", left, right, preferred_element_type=jnp.float32)


def shards(
    tokens,
    condition,
    cotangent,
    w_qkv,
    w_out,
    w_gate,
    w_up,
    w_down,
    w_mod,
    b_mod,
    q_gain,
    k_gain,
    noise_counts,
    time_steps,
    positions,
):
    item_count, local_rows, width = tokens.shape
    total_rows = item_count * local_rows
    patches = local_rows * lax.axis_size("seq")
    head_shape = (item_count, local_rows, HEADS, HD)
    factor = HD ** (-0.5)
    weights_fwd = (
        lax.all_gather(w_qkv, "seq", axis=0, tiled=True),
        lax.all_gather(w_out, "seq", axis=0, tiled=True),
        lax.all_gather(w_gate, "seq", axis=0, tiled=True),
        lax.all_gather(w_up, "seq", axis=0, tiled=True),
        lax.all_gather(w_down, "seq", axis=0, tiled=True),
        lax.all_gather(w_mod, "seq", axis=0, tiled=True),
    )
    qkv_full, out_full, gate_full, up_full, down_full, mod_full = weights_fwd
    first_item = lax.axis_index("dp") * item_count
    item_ids = first_item + jnp.arange(item_count, dtype=jnp.int32)
    running = jnp.cumsum(noise_counts)
    image_ids = jnp.sum((running[None, :] <= item_ids[:, None]).astype(jnp.int32), axis=1)
    chosen = jnp.arange(noise_counts.shape[0], dtype=jnp.int32)[None, :] == image_ids[:, None]
    share = 1.0 / jnp.sum(jnp.where(chosen, noise_counts[None, :], 0), axis=1).astype(jnp.float32)
    condition_in = condition.astype(jnp.float32) + time_embed(time_steps, width)[:, None, :]
    condition_in = condition_in.reshape(total_rows, width)
    lifted_low = jax.nn.silu(condition_in).astype(jnp.bfloat16)
    modulation = matmul(lifted_low, mod_full) + b_mod
    shift_a, scale_a, gate_a, shift_b, scale_b, gate_b = jnp.split(modulation, 6, axis=-1)
    tokens_f = tokens.astype(jnp.float32).reshape(total_rows, width)
    inverse_a = inverse_rms(tokens_f)
    normed_a = tokens_f * inverse_a
    hidden_a = (normed_a * (1.0 + scale_a) + shift_a).astype(jnp.bfloat16)
    projected = matmul(hidden_a, qkv_full).reshape(item_count, local_rows, 3, HEADS, HD)
    cosine, sine = rope_tables(positions, HD)
    query_inv = inverse_rms(projected[:, :, 0])
    query_norm = projected[:, :, 0] * query_inv
    query_rows = rotate_heads(query_norm * q_gain, cosine, sine).astype(jnp.bfloat16)
    key_inv = inverse_rms(projected[:, :, 1])
    key_norm = projected[:, :, 1] * key_inv
    key_rows = rotate_heads(key_norm * k_gain, cosine, sine).astype(jnp.bfloat16)
    value_rows = projected[:, :, 2].astype(jnp.bfloat16)
    key_flat = key_rows.reshape(item_count, local_rows, width)
    value_flat = value_rows.reshape(item_count, local_rows, width)
    key_all, value_all = (
        lax.all_gather(key_flat, "seq", axis=1, tiled=True),
        lax.all_gather(value_flat, "seq", axis=1, tiled=True),
    )

    def attend_item(pieces):
        query_item, key_item, value_item = pieces
        key_heads = key_item.reshape(patches, HEADS, HD)
        value_heads = value_item.reshape(patches, HEADS, HD)
        scores = (
            jnp.einsum("qhd,khd->hqk", query_item, key_heads, preferred_element_type=jnp.float32)
            * factor
        )
        exp_scores = jnp.exp(scores)
        totals = jnp.sum(exp_scores, axis=-1, keepdims=True)
        weights_low = (exp_scores / totals).astype(jnp.bfloat16)
        mixed = jnp.einsum(
            "hqk,khd->qhd", weights_low, value_heads, preferred_element_type=jnp.float32
        )
        return (mixed.reshape(local_rows, width).astype(jnp.bfloat16), totals)

    attended, row_totals = lax.map(attend_item, (query_rows, key_all, value_all))
    attended = attended.reshape(total_rows, width)
    branch_a = matmul(attended, out_full)
    middle = tokens_f + gate_a * branch_a
    inverse_b = inverse_rms(middle)
    normed_b = middle * inverse_b
    hidden_b = (normed_b * (1.0 + scale_b) + shift_b).astype(jnp.bfloat16)
    gate_in = matmul(hidden_b, gate_full)
    up_in = matmul(hidden_b, up_full)
    activated = jax.nn.silu(gate_in)
    inner = (activated * up_in).astype(jnp.bfloat16)
    branch_b = matmul(inner, down_full)
    block_out = (
        (middle + gate_b * branch_b).astype(jnp.bfloat16).reshape(item_count, local_rows, width)
    )
    weights_back = (
        lax.all_gather(w_qkv, "seq", axis=0, tiled=True),
        lax.all_gather(w_out, "seq", axis=0, tiled=True),
        lax.all_gather(w_gate, "seq", axis=0, tiled=True),
        lax.all_gather(w_up, "seq", axis=0, tiled=True),
        lax.all_gather(w_down, "seq", axis=0, tiled=True),
        lax.all_gather(w_mod, "seq", axis=0, tiled=True),
    )
    key_back, value_back = (
        lax.all_gather(key_flat, "seq", axis=1, tiled=True),
        lax.all_gather(value_flat, "seq", axis=1, tiled=True),
    )
    qkv_back, out_back, gate_back, up_back, down_back, mod_back = weights_back
    grad_out = (cotangent.astype(jnp.float32) * share[:, None, None]).reshape(total_rows, width)
    grad_gate_b = grad_out * branch_b
    grad_branch_b = (grad_out * gate_b).astype(jnp.bfloat16)
    grad_w_down = outer_sum(inner, grad_branch_b)
    grad_inner = times_transpose(grad_branch_b, down_back)
    grad_gate_in = (grad_inner * up_in * silu_slope(gate_in)).astype(jnp.bfloat16)
    grad_up_in = (grad_inner * activated).astype(jnp.bfloat16)
    grad_w_gate = outer_sum(hidden_b, grad_gate_in)
    grad_w_up = outer_sum(hidden_b, grad_up_in)
    grad_hidden_b = times_transpose(grad_gate_in, gate_back) + times_transpose(grad_up_in, up_back)
    grad_middle = grad_out + rms_back(grad_hidden_b * (1.0 + scale_b), normed_b, inverse_b)
    grad_gate_a = grad_middle * branch_a
    grad_branch_a = (grad_middle * gate_a).astype(jnp.bfloat16)
    grad_w_out = outer_sum(attended, grad_branch_a)
    grad_attended = (
        times_transpose(grad_branch_a, out_back).astype(jnp.bfloat16).reshape(head_shape)
    )

    def attend_back(pieces):
        query_item, key_item, value_item, grad_item, totals = pieces
        key_heads = key_item.reshape(patches, HEADS, HD)
        value_heads = value_item.reshape(patches, HEADS, HD)
        scores = (
            jnp.einsum("qhd,khd->hqk", query_item, key_heads, preferred_element_type=jnp.float32)
            * factor
        )
        probs = jnp.exp(scores) / totals
        grad_probs = jnp.einsum(
            "qhd,khd->hqk", grad_item, value_heads, preferred_element_type=jnp.float32
        )
        row_inner = jnp.sum(probs * grad_probs, axis=-1, keepdims=True)
        grad_scores = (probs * (grad_probs - row_inner)).astype(jnp.bfloat16)
        query_term = (
            jnp.einsum("hqk,khd->qhd", grad_scores, key_heads, preferred_element_type=jnp.float32)
            * factor
        )
        key_term = (
            jnp.einsum("hqk,qhd->khd", grad_scores, query_item, preferred_element_type=jnp.float32)
            * factor
        )
        value_term = jnp.einsum(
            "hqk,qhd->khd",
            probs.astype(jnp.bfloat16),
            grad_item,
            preferred_element_type=jnp.float32,
        )
        return (query_term, key_term.reshape(patches, width), value_term.reshape(patches, width))

    grad_query, key_terms, value_terms = lax.map(
        attend_back, (query_rows, key_back, value_back, grad_attended, row_totals)
    )
    grad_key, grad_value = (
        lax.psum_scatter(
            key_terms.astype(jnp.bfloat16), "seq", scatter_dimension=1, tiled=True
        ).astype(jnp.float32),
        lax.psum_scatter(
            value_terms.astype(jnp.bfloat16), "seq", scatter_dimension=1, tiled=True
        ).astype(jnp.float32),
    )
    grad_query_norm = unrotate(grad_query, cosine, sine)
    grad_key_norm = unrotate(grad_key.reshape(head_shape), cosine, sine)
    grad_q_gain = jnp.sum(grad_query_norm * query_norm, axis=(0, 1, 2))
    grad_k_gain = jnp.sum(grad_key_norm * key_norm, axis=(0, 1, 2))
    grad_query_raw = rms_back(grad_query_norm * q_gain, query_norm, query_inv)
    grad_key_raw = rms_back(grad_key_norm * k_gain, key_norm, key_inv)
    grad_project = jnp.stack([grad_query_raw, grad_key_raw, grad_value.reshape(head_shape)], axis=2)
    grad_project = grad_project.reshape(total_rows, 3 * width).astype(jnp.bfloat16)
    grad_w_qkv = outer_sum(hidden_a, grad_project)
    grad_hidden_a = times_transpose(grad_project, qkv_back)
    grad_tokens = grad_middle + rms_back(grad_hidden_a * (1.0 + scale_a), normed_a, inverse_a)
    grad_mod_rows = jnp.concatenate(
        [
            grad_hidden_a,
            grad_hidden_a * normed_a,
            grad_gate_a,
            grad_hidden_b,
            grad_hidden_b * normed_b,
            grad_gate_b,
        ],
        axis=-1,
    ).astype(jnp.bfloat16)
    grad_b_mod = jnp.sum(grad_mod_rows, axis=0, dtype=jnp.float32)
    grad_w_mod = outer_sum(lifted_low, grad_mod_rows)
    grad_condition = times_transpose(grad_mod_rows, mod_back) * silu_slope(condition_in)
    sum_qkv, sum_out, sum_gate, sum_up, sum_down, sum_mod, sum_bias = (
        lax.psum_scatter(grad_w_qkv, ("dp", "seq"), scatter_dimension=0, tiled=True),
        lax.psum_scatter(grad_w_out, ("dp", "seq"), scatter_dimension=0, tiled=True),
        lax.psum_scatter(grad_w_gate, ("dp", "seq"), scatter_dimension=0, tiled=True),
        lax.psum_scatter(grad_w_up, ("dp", "seq"), scatter_dimension=0, tiled=True),
        lax.psum_scatter(grad_w_down, ("dp", "seq"), scatter_dimension=0, tiled=True),
        lax.psum_scatter(grad_w_mod, ("dp", "seq"), scatter_dimension=0, tiled=True),
        lax.psum_scatter(grad_b_mod, ("dp", "seq"), scatter_dimension=0, tiled=True),
    )
    sum_q_gain, sum_k_gain = lax.psum((grad_q_gain, grad_k_gain), ("dp", "seq"))
    out_shape = (item_count, local_rows, width)
    return (
        block_out,
        grad_tokens.reshape(out_shape),
        grad_condition.reshape(out_shape),
        sum_qkv,
        sum_out,
        sum_gate,
        sum_up,
        sum_down,
        sum_mod,
        sum_bias,
        sum_q_gain,
        sum_k_gain,
    )


def solution(mesh):
    placed = (
        P("dp", "seq", None),
        P("dp", "seq", None),
        P("dp", "seq", None),
        P("seq", None),
        P("seq", None),
        P("seq", None),
        P("seq", None),
        P("seq", None),
        P("seq", None),
        P(),
        P(),
        P(),
        P(),
        P("dp"),
        P(None, "dp", "seq"),
    )
    return jax.shard_map(
        shards,
        mesh=mesh,
        in_specs=placed,
        out_specs=(
            P("dp", "seq", None),
            P("dp", "seq", None),
            P("dp", "seq", None),
            P(("dp", "seq"), None),
            P(("dp", "seq"), None),
            P(("dp", "seq"), None),
            P(("dp", "seq"), None),
            P(("dp", "seq"), None),
            P(("dp", "seq"), None),
            P(("dp", "seq")),
            P(),
            P(),
        ),
        check_vma=False,
    )
```

profile of v0, /device:TPU:14, one launch (start us, length us, event | category | flops | bytes accessed | tf_op | source)
XLA Modules:
  0.0 2045.2 jit_solution(10666998439557659573)
XLA Ops:
  11.7 99.2 %all-gather.9.cloned.1.call-done = bf16[1152,6912]{1,0:T(8,128)(2,1)} async-done(((bf16[288,6912]{1,0:T(8,128)(2,1)}), bf16[1152,6912]{1,0:T(8,128)(2,1)}) %all-gather.9.cloned.1.call-update) | async-done | bytes 15925264 | tf_op jit(solution)/shard_map/all_gather | solution.py:97
  110.9 8.4 convolution_add_fusion
  123.8 44.5 %all-gather.11.cloned.1.call-done = bf16[1152,3456]{1,0:T(8,128)(2,1)} async-done(((bf16[288,3456]{1,0:T(8,128)(2,1)}), bf16[1152,3456]{1,0:T(8,128)(2,1)}) %all-gather.11.cloned.1.call-update) | async-done | bytes 7962640 | tf_op jit(solution)/shard_map/all_gather | solution.py:92
  168.3 6.8 fusion.83
  191.8 12.3 all-gather.15.cloned.1.call-done
  204.2 11.8 fusion.6
  216.0 14.6 all-gather.13.cloned.1.call-done
  230.5 9.5 fusion.20
  240.0 17.7 all-gather.17.cloned.1.call-done
  257.7 4.6 multiply_reduce_fusion.5
  266.6 43.4 %all-gather.19.cloned.1.call-done = bf16[1152,3072]{1,0:T(8,128)(2,1)} async-done(((bf16[288,3072]{1,0:T(8,128)(2,1)}), bf16[1152,3072]{1,0:T(8,128)(2,1)}) %all-gather.19.cloned.1.call-update) | async-done | bytes 7077904 | tf_op jit(solution)/shard_map/all_gather | solution.py:94
  310.0 7.1 fusion.84
  317.1 45.3 %all-gather.21.cloned.1.call-done = bf16[1152,3072]{1,0:T(8,128)(2,1)} async-done(((bf16[288,3072]{1,0:T(8,128)(2,1)}), bf16[1152,3072]{1,0:T(8,128)(2,1)}) %all-gather.21.cloned.1.call-update) | async-done | bytes 7077904 | tf_op jit(solution)/shard_map/all_gather | solution.py:95
  362.5 7.2 fusion.85
  369.6 45.3 %all-gather.23.cloned.1.call-done = bf16[3072,1152]{1,0:T(8,128)(2,1)} async-done(((bf16[768,1152]{1,0:T(8,128)(2,1)}), bf16[3072,1152]{1,0:T(8,128)(2,1)}) %all-gather.23.cloned.1.call-update) | async-done | bytes 7077904 | tf_op jit(solution)/shard_map/all_gather | solution.py:96
  414.9 7.9 multiply_convert_fusion.2
  422.9 6.9 fusion.87
  434.1 5.9 fusion.86
  446.8 12.6 multiply_reduce_fusion
  459.4 11.9 multiply_convert_fusion
  475.4 10.5 fusion.13
  486.2 6.9 convolution_bitcast_fusion
  499.8 7.1 fusion.91
  506.9 7.0 fusion.90
  513.9 8.1 fusion.92
  527.2 17.1 reduce-scatter.16.cloned.1.call-done
  546.0 7.8 fusion.25
  561.3 14.7 fusion.76
  576.0 579.2 %fusion.82 = (f32[40,3072]{1,0:T(8,128)}, f32[40,6912]{1,0:T(8,128)}) fusion(f32[1152,3072]{1,0:T(8,128)} %fusion.91, f32[1152,6912]{1,0:T(8,128)} %fusion.76), kind=kCustom, calls=%all-reduce-scatter.6 | all-reduce-scatter fusion | flops 12779521 | bytes 47603712
  1158.6 9.5 fusion.88
  1168.2 469.3 %fusion.81 = (f32[48,3456]{1,0:T(8,128)}, f32[48,1152]{1,0:T(8,128)}, f32[40,3072]{1,0:T(8,128)}) fusion(f32[1152,3456]{1,0:T(8,128)} %fusion.88, f32[1152,1152]{1,0:T(8,128)} %fusion.89, f32[1152,3072]{1,0:T(8,128)} %fusion.90), kind=kCustom, calls=%all-reduce-scatter.5 | all-reduce-scatter fusion | flops 11010050 | bytes 36765696
  1643.2 14.2 collective-permute-start.12
  1667.5 6.8 collective-permute-start.15
  1674.3 5.1 collective-permute-done.15
  1681.3 4.5 collective-permute-start.21
  1685.9 5.0 collective-permute-start.14
  1692.8 5.3 collective-permute-start.9
  1698.2 10.0 fusion.12
  1727.9 62.9 %all-reduce.11 = (f32[6912]{0:T(1024)S(1)}, f32[72]{0:T(128)}, f32[72]{0:T(128)}) all-reduce(f32[6912]{0:T(1024)} %convert_reduce_fusion, f32[72]{0:T(128)S(1)} %copy-done.65, f32[72]{0:T(128)S(1)} %reduce_sum.160), channel_id=10, replica_groups=mesh['dp'=8,'seq'=4] {'dp','seq'}, use_global_device_ids=true, to_apply=%region_22.23.clone | all-reduce | flops 7056 | bytes 56448
  1795.5 4.6 collective-permute-start.2
  1808.7 8.5 concatenate.110
  1817.8 14.3 concatenate.112
  1832.2 14.4 concatenate.111
  1860.3 17.6 collective-permute-done.4
  1886.1 53.4 %collective-permute-done.5 = f32[48,3456]{1,0:T(8,128)S(1)} collective-permute-done((f32[48,3456]{1,0:T(8,128)S(1)}, f32[48,3456]{1,0:T(8,128)S(1)}, u32[]{:S(2)}, u32[]{:S(2)}) %collective-permute-start.5) | collective-permute-done | bytes 663584
  1941.4 34.1 %collective-permute-done.6 = f32[48,3456]{1,0:T(8,128)} collective-permute-done((f32[48,3456]{1,0:T(8,128)S(1)}, f32[48,3456]{1,0:T(8,128)}, u32[]{:S(2)}, u32[]{:S(2)}) %collective-permute-start.6) | collective-permute-done | bytes 663584
  1975.4 36.2 %concatenate.109 = f32[420,3456]{1,0:T(8,128)} concatenate(f32[36,3456]{1,0:T(8,128)} %collective-permute-done.7, f32[48,3456]{1,0:T(8,128)} %collective-permute-done.6, f32[48,3456]{1,0:T(8,128)S(1)} %collective-permute-done.5, f32[48,3456]{1,0:T(8,128)} %collective-permute-done.4, f32[48,3456]{1,0:T(8,128)} %collective-permute-done.3, f32[48,3456]{1,0:T(8,128)} %collective-permute-done.2, ...), dimensions={0} | concatenate | bytes 11612160
  2013.6 22.5 %concatenate.113 = f32[164,6912]{1,0:T(8,128)} concatenate(f32[4,6912]{1,0:T(4,128)} %collective-permute-done.27, f32[40,6912]{1,0:T(8,128)} %collective-permute-done.26, f32[40,6912]{1,0:T(8,128)} %collective-permute-done.25, f32[40,6912]{1,0:T(8,128)S(1)} %collective-permute-done.24, f32[40,6912]{1,0:T(8,128)S(1)} %copy-done.19), dimensions={0} | concatenate | bytes 9068544
  (284 shorter events, 149.1 us)
Async XLA Ops:
  7.2 103.7 %all-gather.9.cloned.1.call-start = ((), (), s32[]{:S(2)}) async-start(), calls=%async_computation.3 | async-start | bytes 19906560 | tf_op jit(solution)/shard_map/all_gather | solution.py:97
  7.9 102.9 %copy-start.45 = (bf16[1,256,1152]{2,1,0:T(8,128)(2,1)S(1)}, bf16[1,256,1152]{2,1,0:T(8,128)(2,1)}, u32[]{:S(2)}) copy-start(bf16[1,256,1152]{2,1,0:T(8,128)(2,1)} %param.16) | copy-start | bytes 1769476
  8.0 102.9 %copy-start.69 = (f32[6912]{0:T(1024)S(1)}, f32[6912]{0:T(1024)}, u32[]{:S(2)}) copy-start(f32[6912]{0:T(1024)} %param.24) | copy-start | bytes 82948
  8.0 160.4 %all-gather.11.cloned.1.call-start = ((), (), s32[]{:S(2)}) async-start(), calls=%async_computation.4 | async-start | bytes 9953280 | tf_op jit(solution)/shard_map/all_gather | solution.py:92
  8.7 195.4 %all-gather.15.cloned.1.call-start = ((), (), s32[]{:S(2)}) async-start(), calls=%async_computation.6 | async-start | bytes 2949120 | tf_op jit(solution)/shard_map/all_gather | solution.py:127
  10.3 108.9 %copy-start.49 = (f32[1152]{0:T(1024)}, f32[1152]{0:T(1024)S(1)}, u32[]{:S(2)}) copy-start(f32[1152]{0:T(1024)S(1)} %maximum_reduce_fusion) | copy-start | bytes 13828
  11.7 107.6 %copy-start.53 = (f32[256]{0:T(256)}, f32[256]{0:T(256)S(1)}, u32[]{:S(2)}) copy-start(f32[256]{0:T(256)S(1)} %add_rsqrt_fusion.3) | copy-start | bytes 3076
  179.6 50.9 %all-gather.13.cloned.1.call-start = ((), (), s32[]{:S(2)}) async-start(), calls=%async_computation.5 | async-start | bytes 2949120 | tf_op jit(solution)/shard_map/all_gather | solution.py:128
  180.6 77.1 %all-gather.17.cloned.1.call-start = ((), (), s32[]{:S(2)}) async-start(), calls=%async_computation.7 | async-start | bytes 3317760 | tf_op jit(solution)/shard_map/all_gather | solution.py:93
  181.2 128.8 %all-gather.19.cloned.1.call-start = ((), (), s32[]{:S(2)}) async-start(), calls=%async_computation.8 | async-start | bytes 8847360 | tf_op jit(solution)/shard_map/all_gather | solution.py:94
  181.7 180.7 %all-gather.21.cloned.1.call-start = ((), (), s32[]{:S(2)}) async-start(), calls=%async_computation.9 | async-start | bytes 8847360 | tf_op jit(solution)/shard_map/all_gather | solution.py:95
  182.5 232.4 %all-gather.23.cloned.1.call-start = ((), (), s32[]{:S(2)}) async-start(), calls=%async_computation.10 | async-start | bytes 8847360 | tf_op jit(solution)/shard_map/all_gather | solution.py:96
  183.2 338.8 %reduce-scatter.14.cloned.1.call-start = ((), (), s32[]{:S(2)}) async-start(), calls=%async_computation.11 | async-start | bytes 2949120 | tf_op jit(solution)/shard_map/reduce_scatter | solution.py:227
  475.4 68.9 %reduce-scatter.16.cloned.1.call-start = ((), (), s32[]{:S(2)}) async-start(), calls=%async_computation.12 | async-start | bytes 2949120 | tf_op jit(solution)/shard_map/reduce_scatter | solution.py:230
  485.9 1552.6 %reduce-scatter.18.cloned.1.call-start = ((), (), s32[]{:S(2)}) async-start(), calls=%async_computation.13 | async-start | bytes 14598144 | tf_op jit(solution)/shard_map/reduce_scatter | solution.py:264
  1156.7 503.5 %collective-permute-start.23 = (f32[4,3072]{1,0:T(4,128)}, f32[4,3072]{1,0:T(4,128)}, u32[]{:S(2)}, u32[]{:S(2)}) collective-permute-start(f32[4,3072]{1,0:T(4,128)} %slice.29), channel_id=1, source_target_pairs={{0,4},{1,5},{2,6},{3,7},{4,8},{5,9},{6,10},{7,11},{8,12},{9,13},{1... | collective-permute-start | bytes 147464
  1637.5 43.8 %collective-permute-start.10 = (f32[48,1152]{1,0:T(8,128)}, f32[48,1152]{1,0:T(8,128)}, u32[]{:S(2)}, u32[]{:S(2)}) collective-permute-start(f32[48,1152]{1,0:T(8,128)} %get-tuple-element.68), channel_id=1, source_target_pairs={{0,3},{1,4},{2,5},{3,6},{4,7},{5,8},{6,9},{7,10},{8,11},{9,12},{10... | collective-permute-start | bytes 663560
  1639.4 46.5 %collective-permute-start.11 = (f32[48,1152]{1,0:T(8,128)}, f32[48,1152]{1,0:T(8,128)}, u32[]{:S(2)}, u32[]{:S(2)}) collective-permute-start(f32[48,1152]{1,0:T(8,128)} %get-tuple-element.68), channel_id=1, source_target_pairs={{0,4},{1,5},{2,6},{3,7},{4,8},{5,9},{6,10},{7,11},{8,12},{9,13},{1... | collective-permute-start | bytes 663560
  1643.2 47.7 %collective-permute-start.12 = (f32[48,1152]{1,0:T(8,128)}, f32[48,1152]{1,0:T(8,128)}, u32[]{:S(2)}, u32[]{:S(2)}) collective-permute-start(f32[48,1152]{1,0:T(8,128)} %get-tuple-element.68), channel_id=1, source_target_pairs={{0,5},{1,6},{2,7},{3,8},{4,9},{5,10},{6,11},{7,12},{8,13},{9,14},{... | collective-permute-start | bytes 663560
  1657.4 35.4 %collective-permute-start.13 = (f32[48,1152]{1,0:T(8,128)}, f32[48,1152]{1,0:T(8,128)}, u32[]{:S(2)}, u32[]{:S(2)}) collective-permute-start(f32[48,1152]{1,0:T(8,128)} %get-tuple-element.68), channel_id=1, source_target_pairs={{0,6},{1,7},{2,8},{3,9},{4,10},{5,11},{6,12},{7,13},{8,14},{9,15},... | collective-permute-start | bytes 663560
  1660.3 7.2 collective-permute-start.19
  1667.5 11.9 collective-permute-start.15
  1679.4 42.6 %collective-permute-start.20 = (f32[40,3072]{1,0:T(8,128)}, f32[40,3072]{1,0:T(8,128)}, u32[]{:S(2)}, u32[]{:S(2)}) collective-permute-start(f32[40,3072]{1,0:T(8,128)} %get-tuple-element.72), channel_id=1, source_target_pairs={{0,1},{1,2},{2,3},{3,4},{4,5},{5,6},{6,7},{7,8},{8,9},{9,10},{10,1... | collective-permute-start | bytes 1474568
  1681.3 43.4 %collective-permute-start.21 = (f32[40,3072]{1,0:T(8,128)}, f32[40,3072]{1,0:T(8,128)}, u32[]{:S(2)}, u32[]{:S(2)}) collective-permute-start(f32[40,3072]{1,0:T(8,128)} %get-tuple-element.72), channel_id=1, source_target_pairs={{0,2},{1,3},{2,4},{3,5},{4,6},{5,7},{6,8},{7,9},{8,10},{9,11},{10,... | collective-permute-start | bytes 1474568
  1685.9 29.3 %collective-permute-start.14 = (f32[48,1152]{1,0:T(8,128)}, f32[48,1152]{1,0:T(8,128)}, u32[]{:S(2)}, u32[]{:S(2)}) collective-permute-start(f32[48,1152]{1,0:T(8,128)} %get-tuple-element.68), channel_id=1, source_target_pairs={{0,7},{1,8},{2,9},{3,10},{4,11},{5,12},{6,13},{7,14},{8,15},{9,16}... | collective-permute-start | bytes 663560
  1690.9 26.2 %collective-permute-start.8 = (f32[48,1152]{1,0:T(8,128)}, f32[48,1152]{1,0:T(8,128)}, u32[]{:S(2)}, u32[]{:S(2)}) collective-permute-start(f32[48,1152]{1,0:T(8,128)} %get-tuple-element.68), channel_id=1, source_target_pairs={{0,1},{1,2},{2,3},{3,4},{4,5},{5,6},{6,7},{7,8},{8,9},{9,10},{10,1... | collective-permute-start | bytes 663560
  1692.8 26.3 %collective-permute-start.9 = (f32[48,1152]{1,0:T(8,128)}, f32[48,1152]{1,0:T(8,128)}, u32[]{:S(2)}, u32[]{:S(2)}) collective-permute-start(f32[48,1152]{1,0:T(8,128)} %get-tuple-element.68), channel_id=1, source_target_pairs={{0,2},{1,3},{2,4},{3,5},{4,6},{5,7},{6,8},{7,9},{8,10},{9,11},{10,... | collective-permute-start | bytes 663560
  1715.2 76.3 %copy-start.67 = (f32[256]{0:T(256)S(1)}, f32[256]{0:T(256)}, u32[]{:S(2)}) copy-start(f32[256]{0:T(256)} %get-tuple-element.124) | copy-start | bytes 3076
  1715.2 90.0 %copy-start.55 = (f32[256]{0:T(256)S(1)}, f32[256]{0:T(256)}, u32[]{:S(2)}) copy-start(f32[256]{0:T(256)} %copy-done.53) | copy-start | bytes 3076
  1715.2 76.3 %collective-permute-start.22 = (f32[40,3072]{1,0:T(8,128)}, f32[40,3072]{1,0:T(8,128)}, u32[]{:S(2)}, u32[]{:S(2)}) collective-permute-start(f32[40,3072]{1,0:T(8,128)} %get-tuple-element.72), channel_id=1, source_target_pairs={{0,3},{1,4},{2,5},{3,6},{4,7},{5,8},{6,9},{7,10},{8,11},{9,12},{10... | collective-permute-start | bytes 1474568
  1717.1 76.4 %collective-permute-start.16 = (f32[40,3072]{1,0:T(8,128)}, f32[40,3072]{1,0:T(8,128)}, u32[]{:S(2)}, u32[]{:S(2)}) collective-permute-start(f32[40,3072]{1,0:T(8,128)} %get-tuple-element.69), channel_id=1, source_target_pairs={{0,1},{1,2},{2,3},{3,4},{4,5},{5,6},{6,7},{7,8},{8,9},{9,10},{10,1... | collective-permute-start | bytes 1474568
  1719.2 76.3 %collective-permute-start.17 = (f32[40,3072]{1,0:T(8,128)}, f32[40,3072]{1,0:T(8,128)}, u32[]{:S(2)}, u32[]{:S(2)}) collective-permute-start(f32[40,3072]{1,0:T(8,128)} %get-tuple-element.69), channel_id=1, source_target_pairs={{0,2},{1,3},{2,4},{3,5},{4,6},{5,7},{6,8},{7,9},{8,10},{9,11},{10,... | collective-permute-start | bytes 1474568
  1722.0 78.0 %collective-permute-start.18 = (f32[40,3072]{1,0:T(8,128)}, f32[40,3072]{1,0:T(8,128)}, u32[]{:S(2)}, u32[]{:S(2)}) collective-permute-start(f32[40,3072]{1,0:T(8,128)} %get-tuple-element.69), channel_id=1, source_target_pairs={{0,3},{1,4},{2,5},{3,6},{4,7},{5,8},{6,9},{7,10},{8,11},{9,12},{10... | collective-permute-start | bytes 1474568
  1724.8 77.9 %collective-permute-start.7 = (f32[36,3456]{1,0:T(8,128)}, f32[36,3456]{1,0:T(8,128)}, u32[]{:S(2)}, u32[]{:S(2)}) collective-permute-start(f32[36,3456]{1,0:T(8,128)} %slice.26), channel_id=1, source_target_pairs={{0,8},{1,9},{2,10},{3,11},{4,12},{5,13},{6,14},{7,15},{8,16},{9,17... | collective-permute-start | bytes 1493000
  1791.5 17.2 copy-start.33
  1791.5 55.1 %collective-permute-start = (f32[48,3456]{1,0:T(8,128)}, f32[48,3456]{1,0:T(8,128)}, u32[]{:S(2)}, u32[]{:S(2)}) collective-permute-start(f32[48,3456]{1,0:T(8,128)} %get-tuple-element.67), channel_id=1, source_target_pairs={{0,1},{1,2},{2,3},{3,4},{4,5},{5,6},{6,7},{7,8},{8,9},{9,10},{10,1... | collective-permute-start | bytes 1990664
  1793.5 55.6 %collective-permute-start.1 = (f32[48,3456]{1,0:T(8,128)}, f32[48,3456]{1,0:T(8,128)}, u32[]{:S(2)}, u32[]{:S(2)}) collective-permute-start(f32[48,3456]{1,0:T(8,128)} %get-tuple-element.67), channel_id=1, source_target_pairs={{0,2},{1,3},{2,4},{3,5},{4,6},{5,7},{6,8},{7,9},{8,10},{9,11},{10,... | collective-permute-start | bytes 1990664
  1795.5 57.2 %collective-permute-start.2 = (f32[48,3456]{1,0:T(8,128)}, f32[48,3456]{1,0:T(8,128)}, u32[]{:S(2)}, u32[]{:S(2)}) collective-permute-start(f32[48,3456]{1,0:T(8,128)} %get-tuple-element.67), channel_id=1, source_target_pairs={{0,3},{1,4},{2,5},{3,6},{4,7},{5,8},{6,9},{7,10},{8,11},{9,12},{10... | collective-permute-start | bytes 1990664
  1800.1 58.3 %collective-permute-start.3 = (f32[48,3456]{1,0:T(8,128)}, f32[48,3456]{1,0:T(8,128)}, u32[]{:S(2)}, u32[]{:S(2)}) collective-permute-start(f32[48,3456]{1,0:T(8,128)} %get-tuple-element.67), channel_id=1, source_target_pairs={{0,4},{1,5},{2,6},{3,7},{4,8},{5,9},{6,10},{7,11},{8,12},{9,13},{1... | collective-permute-start | bytes 1990664
  1802.7 75.3 %collective-permute-start.4 = (f32[48,3456]{1,0:T(8,128)}, f32[48,3456]{1,0:T(8,128)}, u32[]{:S(2)}, u32[]{:S(2)}) collective-permute-start(f32[48,3456]{1,0:T(8,128)} %get-tuple-element.67), channel_id=1, source_target_pairs={{0,5},{1,6},{2,7},{3,8},{4,9},{5,10},{6,11},{7,12},{8,13},{9,14},{... | collective-permute-start | bytes 1990664
  1832.2 14.4 copy-start.19
  1832.2 26.2 %copy-start.15 = (f32[48,3456]{1,0:T(8,128)S(1)}, f32[48,3456]{1,0:T(8,128)}, u32[]{:S(2)}) copy-start(f32[48,3456]{1,0:T(8,128)} %get-tuple-element.67) | copy-start | bytes 1990660
  1846.6 167.0 %collective-permute-start.24 = (f32[40,6912]{1,0:T(8,128)S(1)}, f32[40,6912]{1,0:T(8,128)S(1)}, u32[]{:S(2)}, u32[]{:S(2)}) collective-permute-start(f32[40,6912]{1,0:T(8,128)S(1)} %copy-done.19), channel_id=1, source_target_pairs={{0,1},{1,2},{2,3},{3,4},{4,5},{5,6},{6,7},{7,8},{8,9},{9,10},{10,1... | collective-permute-start | bytes 3317768
  1849.2 164.4 %collective-permute-start.25 = (f32[40,6912]{1,0:T(8,128)S(1)}, f32[40,6912]{1,0:T(8,128)}, u32[]{:S(2)}, u32[]{:S(2)}) collective-permute-start(f32[40,6912]{1,0:T(8,128)S(1)} %copy-done.19), channel_id=1, source_target_pairs={{0,2},{1,3},{2,4},{3,5},{4,6},{5,7},{6,8},{7,9},{8,10},{9,11},{10,... | collective-permute-start | bytes 3317768
  1852.7 160.9 %collective-permute-start.26 = (f32[40,6912]{1,0:T(8,128)S(1)}, f32[40,6912]{1,0:T(8,128)}, u32[]{:S(2)}, u32[]{:S(2)}) collective-permute-start(f32[40,6912]{1,0:T(8,128)S(1)} %copy-done.19), channel_id=1, source_target_pairs={{0,3},{1,4},{2,5},{3,6},{4,7},{5,8},{6,9},{7,10},{8,11},{9,12},{10... | collective-permute-start | bytes 3317768
  1858.4 81.1 %collective-permute-start.5 = (f32[48,3456]{1,0:T(8,128)S(1)}, f32[48,3456]{1,0:T(8,128)S(1)}, u32[]{:S(2)}, u32[]{:S(2)}) collective-permute-start(f32[48,3456]{1,0:T(8,128)S(1)} %copy-done.15), channel_id=1, source_target_pairs={{0,6},{1,7},{2,8},{3,9},{4,10},{5,11},{6,12},{7,13},{8,14},{9,15},... | collective-permute-start | bytes 1990664
  1877.9 97.5 %collective-permute-start.6 = (f32[48,3456]{1,0:T(8,128)S(1)}, f32[48,3456]{1,0:T(8,128)}, u32[]{:S(2)}, u32[]{:S(2)}) collective-permute-start(f32[48,3456]{1,0:T(8,128)S(1)} %copy-done.15), channel_id=1, source_target_pairs={{0,7},{1,8},{2,9},{3,10},{4,11},{5,12},{6,13},{7,14},{8,15},{9,16}... | collective-permute-start | bytes 1990664
  1939.5 74.1 %collective-permute-start.27 = (f32[4,6912]{1,0:T(4,128)}, f32[4,6912]{1,0:T(4,128)}, u32[]{:S(2)}, u32[]{:S(2)}) collective-permute-start(f32[4,6912]{1,0:T(4,128)} %slice.30), channel_id=1, source_target_pairs={{0,4},{1,5},{2,6},{3,7},{4,8},{5,9},{6,10},{7,11},{8,12},{9,13},{1... | collective-permute-start | bytes 331784
  (63 other events, 244.0 us)
Sparse Core Ops, SparseCore 0:
  9.6 101.2 all-gather.8
  112.4 55.8 all-gather.10
  179.8 24.3 all-gather.14
  206.1 24.3 all-gather.12
  231.9 25.7 all-gather.16
  259.1 50.8 all-gather.18
  311.6 50.8 all-gather.20
  364.0 50.8 all-gather.22
  475.5 33.0 reduce-scatter.13
  511.2 33.0 reduce-scatter.15
  550.9 242.4 reduce-scatter.17
where the time goes:
time: 2060 us; the launch traced here: 2050 us
  blocking collectives  1110 us (54%)
  waiting for transfers between devices  460 us (22%)
  matrix products  183 us (9%)
  local copies, waits for them, and re-layouts  133 us (6%)
  starting transfers between devices  94.2 us (5%)
  other arithmetic  47.3 us (2%)
    unnamed x3, blocking collectives  1110 us
    unnamed x160, local copies, waits for them, and re-layouts  128 us
    unnamed x39, waiting for transfers between devices  121 us
    all_gather x1, waiting for transfers between devices, shards(): lax.all_gather(w_mod, 'seq', axis=0, tiled=True)  99.2 us
    unnamed x28, starting transfers between devices  93.3 us
    dot_general x6, matrix products, outer_sum(): jnp.einsum('ra,rb->ab', left, right, preferred_element_type=jnp.float32)  49.7 us
    all_gather x1, waiting for transfers between devices, shards(): lax.all_gather(w_up, 'seq', axis=0, tiled=True)  45.3 us
    all_gather x1, waiting for transfers between devices, shards(): lax.all_gather(w_down, 'seq', axis=0, tiled=True)  45.3 us
  transfers between devices with their start and end apart: 39, of which 15 were waited for; matrix products, arithmetic and copies ran while one was open for 65% of the time, Pallas kernels for 0%

commit v1 on v0

v1 whole, which is shorter than its diff:
```python
import math

import jax
import jax.numpy as jnp
from jax import lax
from jax.sharding import PartitionSpec as P

HEADS = 16
HD = 72
EPSILON = 1e-06
BF16 = jnp.bfloat16
F32 = jnp.float32


def inverse_rms(values):
    return lax.rsqrt(jnp.mean(values * values, axis=-1, keepdims=True) + EPSILON)


def rms_back(grad_in, normed, inverse):
    return inverse * (grad_in - normed * jnp.mean(grad_in * normed, axis=-1, keepdims=True))


def silu_slope(values):
    logistic = jax.nn.sigmoid(values)
    return logistic * (1.0 + values * (1.0 - logistic))


def time_embed(steps, width):
    half_width = width // 2
    frequency = jnp.exp(-math.log(10000.0) * jnp.arange(half_width, dtype=F32) / half_width)
    angles = steps.astype(F32)[:, None] * frequency[None, :]
    return jnp.concatenate([jnp.cos(angles), jnp.sin(angles)], axis=-1)


def rope_tables(positions, head_size):
    quarter = head_size // 4
    frequency = jnp.exp(-math.log(10000.0) * jnp.arange(quarter, dtype=F32) / quarter)
    along_rows = positions[0].astype(F32)[..., None] * frequency
    along_cols = positions[1].astype(F32)[..., None] * frequency
    angles = jnp.concatenate([along_rows, along_rows, along_cols, along_cols], axis=-1)
    return (jnp.cos(angles)[..., None, :], jnp.sin(angles)[..., None, :])


def quarter_turn(values):
    first, second, third, fourth = jnp.split(values, 4, axis=-1)
    return jnp.concatenate([-second, first, -fourth, third], axis=-1)


def rotate_heads(values, cosine, sine):
    return values * cosine + quarter_turn(values) * sine


def unrotate(grad_in, cosine, sine):
    return grad_in * cosine - quarter_turn(grad_in * sine)


def matmul(left, right):
    return jnp.dot(left, right, preferred_element_type=F32)


def outer_sum(left, right):
    return jnp.einsum("ra,rb->ab", left, right, preferred_element_type=F32)


def times_transpose(left, right):
    return jnp.einsum("rb,ab->ra", left, right, preferred_element_type=F32)


def gather_rows(values):
    return lax.all_gather(values, "seq", axis=0, tiled=True)


def scatter_rows(partial):
    return lax.psum_scatter(
        partial.astype(BF16), "seq", scatter_dimension=0, tiled=True
    ).astype(F32)


def rows_to_columns(values, blocks):
    rows, columns = values.shape
    ways = lax.axis_size("seq")
    values = values.reshape(rows, blocks, ways, columns // (blocks * ways))
    moved = lax.all_to_all(values, "seq", split_axis=2, concat_axis=0, tiled=True)
    return moved.reshape(rows * ways, columns // ways)


def columns_to_rows(values, blocks):
    rows, columns = values.shape
    ways = lax.axis_size("seq")
    values = values.reshape(rows, blocks, 1, columns // blocks)
    moved = lax.all_to_all(values, "seq", split_axis=0, concat_axis=2, tiled=True)
    return moved.reshape(rows // ways, columns * ways)


def sum_columns(partial, blocks):
    mine = lax.psum_scatter(partial.astype(BF16), "dp", scatter_dimension=0, tiled=True)
    return columns_to_rows(mine, blocks).astype(F32)


def sum_rows(partial):
    mine = lax.psum_scatter(partial.astype(BF16), "dp", scatter_dimension=0, tiled=True)
    n_dp, n_seq = lax.axis_size("dp"), lax.axis_size("seq")
    pairs = []
    for d in range(n_dp):
        for s in range(n_seq):
            pairs.append((d * n_seq + s, s * n_dp + d))
    return lax.ppermute(mine, ("dp", "seq"), pairs).astype(F32)


def shards(
    tokens,
    condition,
    cotangent,
    w_qkv,
    w_out,
    w_gate,
    w_up,
    w_down,
    w_mod,
    b_mod,
    q_gain,
    k_gain,
    noise_counts,
    time_steps,
    positions,
):
    local_rows, width = tokens.shape[1:]
    ways = lax.axis_size("seq")
    patches = local_rows * ways
    local_heads = HEADS // ways
    factor = HD ** (-0.5)
    mod_full = gather_rows(w_mod)
    qkv_cols = rows_to_columns(w_qkv, 3)
    gate_cols = rows_to_columns(w_gate, 1)
    up_cols = rows_to_columns(w_up, 1)
    all_positions = lax.all_gather(positions[:, 0], "seq", axis=1, tiled=True)
    cosine, sine = rope_tables(all_positions, HD)

    item = lax.axis_index("dp")
    running = jnp.cumsum(noise_counts)
    image_id = jnp.sum((running <= item).astype(jnp.int32))
    chosen = jnp.arange(noise_counts.shape[0], dtype=jnp.int32) == image_id
    share = 1.0 / jnp.sum(jnp.where(chosen, noise_counts, 0)).astype(F32)

    condition_in = condition[0].astype(F32) + time_embed(time_steps, width)
    lifted_low = jax.nn.silu(condition_in).astype(BF16)
    modulation = matmul(lifted_low, mod_full) + b_mod
    shift_a, scale_a, gate_a, shift_b, scale_b, gate_b = jnp.split(modulation, 6, axis=-1)
    tokens_f = tokens[0].astype(F32)
    inverse_a = inverse_rms(tokens_f)
    normed_a = tokens_f * inverse_a
    hidden_a = gather_rows((normed_a * (1.0 + scale_a) + shift_a).astype(BF16))
    lifted_full = gather_rows(lifted_low)
    grad_out = cotangent[0].astype(F32) * share
    grad_branch_b = gather_rows((grad_out * gate_b).astype(BF16))

    projected = matmul(hidden_a, qkv_cols).reshape(patches, 3, local_heads, HD)
    query_inv = inverse_rms(projected[:, 0])
    query_norm = projected[:, 0] * query_inv
    query_rows = rotate_heads(query_norm * q_gain, cosine, sine).astype(BF16)
    key_inv = inverse_rms(projected[:, 1])
    key_norm = projected[:, 1] * key_inv
    key_rows = rotate_heads(key_norm * k_gain, cosine, sine).astype(BF16)
    value_rows = projected[:, 2].astype(BF16)

    scores = jnp.einsum("qhd,khd->hqk", query_rows, key_rows, preferred_element_type=F32) * factor
    exp_scores = jnp.exp(scores)
    totals = jnp.sum(exp_scores, axis=-1, keepdims=True)
    weights_low = (exp_scores / totals).astype(BF16)
    mixed = jnp.einsum("hqk,khd->qhd", weights_low, value_rows, preferred_element_type=F32)
    attended = mixed.reshape(patches, local_heads * HD).astype(BF16)

    branch_a = scatter_rows(matmul(attended, w_out))
    middle = tokens_f + gate_a * branch_a
    inverse_b = inverse_rms(middle)
    normed_b = middle * inverse_b
    hidden_b = gather_rows((normed_b * (1.0 + scale_b) + shift_b).astype(BF16))
    gate_in = matmul(hidden_b, gate_cols)
    up_in = matmul(hidden_b, up_cols)
    activated = jax.nn.silu(gate_in)
    inner = (activated * up_in).astype(BF16)
    branch_b = scatter_rows(matmul(inner, w_down))
    block_out = (middle + gate_b * branch_b).astype(BF16)

    grad_gate_b = grad_out * branch_b
    grad_w_down = sum_rows(outer_sum(inner, grad_branch_b))
    grad_inner = times_transpose(grad_branch_b, w_down)
    grad_gate_in = (grad_inner * up_in * silu_slope(gate_in)).astype(BF16)
    grad_up_in = (grad_inner * activated).astype(BF16)
    grad_w_gate = sum_columns(outer_sum(hidden_b, grad_gate_in), 1)
    grad_w_up = sum_columns(outer_sum(hidden_b, grad_up_in), 1)
    grad_hidden_b = scatter_rows(
        times_transpose(grad_gate_in, gate_cols) + times_transpose(grad_up_in, up_cols)
    )
    grad_middle = grad_out + rms_back(grad_hidden_b * (1.0 + scale_b), normed_b, inverse_b)
    grad_gate_a = grad_middle * branch_a
    grad_branch_a = gather_rows((grad_middle * gate_a).astype(BF16))
    grad_w_out = sum_rows(outer_sum(attended, grad_branch_a))
    grad_attended = (
        times_transpose(grad_branch_a, w_out).astype(BF16).reshape(patches, local_heads, HD)
    )

    scores = jnp.einsum("qhd,khd->hqk", query_rows, key_rows, preferred_element_type=F32) * factor
    probs = jnp.exp(scores) / totals
    grad_probs = jnp.einsum("qhd,khd->hqk", grad_attended, value_rows, preferred_element_type=F32)
    row_inner = jnp.sum(probs * grad_probs, axis=-1, keepdims=True)
    grad_scores = (probs * (grad_probs - row_inner)).astype(BF16)
    grad_query = (
        jnp.einsum("hqk,khd->qhd", grad_scores, key_rows, preferred_element_type=F32) * factor
    )
    grad_key = (
        jnp.einsum("hqk,qhd->khd", grad_scores, query_rows, preferred_element_type=F32) * factor
    )
    grad_value = jnp.einsum(
        "hqk,qhd->khd", probs.astype(BF16), grad_attended, preferred_element_type=F32
    )
    grad_query_norm = unrotate(grad_query, cosine, sine)
    grad_key_norm = unrotate(grad_key, cosine, sine)
    grad_q_gain = jnp.sum(grad_query_norm * query_norm, axis=(0, 1))
    grad_k_gain = jnp.sum(grad_key_norm * key_norm, axis=(0, 1))
    grad_query_raw = rms_back(grad_query_norm * q_gain, query_norm, query_inv)
    grad_key_raw = rms_back(grad_key_norm * k_gain, key_norm, key_inv)
    grad_project = jnp.stack([grad_query_raw, grad_key_raw, grad_value], axis=1)
    grad_project = grad_project.reshape(patches, 3 * local_heads * HD).astype(BF16)
    grad_w_qkv = sum_columns(outer_sum(hidden_a, grad_project), 3)
    grad_hidden_a = scatter_rows(times_transpose(grad_project, qkv_cols))
    grad_tokens = grad_middle + rms_back(grad_hidden_a * (1.0 + scale_a), normed_a, inverse_a)
    grad_mod_rows = jnp.concatenate(
        [
            grad_hidden_a,
            grad_hidden_a * normed_a,
            grad_gate_a,
            grad_hidden_b,
            grad_hidden_b * normed_b,
            grad_gate_b,
        ],
        axis=-1,
    ).astype(BF16)
    grad_b_mod = jnp.sum(grad_mod_rows, axis=0, dtype=F32)
    grad_mod_cols = rows_to_columns(grad_mod_rows, 6)
    grad_w_mod = sum_columns(outer_sum(lifted_full, grad_mod_cols), 6)
    grad_condition = times_transpose(grad_mod_rows, mod_full) * silu_slope(condition_in)
    sum_bias = lax.psum_scatter(grad_b_mod, ("dp", "seq"), scatter_dimension=0, tiled=True)
    sum_q_gain, sum_k_gain = lax.psum((grad_q_gain, grad_k_gain), ("dp", "seq"))
    return (
        block_out[None],
        grad_tokens[None],
        grad_condition[None],
        grad_w_qkv,
        grad_w_out,
        grad_w_gate,
        grad_w_up,
        grad_w_down,
        grad_w_mod,
        sum_bias,
        sum_q_gain,
        sum_k_gain,
    )


def solution(mesh):
    placed = (
        P("dp", "seq", None),
        P("dp", "seq", None),
        P("dp", "seq", None),
        P("seq", None),
        P("seq", None),
        P("seq", None),
        P("seq", None),
        P("seq", None),
        P("seq", None),
        P(),
        P(),
        P(),
        P(),
        P("dp"),
        P(None, "dp", "seq"),
    )
    return jax.shard_map(
        shards,
        mesh=mesh,
        in_specs=placed,
        out_specs=(
            P("dp", "seq", None),
            P("dp", "seq", None),
            P("dp", "seq", None),
            P(("dp", "seq"), None),
            P(("dp", "seq"), None),
            P(("dp", "seq"), None),
            P(("dp", "seq"), None),
            P(("dp", "seq"), None),
            P(("dp", "seq"), None),
            P(("dp", "seq")),
            P(),
            P(),
        ),
        check_vma=False,
    )
```

time: 2060 us -> 973 us (0.47)
  the two profiles are of different devices: /device:TPU:14 before, /device:TPU:0 now
where the time goes in v1:
time: 973 us; the launch traced here: 967 us
  waiting for transfers between devices  478 us (49%)
  blocking collectives  156 us (16%)
  matrix products  137 us (14%)
  local copies, waits for them, and re-layouts  90.3 us (9%)
  other arithmetic  49.1 us (5%)
  starting transfers between devices  39.6 us (4%)
  between operations  17.2 us (2%)
    all_gather x6, waiting for transfers between devices, gather_rows(): return lax.all_gather(values, 'seq', axis=0, tiled=True)  128 us
    reduce_scatter x4, waiting for transfers between devices, sum_columns(): lax.psum_scatter(partial.astype(BF16), 'dp', scatter_dimension=0, tiled=T...  124 us
    reduce_scatter x4, waiting for transfers between devices, scatter_rows(): lax.psum_scatter(partial.astype(BF16), 'seq', scatter_dimension=0, tiled=...  99.2 us
    unnamed x2, blocking collectives  73 us
    reduce_scatter x1, waiting for transfers between devices, sum_rows(): lax.psum_scatter(partial.astype(BF16), 'dp', scatter_dimension=0, tiled=T...  66 us
    all_to_all x3, waiting for transfers between devices, rows_to_columns(): lax.all_to_all(values, 'seq', split_axis=2, concat_axis=0, tiled=True)  44.2 us
    all_to_all x1, blocking collectives, rows_to_columns(): lax.all_to_all(values, 'seq', split_axis=2, concat_axis=0, tiled=True)  43.8 us
    all_gather x1, blocking collectives, shards(): all_positions = lax.all_gather(positions[:, 0], 'seq', axis=1, tiled=True)  38.9 us
  transfers between devices with their start and end apart: 26, of which 16 were waited for; matrix products, arithmetic and copies ran while one was open for 19% of the time, Pallas kernels for 0%

profile of v1, /device:TPU:0, one launch (start us, length us, event | category | flops | bytes accessed | tf_op | source)
XLA Modules:
  0.0 966.8 jit_solution(11953099768202177205)
XLA Ops:
  9.8 103.6 %all-gather.8.cloned.1.call-done = bf16[1152,6912]{1,0:T(8,128)(2,1)} async-done(((bf16[288,6912]{1,0:T(8,128)(2,1)}), bf16[1152,6912]{1,0:T(8,128)(2,1)}) %all-gather.8.cloned.1.call-update) | async-done | bytes 15925264 | tf_op jit(solution)/shard_map/all_gather | solution.py:70
  113.4 8.4 convolution_add_fusion
  125.8 4.8 reshape.343
  130.5 3.7 copy.115
  134.2 4.7 all-to-all-start
  139.0 38.9 %all-gather = s32[2,1,1024]{2,1,0:T(1,128)S(1)} all-gather(s32[2,1,256]{2,1,0:T(1,128)S(1)} %copy-done.51), channel_id=2, replica_groups=mesh['dp'=8,'seq'=4] {'seq'}, dimensions={2}, use_global_device_ids=true | all-gather | bytes 10240 | tf_op jit(solution)/shard_map/all_gather | solution.py:136
  179.9 7.1 copy.116
  187.0 5.3 reshape.344
  192.3 4.8 fusion.9
  217.1 29.8 %reduce-scatter.12.cloned.1.call-done = bf16[256,1152]{1,0:T(8,128)(2,1)} async-done(((bf16[1024,1152]{1,0:T(8,128)(2,1)}), bf16[256,1152]{1,0:T(8,128)(2,1)}) %reduce-scatter.12.cloned.1.call-update) | async-done | bytes 589840 | tf_op jit(solution)/shard_map/reduce_scatter | solution.py:74
  253.0 4.4 reshape.347
  260.4 4.8 all-to-all-start.2
  265.2 4.4 reshape.345
  272.6 21.6 %all-to-all-done.2 = bf16[288,1,4,768]{3,0,1,2:T(8,128)(2,1)} async-done(((bf16[288,1,4,768]{3,0,1,2:T(8,128)(2,1)}), bf16[288,1,4,768]{3,0,1,2:T(8,128)(2,1)}, u32[]{:S(2)}, u32[]{:S(2)}) %all-to-all-start.2) | async-done | bytes 1769504 | tf_op jit(solution)/shard_map/all_to_all | solution.py:83
  294.2 4.4 all-to-all-start.1
  298.7 6.1 fusion.72
  304.8 22.7 %all-to-all-done.1 = bf16[288,1,4,768]{3,0,1,2:T(8,128)(2,1)} async-done(((bf16[288,1,4,768]{3,0,1,2:T(8,128)(2,1)}), bf16[288,1,4,768]{3,0,1,2:T(8,128)(2,1)}, u32[]{:S(2)}, u32[]{:S(2)}) %all-to-all-start.1) | async-done | bytes 1769504 | tf_op jit(solution)/shard_map/all_to_all | solution.py:83
  327.5 6.1 fusion.71
  333.5 7.8 multiply_convert_fusion.1
  341.4 4.8 fusion.73
  346.2 5.2 add_convert_fusion
  351.5 5.0 convolution_convert_fusion.2
  356.8 27.8 %reduce-scatter.16.cloned.1.call-done = bf16[256,1152]{1,0:T(8,128)(2,1)} async-done(((bf16[1024,1152]{1,0:T(8,128)(2,1)}), bf16[256,1152]{1,0:T(8,128)(2,1)}) %reduce-scatter.16.cloned.1.call-update) | async-done | bytes 589840 | tf_op jit(solution)/shard_map/reduce_scatter | solution.py:74
  386.4 33.8 %reduce-scatter.14.cloned.1.call-done = bf16[256,1152]{1,0:T(8,128)(2,1)} async-done(((bf16[1024,1152]{1,0:T(8,128)(2,1)}), bf16[256,1152]{1,0:T(8,128)(2,1)}) %reduce-scatter.14.cloned.1.call-update) | async-done | bytes 589840 | tf_op jit(solution)/shard_map/reduce_scatter | solution.py:74
  420.2 4.1 multiply_convert_fusion.4
  424.4 24.2 %all-gather.16.cloned.1.call-done = bf16[1024,1152]{1,0:T(8,128)(2,1)} async-done(((bf16[256,1152]{1,0:T(8,128)(2,1)}), bf16[1024,1152]{1,0:T(8,128)(2,1)}) %all-gather.16.cloned.1.call-update) | async-done | bytes 2359312 | tf_op jit(solution)/shard_map/all_gather | solution.py:70
  451.6 8.4 fusion.15
  461.2 9.0 multiply_reduce_fusion
  470.1 8.0 multiply_convert_fusion
  481.5 6.1 broadcast_multiply_fusion
  495.0 4.1 convolution_convert_fusion.1
  500.2 5.4 convolution_convert_fusion.7
  505.6 6.0 convolution_convert_fusion.6
  511.7 5.6 convolution_convert_fusion.5
  518.4 6.2 convolution_convert_fusion.4
  524.6 7.7 reduce-scatter.18.cloned.1.call-done
  552.5 43.8 %all_to_all.96 = bf16[256,6,4,288]{0,3,1,2:T(8,128)(2,1)S(1)} all-to-all(bf16[256,6,4,288]{0,3,1,2:T(8,128)(2,1)S(1)} %copy.135), channel_id=1, replica_groups=mesh['dp'=8,'seq'=4] {'seq'}, dimensions={2} | all-to-all | bytes 7077888 | tf_op jit(solution)/shard_map/all_to_all | solution.py:83
  601.7 9.3 convolution_convert_fusion
  611.0 17.0 %reduce-scatter.22.cloned.1.call-done = bf16[144,768]{1,0:T(8,128)(2,1)} async-done(((bf16[1152,768]{1,0:T(8,128)(2,1)}), bf16[144,768]{1,0:T(8,128)(2,1)}) %reduce-scatter.22.cloned.1.call-update) | async-done | bytes 221200 | tf_op jit(solution)/shard_map/reduce_scatter | solution.py:96
  635.6 61.0 %reduce-scatter.24.cloned.1.call-done = bf16[144,768]{1,0:T(8,128)(2,1)} async-done(((bf16[1152,768]{1,0:T(8,128)(2,1)}), bf16[144,768]{1,0:T(8,128)(2,1)}) %reduce-scatter.24.cloned.1.call-update) | async-done | bytes 221200 | tf_op jit(solution)/shard_map/reduce_scatter | solution.py:96
  699.0 66.0 %reduce-scatter.26.cloned.1.call-done = bf16[96,1152]{1,0:T(8,128)(2,1)} async-done(((bf16[768,1152]{1,0:T(8,128)(2,1)}), bf16[96,1152]{1,0:T(8,128)(2,1)}) %reduce-scatter.26.cloned.1.call-update) | async-done | bytes 221200 | tf_op jit(solution)/shard_map/reduce_scatter | solution.py:101
  774.9 31.9 %fusion = bf16[48,1152]{1,0:T(8,128)(2,1)S(1)} fusion(bf16[288,1152]{1,0:T(8,128)(2,1)S(1)} %convolution_convert_fusion.8), kind=kCustom, calls=%all-reduce-scatter | all-reduce-scatter fusion | flops 442369 | bytes 774656
  816.0 28.9 %reduce-scatter.20.cloned.1.call-done = bf16[144,864]{1,0:T(8,128)(2,1)} async-done(((bf16[1152,864]{1,0:T(8,128)(2,1)}), bf16[144,864]{1,0:T(8,128)(2,1)}) %reduce-scatter.20.cloned.1.call-update) | async-done | bytes 248848 | tf_op jit(solution)/shard_map/reduce_scatter | solution.py:96
  862.9 41.1 %all-reduce.3 = (f32[6912]{0:T(1024)S(1)}, f32[72]{0:T(128)}, f32[72]{0:T(128)}) all-reduce(f32[6912]{0:T(1024)S(1)} %convert_reduce_fusion, f32[72]{0:T(128)S(1)} %copy-done.53, f32[72]{0:T(128)S(1)} %copy-done.52), channel_id=13, replica_groups=mesh['dp'=8,'seq'=4] {'dp','seq'}, use_global_device_ids=true, to_apply=%region_24.25.clone | all-reduce | flops 7056 | bytes 56448
  906.4 12.5 %fusion.8 = f32[1,256,1152]{2,1,0:T(8,128)} fusion(bf16[256,6912]{1,0:T(8,128)(2,1)} %copy-done.21, bf16[1152,6912]{1,0:T(8,128)(2,1)} %all-gather.8.cloned.1.call-done, bf16[1,256,1152]{2,1,0:T(8,128)(2,1)S(1)} %copy-done.35, f32[1152]{0:T(1024)S(1)} %copy-done.41), kind=kOutput, calls=%fused_computation.27 | convolution fusion | flops 4079812608 | bytes 21238272 | tf_op jit(solution)/shard_map/rb,ab->ra/dot_general | solution.py:66
  918.9 17.6 %reduce-scatter.28.cloned.1.call-done = bf16[144,1728]{1,0:T(8,128)(2,1)} async-done(((bf16[1152,1728]{1,0:T(8,128)(2,1)}), bf16[144,1728]{1,0:T(8,128)(2,1)}) %reduce-scatter.28.cloned.1.call-update) | async-done | bytes 497680 | tf_op jit(solution)/shard_map/reduce_scatter | solution.py:96
  939.0 4.2 all-to-all-start.7
  945.9 10.1 %all-to-all-done.7 = bf16[144,6,1,288]{3,1,2,0:T(8,128)(2,1)} async-done(((bf16[144,6,1,288]{3,1,2,0:T(8,128)(2,1)}), bf16[144,6,1,288]{3,1,2,0:T(8,128)(2,1)}, u32[]{:S(2)}, u32[]{:S(2)}) %all-to-all-start.7) | async-done | bytes 497696 | tf_op jit(solution)/shard_map/all_to_all | solution.py:91
  (273 shorter events, 141.6 us)
Async XLA Ops:
  7.2 326.4 %copy-start = (bf16[768,1152]{1,0:T(8,128)(2,1)S(1)}, bf16[768,1152]{1,0:T(8,128)(2,1)}, u32[]{:S(2)}) copy-start(bf16[768,1152]{1,0:T(8,128)(2,1)} %param.22) | copy-start | bytes 5308420
  7.2 106.2 %all-gather.8.cloned.1.call-start = ((), (), s32[]{:S(2)}) async-start(), calls=%async_computation.17 | async-start | bytes 19906560 | tf_op jit(solution)/shard_map/all_gather | solution.py:70
  8.0 184.3 %all-gather.10.cloned.1.call-start = ((), (), s32[]{:S(2)}) async-start(), calls=%async_computation.18 | async-start | bytes 2949120 | tf_op jit(solution)/shard_map/all_gather | solution.py:70
  9.5 112.3 %copy-start.45 = (f32[256]{0:T(256)}, f32[256]{0:T(256)S(1)}, u32[]{:S(2)}) copy-start(f32[256]{0:T(256)S(1)} %add_rsqrt_fusion.3) | copy-start | bytes 3076
  9.8 112.0 %copy-start.23 = (bf16[256,1152]{1,0:T(8,128)(2,1)}, bf16[256,1152]{1,0:T(8,128)(2,1)S(1)}, u32[]{:S(2)}) copy-start(bf16[256,1152]{1,0:T(8,128)(2,1)S(1)} %fusion.46) | copy-start | bytes 1769476
  134.2 45.6 %all-to-all-start = ((bf16[288,3,4,288]{3,0,1,2:T(8,128)(2,1)}), bf16[288,3,4,288]{3,0,1,2:T(8,128)(2,1)}, u32[]{:S(2)}, u32[]{:S(2)}) async-start(bf16[288,3,4,288]{3,0,1,2:T(8,128)(2,1)} %copy.115), calls=%async_computation | async-start | bytes 5308416 | tf_op jit(solution)/shard_map/all_to_all | solution.py:83
  138.9 107.9 %reduce-scatter.12.cloned.1.call-start = ((), (), s32[]{:S(2)}) async-start(), calls=%async_computation.19 | async-start | bytes 2949120 | tf_op jit(solution)/shard_map/reduce_scatter | solution.py:74
  197.1 6.6 copy-start.7
  203.7 5.8 copy-start.2
  203.7 6.1 copy-start.38
  203.7 7.0 copy-start.55
  213.6 85.0 %all-gather.12.cloned.1.call-start = ((), (), s32[]{:S(2)}) async-start(), calls=%async_computation.20 | async-start | bytes 2949120 | tf_op jit(solution)/shard_map/all_gather | solution.py:70
  248.7 171.5 %copy-start.4 = (f32[256,1152]{1,0:T(8,128)}, f32[256,1152]{1,0:T(8,128)S(1)}, u32[]{:S(2)}) copy-start(f32[256,1152]{1,0:T(8,128)S(1)} %get-tuple-element.36) | copy-start | bytes 3538948
  252.4 81.1 %all-gather.14.cloned.1.call-start = ((), (), s32[]{:S(2)}) async-start(), calls=%async_computation.22 | async-start | bytes 2949120 | tf_op jit(solution)/shard_map/all_gather | solution.py:70
  260.4 33.7 %all-to-all-start.2 = ((bf16[288,1,4,768]{3,0,1,2:T(8,128)(2,1)}), bf16[288,1,4,768]{3,0,1,2:T(8,128)(2,1)}, u32[]{:S(2)}, u32[]{:S(2)}) async-start(bf16[288,1,4,768]{3,0,1,2:T(8,128)(2,1)} %copy.119), calls=%async_computation.3 | async-start | bytes 3538944 | tf_op jit(solution)/shard_map/all_to_all | solution.py:83
  294.2 33.3 %all-to-all-start.1 = ((bf16[288,1,4,768]{3,0,1,2:T(8,128)(2,1)}), bf16[288,1,4,768]{3,0,1,2:T(8,128)(2,1)}, u32[]{:S(2)}, u32[]{:S(2)}) async-start(bf16[288,1,4,768]{3,0,1,2:T(8,128)(2,1)} %copy.118), calls=%async_computation.2 | async-start | bytes 3538944 | tf_op jit(solution)/shard_map/all_to_all | solution.py:83
  298.6 86.0 %reduce-scatter.16.cloned.1.call-start = ((), (), s32[]{:S(2)}) async-start(), calls=%async_computation.23 | async-start | bytes 2949120 | tf_op jit(solution)/shard_map/reduce_scatter | solution.py:74
  351.4 68.8 %reduce-scatter.14.cloned.1.call-start = ((), (), s32[]{:S(2)}) async-start(), calls=%async_computation.21 | async-start | bytes 2949120 | tf_op jit(solution)/shard_map/reduce_scatter | solution.py:74
  356.5 28.1 %copy-start.43 = (f32[256]{0:T(256)S(1)}, f32[256]{0:T(256)}, u32[]{:S(2)}) copy-start(f32[256]{0:T(256)} %copy-done.42) | copy-start | bytes 3076
  356.5 63.7 %copy-start.19 = (bf16[1,256,1152]{2,1,0:T(8,128)(2,1)S(1)}, bf16[1,256,1152]{2,1,0:T(8,128)(2,1)}, u32[]{:S(2)}) copy-start(bf16[1,256,1152]{2,1,0:T(8,128)(2,1)} %param.17) | copy-start | bytes 1769476
  356.5 92.1 %all-gather.16.cloned.1.call-start = ((), (), s32[]{:S(2)}) async-start(), calls=%async_computation.24 | async-start | bytes 2949120 | tf_op jit(solution)/shard_map/all_gather | solution.py:70
  384.6 35.6 %copy-start.10 = (bf16[256,1152]{1,0:T(8,128)(2,1)S(1)}, bf16[256,1152]{1,0:T(8,128)(2,1)}, u32[]{:S(2)}) copy-start(bf16[256,1152]{1,0:T(8,128)(2,1)} %reduce-scatter.16.cloned.1.call-done) | copy-start | bytes 1769476
  424.4 27.2 %copy-start.39 = (f32[4,1024]{1,0:T(4,128)S(1)}, f32[4,1024]{1,0:T(4,128)}, u32[]{:S(2)}) copy-start(f32[4,1024]{1,0:T(4,128)} %copy-done.38) | copy-start | bytes 49156
  424.4 107.9 %reduce-scatter.18.cloned.1.call-start = ((), (), s32[]{:S(2)}) async-start(), calls=%async_computation.25 | async-start | bytes 2949120 | tf_op jit(solution)/shard_map/reduce_scatter | solution.py:74
  448.6 11.3 %slice-start = ((s8[16777216]{0:T(1024)(128)(4,1)}), s8[4194304]{0:T(1024)(128)(4,1)S(1)}, s32[]{:S(2)}) async-start(s8[16777216]{0:T(1024)(128)(4,1)} %bitcast.204), calls=%async_computation.32 | async-start | bytes 8388608
  451.6 8.4 slice-start.1
  451.6 8.4 slice-start.2
  451.6 9.6 slice-start.3
  470.1 8.0 copy-start.15
  499.1 102.5 %all-gather.18.cloned.1.call-start = ((), (), s32[]{:S(2)}) async-start(), calls=%async_computation.30 | async-start | bytes 2949120 | tf_op jit(solution)/shard_map/all_gather | solution.py:70
  499.7 128.3 %reduce-scatter.22.cloned.1.call-start = ((), (), s32[]{:S(2)}) async-start(), calls=%async_computation.27 | async-start | bytes 1990656 | tf_op jit(solution)/shard_map/reduce_scatter | solution.py:96
  505.6 191.0 %reduce-scatter.24.cloned.1.call-start = ((), (), s32[]{:S(2)}) async-start(), calls=%async_computation.28 | async-start | bytes 1990656 | tf_op jit(solution)/shard_map/reduce_scatter | solution.py:96
  511.6 253.4 %reduce-scatter.26.cloned.1.call-start = ((), (), s32[]{:S(2)}) async-start(), calls=%async_computation.29 | async-start | bytes 1990656 | tf_op jit(solution)/shard_map/reduce_scatter | solution.py:101
  517.3 327.7 %reduce-scatter.20.cloned.1.call-start = ((), (), s32[]{:S(2)}) async-start(), calls=%async_computation.26 | async-start | bytes 2322432 | tf_op jit(solution)/shard_map/reduce_scatter | solution.py:96
  524.5 10.1 %copy-start.46 = (f32[256]{0:T(256)S(1)}, f32[256]{0:T(256)}, u32[]{:S(2)}) copy-start(f32[256]{0:T(256)} %copy-done.45) | copy-start | bytes 3076
  524.6 411.9 %reduce-scatter.28.cloned.1.call-start = ((), (), s32[]{:S(2)}) async-start(), calls=%async_computation.31 | async-start | bytes 4644864 | tf_op jit(solution)/shard_map/reduce_scatter | solution.py:96
  610.9 23.4 %copy-start.54 = (u32[32]{0:T(128)S(1)}, u32[32]{0:T(128)}, u32[]{:S(2)}) copy-start(u32[32]{0:T(128)} %constant.57) | copy-start | bytes 388
  630.9 137.5 %all-to-all-start.4 = ((bf16[4,2,13824]{2,1,0:T(2,128)(2,1)}), bf16[4,2,13824]{2,1,0:T(2,128)(2,1)S(1)}, u32[]{:S(2)}, u32[]{:S(2)}) async-start(bf16[4,2,13824]{2,1,0:T(2,128)(2,1)} %reshape.376), calls=%async_computation.10 | async-start | bytes 442368 | tf_op jit(solution)/shard_map/all_to_all | solution.py:91
  765.0 88.4 %collective-permute-start.1 = (bf16[96,1152]{1,0:T(8,128)(2,1)}, bf16[96,1152]{1,0:T(8,128)(2,1)}, u32[]{:S(2)}, u32[]{:S(2)}) collective-permute-start(bf16[96,1152]{1,0:T(8,128)(2,1)} %reduce-scatter.26.cloned.1.call-done), channel_id=1, source_target_pairs={{0,0},{1,8},{2,16},{3,24},{4,1},{5,9},{6,17},{7,25},{8,2},{9,10},{... | collective-permute-start | bytes 663560 | tf_op jit(solution)/shard_map/ppermute | solution.py:107
  768.5 44.6 %all-to-all-start.5 = ((bf16[4,2,13824]{2,1,0:T(2,128)(2,1)}), bf16[4,2,13824]{2,1,0:T(2,128)(2,1)S(1)}, u32[]{:S(2)}, u32[]{:S(2)}) async-start(bf16[4,2,13824]{2,1,0:T(2,128)(2,1)} %reshape.378), calls=%async_computation.12 | async-start | bytes 442368 | tf_op jit(solution)/shard_map/all_to_all | solution.py:91
  806.8 7.9 collective-permute-start.2
  809.5 5.2 collective-permute-start.3
  815.4 39.8 %collective-permute-start = (bf16[36,1152]{1,0:T(8,128)(2,1)S(1)}, bf16[36,1152]{1,0:T(8,128)(2,1)S(1)}, u32[]{:S(2)}, u32[]{:S(2)}) collective-permute-start(bf16[36,1152]{1,0:T(8,128)(2,1)S(1)} %constant_dynamic-slice_fusion), channel_id=1, source_target_pairs={{0,0},{1,8},{2,16},{3,24},{4,1},{5,9},{6,17},{7,25},{8,2},{9,10},{... | collective-permute-start | bytes 248840 | tf_op jit(solution)/shard_map/ppermute | solution.py:107
  847.1 11.6 %all-to-all-start.3 = ((bf16[144,3,1,288]{3,1,2,0:T(4,128)(2,1)}), bf16[144,3,1,288]{3,1,2,0:T(4,128)(2,1)S(1)}, u32[]{:S(2)}, u32[]{:S(2)}) async-start(bf16[144,3,1,288]{3,1,2,0:T(4,128)(2,1)} %bitcast.40), calls=%async_computation.8 | async-start | bytes 884736 | tf_op jit(solution)/shard_map/all_to_all | solution.py:91
  862.9 43.4 %copy-start.35 = (bf16[1,256,1152]{2,1,0:T(8,128)(2,1)S(1)}, bf16[1,256,1152]{2,1,0:T(8,128)(2,1)}, u32[]{:S(2)}) copy-start(bf16[1,256,1152]{2,1,0:T(8,128)(2,1)} %param.16) | copy-start | bytes 1769476
  862.9 43.4 %copy-start.41 = (f32[1152]{0:T(1024)S(1)}, f32[1152]{0:T(1024)}, u32[]{:S(2)}) copy-start(f32[1152]{0:T(1024)} %copy-done.40) | copy-start | bytes 13828
  918.9 24.4 %copy-start.13 = (f32[256,1152]{1,0:T(8,128)S(1)}, f32[256,1152]{1,0:T(8,128)}, u32[]{:S(2)}) copy-start(f32[256,1152]{1,0:T(8,128)} %get-tuple-element.34) | copy-start | bytes 3538948
  939.0 17.0 %all-to-all-start.7 = ((bf16[144,6,1,288]{3,1,2,0:T(8,128)(2,1)}), bf16[144,6,1,288]{3,1,2,0:T(8,128)(2,1)}, u32[]{:S(2)}, u32[]{:S(2)}) async-start(bf16[144,6,1,288]{3,1,2,0:T(8,128)(2,1)} %bitcast.209), calls=%async_computation.16 | async-start | bytes 1769472 | tf_op jit(solution)/shard_map/all_to_all | solution.py:91
  (42 other events, 90.9 us)
Sparse Core Ops, SparseCore 0:
  9.6 103.7 all-gather.7
  125.9 30.4 all-gather.9
  213.8 33.0 reduce-scatter.11
  252.5 30.8 all-gather.11
  285.5 31.1 all-gather.13
  351.5 33.0 reduce-scatter.15
  387.1 33.0 reduce-scatter.13
  424.5 24.0 all-gather.15
  499.2 33.0 reduce-scatter.17
  533.7 24.0 all-gather.17
  561.3 66.6 reduce-scatter.21
  631.7 64.7 reduce-scatter.23
  700.0 64.9 reduce-scatter.25
  768.8 76.0 reduce-scatter.19
  848.8 87.6 reduce-scatter.27

commit v2 on v1

--- a/solution.py
+++ b/solution.py
@@ -3,6 +3,8 @@
 import jax
 import jax.numpy as jnp
 from jax import lax
+from jax.experimental import pallas as pl
+from jax.experimental.pallas import tpu as pltpu
 from jax.sharding import PartitionSpec as P
 
 HEADS = 16
@@ -66,14 +68,302 @@
     return jnp.einsum("rb,ab->ra", left, right, preferred_element_type=F32)
 
 
+MESH = pl.DeviceIdType.MESH
+SUM_ID, GATHER_ID, SCATTER_ID, WEIGHT_ID = 1, 2, 3, 4
+
+
+def greet(partners):
+    barrier = pltpu.get_barrier_semaphore()
+    for partner in partners:
+        pl.semaphore_signal(barrier, inc=1, device_id=partner, device_id_type=MESH)
+    pl.semaphore_wait(barrier, len(partners))
+
+
+def group_partners():
+    item, column = lax.axis_index("dp"), lax.axis_index("seq")
+    core = lax.rem(column, 2)
+    return (item, column + 1 - 2 * core), (item, lax.rem(column + 2, 4))
+
+
+GATHER_PIECES = 4
+
+
+def gather_kernel(own_ref, out_ref, local_sem, send_sem, recv_sem):
+    column = lax.axis_index("seq")
+    sibling, across = group_partners()
+    greet([sibling, across])
+    local = pltpu.make_async_copy(own_ref, out_ref.at[column], local_sem)
+    local.start()
+    rows = own_ref.shape[0] // GATHER_PIECES
+
+    def remote(source, place, piece, kind, target):
+        part = pl.ds(piece * rows, rows)
+        return pltpu.make_async_remote_copy(
+            src_ref=source.at[part],
+            dst_ref=out_ref.at[place, part],
+            send_sem=send_sem.at[kind, piece],
+            recv_sem=recv_sem.at[kind, piece],
+            device_id=target,
+            device_id_type=MESH,
+        )
+
+    far = lax.rem(column + 2, 4)
+    pieces = range(GATHER_PIECES)
+    over = [remote(own_ref, column, piece, 0, across) for piece in pieces]
+    beside = [remote(own_ref, column, piece, 1, sibling) for piece in pieces]
+    onward = [remote(out_ref.at[far], far, piece, 2, sibling) for piece in pieces]
+    for copy in over:
+        copy.start()
+    for copy in beside:
+        copy.start()
+    for piece in pieces:
+        over[piece].wait_recv()
+        onward[piece].start()
+    for piece in pieces:
+        over[piece].wait_send()
+        beside[piece].wait()
+        onward[piece].wait()
+    local.wait()
+
+
 def gather_rows(values):
-    return lax.all_gather(values, "seq", axis=0, tiled=True)
+    rows, columns = values.shape
+    gathered = pl.pallas_call(
+        gather_kernel,
+        out_shape=jax.ShapeDtypeStruct((4, rows, columns), values.dtype),
+        in_specs=[pl.BlockSpec(memory_space=pltpu.VMEM)],
+        out_specs=pl.BlockSpec(memory_space=pltpu.VMEM),
+        scratch_shapes=[
+            pltpu.SemaphoreType.DMA,
+            pltpu.SemaphoreType.DMA((3, GATHER_PIECES)),
+            pltpu.SemaphoreType.DMA((3, GATHER_PIECES)),
+        ],
+        compiler_params=pltpu.CompilerParams(
+            collective_id=GATHER_ID, has_side_effects=True, vmem_limit_bytes=48 * 2**20
+        ),
+        name="gather_rows",
+    )(values)
+    return gathered.reshape(4 * rows, columns)
+
+
+def scatter_kernel(parts_ref, out_ref, near, low, far, send_sem, recv_sem):
+    column = lax.axis_index("seq")
+    core, chip = lax.rem(column, 2), column // 2
+    sibling, across = group_partners()
+    greet([sibling, across])
+    rows = out_ref.shape[0] // 2
+
+    def remote(source, target_ref, index, target):
+        return pltpu.make_async_remote_copy(
+            src_ref=source,
+            dst_ref=target_ref,
+            send_sem=send_sem.at[index],
+            recv_sem=recv_sem.at[index],
+            device_id=target,
+            device_id_type=MESH,
+        )
+
+    parts = [pl.ds(piece * rows, rows) for piece in range(2)]
+    beside = [
+        remote(parts_ref.at[1 - chip, 1 - core, part], near.at[0, part], i, sibling)
+        for i, part in enumerate(parts)
+    ]
+    beside.append(remote(parts_ref.at[chip, 1 - core], near.at[1], 2, sibling))
+    for copy in beside:
+        copy.start()
+    over = [remote(low.at[part], far.at[part], 3 + i, across) for i, part in enumerate(parts)]
+    for i, part in enumerate(parts):
+        beside[i].wait_recv()
+        pair = parts_ref[1 - chip, core, part].astype(F32) + near[0, part].astype(F32)
+        low[part] = pair.astype(BF16)
+        over[i].start()
+    beside[2].wait_recv()
+    out_ref[...] = parts_ref[chip, core].astype(F32) + near[1].astype(F32)
+    for i, part in enumerate(parts):
+        over[i].wait()
+        out_ref[part] += far[part].astype(F32)
+    for copy in beside:
+        copy.wait_send()
 
 
 def scatter_rows(partial):
-    return lax.psum_scatter(
-        partial.astype(BF16), "seq", scatter_dimension=0, tiled=True
-    ).astype(F32)
+    rows, columns = partial.shape[0] // 4, partial.shape[1]
+    return pl.pallas_call(
+        scatter_kernel,
+        out_shape=jax.ShapeDtypeStruct((rows, columns), F32),
+        in_specs=[pl.BlockSpec(memory_space=pltpu.VMEM)],
+        out_specs=pl.BlockSpec(memory_space=pltpu.VMEM),
+        scratch_shapes=[
+            pltpu.VMEM((2, rows, columns), BF16),
+            pltpu.VMEM((rows, columns), BF16),
+            pltpu.VMEM((rows, columns), BF16),
+            pltpu.SemaphoreType.DMA((5,)),
+            pltpu.SemaphoreType.DMA((5,)),
+        ],
+        compiler_params=pltpu.CompilerParams(
+            collective_id=SCATTER_ID, has_side_effects=True, vmem_limit_bytes=48 * 2**20
+        ),
+        name="scatter_rows",
+    )(partial.astype(BF16).reshape(2, 2, rows, columns))
+
+
+def weight_blocks():
+    blocks = [(0, None, 0, 1152), (1, 0, 0, 512), (1, 1, 0, 512), (0, None, 2304, 1152)]
+    blocks += [(k, j, 0, 384) for k in (2, 3) for j in (0, 1)]
+    return blocks + [(0, None, 4608, 1152)]
+
+
+FIRST_ROWS = 80
+
+
+def weights_kernel(*refs):
+    ins, outs = refs[:4], refs[4:8]
+    held, (local_sem, send_sem, recv_sem) = refs[8:12], refs[12:]
+    item, column = lax.axis_index("dp"), lax.axis_index("seq")
+    core, chip = lax.rem(column, 2), column // 2
+    y_bit, z_bit = lax.rem(item, 2), lax.rem(item // 2, 2)
+    sibling = (item, column + 1 - 2 * core)
+    y_near = (item + 1 - 2 * y_bit, column)
+    z_near = (item + 2 - 4 * z_bit, column)
+    cores = [core, 1 - core]
+    far = [(1 - chip) * 2 + k for k in cores]
+    greet([(item, far[0]), (item, far[1]), sibling, y_near, z_near])
+    blocks = weight_blocks()
+    count = len(blocks)
+    half_rows = ins[0].shape[0] // 2
+
+    def copy(source, target_ref, block, kind, target):
+        return pltpu.make_async_remote_copy(
+            src_ref=source,
+            dst_ref=target_ref,
+            send_sem=send_sem.at[block, kind],
+            recv_sem=recv_sem.at[block, kind],
+            device_id=target,
+            device_id_type=MESH,
+        )
+
+    def piece(ref, block, y_pick, z_pick, first_row=0, rows=half_rows):
+        _, _, start, columns = blocks[block]
+        return ref.at[
+            pl.ds(pl.multiple_of(z_pick * half_rows + first_row, 16), rows),
+            pl.ds(pl.multiple_of(start + y_pick * columns, 128), columns),
+        ]
+
+    def mine_for(array, target):
+        if array == 0:
+            return ins[0]
+        if array == 1:
+            return ins[1].at[target]
+        columns = outs[array].shape[2]
+        return ins[array].at[:, pl.ds(pl.multiple_of(target * columns, 128), columns)]
+
+    def over(block):
+        array, offset, _, _ = blocks[block]
+        goal = far[offset or 0]
+        if array >= 2:
+            columns = blocks[block][3]
+            source = ins[array].at[
+                pl.ds(pl.multiple_of(z_bit * half_rows, 16), half_rows),
+                pl.ds(pl.multiple_of(goal * 2 * columns + y_bit * columns, 128), columns),
+            ]
+        else:
+            source = piece(mine_for(array, goal), block, y_bit, z_bit)
+        return copy(source, piece(outs[array].at[column], block, y_bit, z_bit), block, 0, (item, goal))
+
+    def onward(block, kind):
+        array, offset, _, _ = blocks[block]
+        ref = outs[array].at[far[offset or 0]]
+        if kind == 1:
+            part, target = piece(ref, block, y_bit, z_bit), y_near
+        elif kind == 2:
+            part, target = piece(ref, block, y_bit, z_bit), z_near
+        elif kind == 3:
+            part, target = piece(ref, block, 1 - y_bit, z_bit, 0, FIRST_ROWS), z_near
+        else:
+            rest = half_rows - FIRST_ROWS
+            part, target = piece(ref, block, y_bit, 1 - z_bit, FIRST_ROWS, rest), y_near
+        return copy(part, part, block, kind, target)
+
+    def share(block):
+        _, _, start, columns = blocks[block]
+        part = outs[0].at[far[0], :, pl.ds(start, 2 * columns)]
+        return copy(part, part, block, 5, sibling)
+
+    beside = [
+        copy(mine_for(k, sibling[1]), outs[k].at[column], k, 6, sibling) for k in range(4)
+    ]
+    load = [
+        pltpu.make_async_copy(mine_for(k, column), held[k], local_sem.at[0, k]) for k in range(4)
+    ]
+    store = [
+        pltpu.make_async_copy(held[k], outs[k].at[column], local_sem.at[1, k]) for k in range(4)
+    ]
+    over(0).start()
+    over(1).start()
+    for k in range(4):
+        beside[k].start()
+        load[k].start()
+    for k in range(4):
+        load[k].wait()
+        store[k].start()
+    for step in range(count + 2):
+        if step < count:
+            over(step).wait_recv()
+            if step + 2 < count:
+                over(step + 2).start()
+            onward(step, 1).start()
+            onward(step, 2).start()
+        if 0 <= step - 1 < count:
+            onward(step - 1, 1).wait_recv()
+            onward(step - 1, 3).start()
+            onward(step - 1, 2).wait_recv()
+            onward(step - 1, 4).start()
+        if 0 <= step - 2 < count:
+            onward(step - 2, 3).wait_recv()
+            onward(step - 2, 4).wait_recv()
+            if blocks[step - 2][0] == 0:
+                share(step - 2).start()
+    for block in range(count):
+        over(block).wait_send()
+        for kind in range(1, 5):
+            onward(block, kind).wait_send()
+        if blocks[block][0] == 0:
+            share(block).wait()
+    for k in range(4):
+        beside[k].wait()
+        store[k].wait()
+
+
+def gather_weights(w_mod, w_qkv, w_gate, w_up):
+    rows, width = w_mod.shape[0], w_qkv.shape[1] // 3
+    head_cols = 3 * width // 4
+    qkv = jnp.transpose(w_qkv.reshape(rows, 3, 4, width // 4), (2, 0, 1, 3))
+    qkv = jnp.pad(qkv.reshape(4, rows, head_cols), ((0, 0), (0, 0), (0, -head_cols % 256)))
+    shapes = [
+        w_mod.shape,
+        qkv.shape[1:],
+        (rows, w_gate.shape[1] // 4),
+        (rows, w_up.shape[1] // 4),
+    ]
+    count = len(weight_blocks())
+    gathered = pl.pallas_call(
+        weights_kernel,
+        out_shape=[jax.ShapeDtypeStruct((4,) + shape, BF16) for shape in shapes],
+        in_specs=[pl.BlockSpec(memory_space=pl.ANY)] * 4,
+        out_specs=[pl.BlockSpec(memory_space=pl.ANY)] * 4,
+        scratch_shapes=[pltpu.VMEM(shape, BF16) for shape in shapes]
+        + [
+            pltpu.SemaphoreType.DMA((2, 4)),
+            pltpu.SemaphoreType.DMA((count, 7)),
+            pltpu.SemaphoreType.DMA((count, 7)),
+        ],
+        compiler_params=pltpu.CompilerParams(
+            collective_id=WEIGHT_ID, has_side_effects=True, vmem_limit_bytes=56 * 2**20
+        ),
+        name="gather_weights",
+    )(w_mod, qkv, w_gate, w_up)
+    mod, qkv, gate, up = [part.reshape(4 * rows, part.shape[2]) for part in gathered]
+    return mod, qkv[:, :head_cols], gate, up
 
 
 def rows_to_columns(values, blocks):
@@ -92,19 +382,445 @@
     return moved.reshape(rows // ways, columns * ways)
 
 
-def sum_columns(partial, blocks):
-    mine = lax.psum_scatter(partial.astype(BF16), "dp", scatter_dimension=0, tiled=True)
-    return columns_to_rows(mine, blocks).astype(F32)
-
-
-def sum_rows(partial):
-    mine = lax.psum_scatter(partial.astype(BF16), "dp", scatter_dimension=0, tiled=True)
+TILE = 128
+
+
+def first_tile(place, tiles):
+    return (tiles * place) // 4
+
+
+def padded_rows(rows):
+    return -(-rows // 16) * 16
+
+
+class Part:
+    def __init__(self, left, right, rows, columns, order, by_rows=False):
+        self.left, self.right, self.rows, self.columns = left, right, rows, columns
+        self.order, self.by_rows = order, by_rows
+        self.slab = padded_rows(rows)
+
+
+def grads_kernel(parts, names, groups, n_out, *refs):
+    refs = list(refs)
+
+    def take(count):
+        taken = refs[:count]
+        del refs[:count]
+        return taken
+
+    ins = dict(zip(names, take(len(names)), strict=True))
+    shared = take(groups)
+    small_in = take(1)[0]
+    count = len(parts)
+    outs = take(count)
+    small_out = take(1)[0]
+    held = dict(zip(names, take(len(names)), strict=True))
+    gathered = take(groups)
+    own, first_in, second_in, third_in = take(count), take(count), take(count), take(count)
+    slabs, slab_in = take(count), take(count)
+    total, small, small_came = take(3)
+    load_sem, share_send, share_recv, own_sem, send_sem, recv_sem = take(6)
+    last_send, last_recv, small_send, small_recv = take(4)
+
+    item, column = lax.axis_index("dp"), lax.axis_index("seq")
+    bits = [lax.rem(item, 2), lax.rem(item // 2, 2), item // 4]
+    partners = [(item + (1 - 2 * bits[k]) * (1 << k), column) for k in range(3)]
+    peers = [(item, lax.rem(column + k, 4)) for k in range(1, 4)]
+    owner = (2 * column + item // 4, lax.rem(item, 4))
+    feeder = (4 * lax.rem(item, 2) + column, item // 2)
+    elsewhere = jnp.logical_or(owner[0] != item, owner[1] != column)
+
+    loads = {
+        name: pltpu.make_async_copy(ins[name], held[name], load_sem.at[i])
+        for i, name in enumerate(names)
+    }
+    for name in names:
+        loads[name].start()
+
+    barrier = pltpu.get_barrier_semaphore()
+    for partner in partners + peers:
+        pl.semaphore_signal(barrier, inc=1, device_id=partner, device_id_type=MESH)
+    waits = 6
+    if any(part.by_rows for part in parts):
+        waits = 6 + elsewhere.astype(jnp.int32)
+
+        @pl.when(elsewhere)
+        def _():
+            pl.semaphore_signal(barrier, inc=1, device_id=feeder, device_id_type=MESH)
+
+    pl.semaphore_wait(barrier, waits)
+
+    def remote(source, target_ref, send, recv, target):
+        return pltpu.make_async_remote_copy(
+            src_ref=source,
+            dst_ref=target_ref,
+            send_sem=send,
+            recv_sem=recv,
+            device_id=target,
+            device_id_type=MESH,
+        )
+
+    def columns_of(group, place):
+        wide, narrow = shared[group].shape[1], gathered[group].shape[2]
+        if wide == narrow:
+            return shared[group]
+        start = first_tile(place, wide // TILE) * TILE
+        return shared[group].at[:, pl.ds(pl.multiple_of(start, TILE), narrow)]
+
+    shares = [
+        [
+            remote(
+                columns_of(group, peer[1]),
+                gathered[group].at[column],
+                share_send.at[group, k],
+                share_recv.at[group, k],
+                peer,
+            )
+            for k, peer in enumerate(peers)
+        ]
+        for group in range(groups)
+    ]
+    own_shares = [
+        pltpu.make_async_copy(columns_of(g, column), gathered[g].at[column], own_sem.at[g])
+        for g in range(groups)
+    ]
+    for group in range(groups):
+        own_shares[group].start()
+        for copy in shares[group]:
+            copy.start()
+    ready = set()
+
+    def operand(name):
+        if isinstance(name, int):
+            if name not in ready:
+                own_shares[name].wait()
+                for copy in shares[name]:
+                    copy.wait()
+            ready.add(name)
+            ref = gathered[name]
+            return ref[...].reshape(4 * ref.shape[1], ref.shape[2])
+        if name not in ready:
+            loads[name].wait()
+        ready.add(name)
+        return held[name][...]
+
+    def multiply(index):
+        part = parts[index]
+        left, right = operand(part.left), operand(part.right)
+        if isinstance(part.right, int):
+            sums = jnp.sum(right.astype(F32), axis=0, keepdims=True)
+            for tile in range(part.columns // TILE):
+                row = 8 * (part.right - 1) + tile
+                small[0, row : row + 1] = sums[:, tile * TILE : (tile + 1) * TILE]
+        step = 384 if part.slab == part.rows else left.shape[1]
+        for start in range(0, left.shape[1], step):
+            product = lax.dot_general(
+                left[:, start : start + step],
+                right,
+                (((0,), (0,)), ((), ())),
+                preferred_element_type=F32,
+            )
+            if part.slab == part.rows:
+                product = product.astype(BF16)
+                for d in range(8):
+                    low = max(start, d * part.rows)
+                    high = min(start + step, (d + 1) * part.rows)
+                    if low < high:
+                        own[index][
+                            d // 4, d // 2 % 2, d % 2, low - d * part.rows : high - d * part.rows
+                        ] = product[low - start : high - start]
+            else:
+                total[: left.shape[1], : part.columns] = product
+                for d in range(8):
+                    own[index][d // 4, d // 2 % 2, d % 2] = cut(
+                        d * part.rows, part.rows, part.slab, part.columns
+                    )
+
+    def cut(start, rows, padded, columns):
+        values = total[start : start + rows, :columns]
+        if padded > rows:
+            values = jnp.concatenate([values, jnp.zeros((padded - rows, columns), F32)], axis=0)
+        return values.astype(BF16)
+
+    def half(index, mine):
+        order = parts[index].order
+        pick = bits[order] if mine else 1 - bits[order]
+        return (slice(None), slice(None), pick) if order == 0 else (slice(None), pick)
+
+    def pick_own(index, high, low):
+        order = parts[index].order
+        return (high, low, bits[0]) if order == 0 else (high, bits[1], low)
+
+    def stage(index, step):
+        part = parts[index]
+        sems = send_sem.at[index, step], recv_sem.at[index, step]
+        other = 1 - part.order
+        if step == 0:
+            source, target = own[index].at[half(index, False)], first_in[index]
+            return remote(source, target, *sems, partners[part.order])
+        if step == 1:
+            place = pick_own(index, slice(None), 1 - bits[other])
+            return remote(own[index].at[place], second_in[index], *sems, partners[other])
+        place = pick_own(index, 1 - bits[2], bits[other])
+        return remote(own[index].at[place], third_in[index], *sems, partners[2])
+
+    def begin(index):
+        multiply(index)
+        stage(index, 0).start()
+
+    def end_first(index):
+        stage(index, 0).wait()
+        for high in range(2):
+            for low in range(2):
+                place = pick_own(index, high, low)
+                mine = own[index][place].astype(F32)
+                own[index][place] = (mine + first_in[index][high, low].astype(F32)).astype(BF16)
+        stage(index, 1).start()
+
+    def end_second(index):
+        stage(index, 1).wait()
+        for high in range(2):
+            place = pick_own(index, high, bits[1 - parts[index].order])
+            mine = own[index][place].astype(F32)
+            own[index][place] = (mine + second_in[index][high].astype(F32)).astype(BF16)
+        stage(index, 2).start()
+
+    def last(index):
+        if parts[index].by_rows:
+            sems = last_send.at[index, 0], last_recv.at[index, 0]
+            return [remote(slabs[index], slab_in[index], *sems, owner)]
+        return [
+            remote(
+                slabs[index].at[peer[1]],
+                slab_in[index].at[column],
+                last_send.at[index, k],
+                last_recv.at[index, k],
+                peer,
+            )
+            for k, peer in enumerate(peers)
+        ]
+
+    def end_third(index):
+        part = parts[index]
+        stage(index, 2).wait()
+        place = pick_own(index, bits[2], bits[1 - part.order])
+        sums = own[index][place].astype(F32) + third_in[index][...].astype(F32)
+        if part.by_rows:
+            slabs[index][...] = sums.astype(BF16)
+
+            @pl.when(elsewhere)
+            def _():
+                last(index)[0].start()
+
+            @pl.when(jnp.logical_not(elsewhere))
+            def _():
+                slab_in[index][...] = slabs[index][...]
+
+            return
+        total[: part.rows, : part.columns] = sums
+        rows = part.rows // 4
+        for k in range(4):
+            slabs[index][k] = cut(k * rows, rows, padded_rows(rows), part.columns)
+        for copy in last(index):
+            copy.start()
+        slab_in[index][column] = slabs[index][column]
+
+    def end_last(index):
+        part = parts[index]
+        if part.by_rows:
+
+            @pl.when(elsewhere)
+            def _():
+                last(index)[0].wait()
+
+            outs[index][...] = slab_in[index][...].astype(F32)[: part.rows]
+            return
+        for copy in last(index):
+            copy.wait()
+        rows = part.rows // 4
+        wide = outs[index].shape[-1]
+        for k in range(4):
+            values = slab_in[index][k].astype(F32)[:rows]
+            if len(outs[index].shape) == 3:
+                outs[index][k] = values
+            else:
+                start = first_tile(k, wide // TILE) * TILE
+                outs[index][:, start : start + part.columns] = values
+
+    def small_step(step):
+        if step < 3:
+            sems = small_send.at[step], small_recv.at[step]
+            return [remote(small.at[step], small_came.at[step], *sems, partners[step])]
+        return [
+            remote(small.at[3], small_out.at[column], small_send.at[3 + k], small_recv.at[3 + k], peer)
+            for k, peer in enumerate(peers)
+        ]
+
+    small[0] = small_in[...]
+    ahead = 2
+    for index in range(min(ahead, count)):
+        begin(index)
+    for step in range(count + 3):
+        if step < count:
+            end_first(step)
+            if step + ahead < count:
+                begin(step + ahead)
+        if 0 <= step - 1 < count:
+            end_second(step - 1)
+        if 0 <= step - 2 < count:
+            end_third(step - 2)
+        if 0 <= step - 3 < count:
+            end_last(step - 3)
+        at = step - (count - ahead)
+        if at == 0:
+            small_step(0)[0].start()
+        if 1 <= at <= 3:
+            small_step(at - 1)[0].wait()
+            small[at] = small[at - 1] + small_came[at - 1]
+            for copy in small_step(at):
+                copy.start()
+    small_out[column] = small[3]
+    for copy in small_step(3):
+        copy.wait()
+
+
+def weight_grads(parts, arrays, shared, small, out_shapes):
+    count, groups = len(parts), len(shared)
+    names = tuple(arrays)
+    tokens_all = 4 * shared[0].shape[0]
+    scratch = [pltpu.VMEM(value.shape, BF16) for value in arrays.values()]
+    for index, value in enumerate(shared):
+        columns = value.shape[1] if index == 0 else -(-value.shape[1] // (4 * TILE)) * TILE
+        scratch.append(pltpu.VMEM((4, tokens_all // 4, columns), BF16))
+    for lead in ((2, 2, 2), (2, 2), (2,), ()):
+        scratch += [pltpu.VMEM(lead + (part.slab, part.columns), BF16) for part in parts]
+    for _ in range(2):
+        for part in parts:
+            if part.by_rows:
+                scratch.append(pltpu.VMEM((part.slab, part.columns), BF16))
+            else:
+                scratch.append(pltpu.VMEM((4, padded_rows(part.rows // 4), part.columns), BF16))
+    widest = max(part.columns for part in parts)
+    tallest = max(8 * part.rows if part.by_rows and part.slab > part.rows else part.rows for part in parts)
+    scratch += [
+        pltpu.VMEM((tallest, widest), F32),
+        pltpu.VMEM((4,) + small.shape, F32),
+        pltpu.VMEM((3,) + small.shape, F32),
+        pltpu.SemaphoreType.DMA((len(names),)),
+        pltpu.SemaphoreType.DMA((groups, 3)),
+        pltpu.SemaphoreType.DMA((groups, 3)),
+        pltpu.SemaphoreType.DMA((groups,)),
+        pltpu.SemaphoreType.DMA((count, 3)),
+        pltpu.SemaphoreType.DMA((count, 3)),
+        pltpu.SemaphoreType.DMA((count, 3)),
+        pltpu.SemaphoreType.DMA((count, 3)),
+        pltpu.SemaphoreType.DMA((6,)),
+        pltpu.SemaphoreType.DMA((6,)),
+    ]
+
+    def kernel(*refs):
+        grads_kernel(parts, names, groups, count, *refs)
+
+    return pl.pallas_call(
+        kernel,
+        out_shape=[jax.ShapeDtypeStruct(shape, F32) for shape in out_shapes]
+        + [jax.ShapeDtypeStruct((4,) + small.shape, F32)],
+        in_specs=[pl.BlockSpec(memory_space=pl.ANY)] * (len(names) + groups)
+        + [pl.BlockSpec(memory_space=pltpu.VMEM)],
+        out_specs=[pl.BlockSpec(memory_space=pltpu.VMEM)] * (count + 1),
+        scratch_shapes=scratch,
+        compiler_params=pltpu.CompilerParams(
+            collective_id=SUM_ID, has_side_effects=True, vmem_limit_bytes=63 * 2**20
+        ),
+        name="weight_grads",
+    )(*arrays.values(), *shared, small)
+
+
+def to_owners(rows):
     n_dp, n_seq = lax.axis_size("dp"), lax.axis_size("seq")
     pairs = []
     for d in range(n_dp):
         for s in range(n_seq):
             pairs.append((d * n_seq + s, s * n_dp + d))
-    return lax.ppermute(mine, ("dp", "seq"), pairs).astype(F32)
+    return lax.ppermute(rows, ("dp", "seq"), pairs)
+
+
+def columns_to_rows(values, blocks):
+    rows, columns = values.shape
+    ways = lax.axis_size("seq")
+    values = values.reshape(rows, blocks, 1, columns // blocks)
+    moved = lax.all_to_all(values, "seq", split_axis=0, concat_axis=2, tiled=True)
+    return moved.reshape(rows // ways, columns * ways)
+
+
+def plain_weight_grads(arrays, shared, bias_rows, gains):
+    def share(partial):
+        return lax.psum_scatter(partial.astype(BF16), "dp", scatter_dimension=0, tiled=True)
+
+    def by_columns(left, right, blocks):
+        return columns_to_rows(share(outer_sum(left, right)), blocks).astype(F32)
+
+    def by_rows(left, right):
+        return to_owners(share(outer_sum(left, right))).astype(F32)
+
+    lifted = gather_rows(shared[0])
+    mod_rows = jnp.concatenate([shared[1], shared[2]], axis=1)
+    mod = by_columns(lifted, rows_to_columns(mod_rows, 6), 6)
+    bias = lax.psum_scatter(bias_rows, ("dp", "seq"), scatter_dimension=0, tiled=True)
+    return (
+        by_columns(arrays["hidden_a"], arrays["grad_project"], 3),
+        by_rows(arrays["attended"], arrays["grad_branch_a"]),
+        by_columns(arrays["hidden_b"], arrays["grad_gate_in"], 1),
+        by_columns(arrays["hidden_b"], arrays["grad_up_in"], 1),
+        by_rows(arrays["inner"], arrays["grad_branch_b"]),
+        mod,
+        bias,
+        lax.psum(gains, ("dp", "seq")),
+    )
+
+
+def all_weight_grads(arrays, shared, gains):
+    if lax.axis_size("dp") != 8:
+        bias_rows = jnp.concatenate([jnp.sum(part.astype(F32), axis=0) for part in shared[1:]])
+        return plain_weight_grads(arrays, shared, bias_rows, gains)
+    width, wide = arrays["hidden_a"].shape[1], shared[1].shape[1]
+    ff, heads = arrays["inner"].shape[1], arrays["attended"].shape[1]
+    mod = -(-wide // (4 * TILE)) * TILE
+    rows = width // 8
+    parts = [
+        Part("inner", "grad_branch_b", ff // 8, width, 0, True),
+        Part("hidden_b", "grad_gate_in", rows, ff, 1),
+        Part("hidden_b", "grad_up_in", rows, ff, 0),
+        Part("attended", "grad_branch_a", heads // 8, width, 1, True),
+        Part("hidden_a", "grad_project", rows, 3 * heads, 0),
+        Part(0, 2, rows, mod, 0),
+        Part(0, 1, rows, mod, 0),
+    ]
+    small = jnp.pad(gains, ((0, 0), (0, TILE - gains.shape[1])))
+    small = jnp.concatenate([jnp.zeros((16, TILE), F32), small, jnp.zeros((6, TILE), F32)])
+    own = rows // 4
+    shapes = [
+        (ff // 8, width),
+        (own, 4 * ff),
+        (own, 4 * ff),
+        (heads // 8, width),
+        (4, own, 3 * heads),
+        (own, wide),
+        (own, wide),
+    ]
+    down, gate, up, out, qkv, mod_b, mod_a, small = weight_grads(parts, arrays, shared, small, shapes)
+    qkv = jnp.transpose(qkv.reshape(4, own, 3, heads), (1, 2, 0, 3)).reshape(own, 3 * width)
+    sums = small[:, :16].reshape(4, 2, 8 * TILE)
+    tiles = wide // TILE
+    edges = [first_tile(k, tiles) for k in range(4)] + [tiles]
+    bias = jnp.concatenate(
+        [sums[k, g, : (edges[k + 1] - edges[k]) * TILE] for g in range(2) for k in range(4)]
+    )
+    own_bias = bias.shape[0] // 32
+    place = lax.axis_index("dp") * 4 + lax.axis_index("seq")
+    bias = lax.dynamic_slice(bias, (place * own_bias,), (own_bias,))
+    gains = jnp.sum(small[:, 16:18, :HD], axis=0)
+    return qkv, out, gate, up, down, jnp.concatenate([mod_a, mod_b], axis=1), bias, gains
 
 
 def shards(
@@ -129,10 +845,7 @@
     patches = local_rows * ways
     local_heads = HEADS // ways
     factor = HD ** (-0.5)
-    mod_full = gather_rows(w_mod)
-    qkv_cols = rows_to_columns(w_qkv, 3)
-    gate_cols = rows_to_columns(w_gate, 1)
-    up_cols = rows_to_columns(w_up, 1)
+    mod_full, qkv_cols, gate_cols, up_cols = gather_weights(w_mod, w_qkv, w_gate, w_up)
     all_positions = lax.all_gather(positions[:, 0], "seq", axis=1, tiled=True)
     cosine, sine = rope_tables(all_positions, HD)
 
@@ -150,7 +863,6 @@
     inverse_a = inverse_rms(tokens_f)
     normed_a = tokens_f * inverse_a
     hidden_a = gather_rows((normed_a * (1.0 + scale_a) + shift_a).astype(BF16))
-    lifted_full = gather_rows(lifted_low)
     grad_out = cotangent[0].astype(F32) * share
     grad_branch_b = gather_rows((grad_out * gate_b).astype(BF16))
 
@@ -183,19 +895,15 @@
     block_out = (middle + gate_b * branch_b).astype(BF16)
 
     grad_gate_b = grad_out * branch_b
-    grad_w_down = sum_rows(outer_sum(inner, grad_branch_b))
     grad_inner = times_transpose(grad_branch_b, w_down)
     grad_gate_in = (grad_inner * up_in * silu_slope(gate_in)).astype(BF16)
     grad_up_in = (grad_inner * activated).astype(BF16)
-    grad_w_gate = sum_columns(outer_sum(hidden_b, grad_gate_in), 1)
-    grad_w_up = sum_columns(outer_sum(hidden_b, grad_up_in), 1)
     grad_hidden_b = scatter_rows(
         times_transpose(grad_gate_in, gate_cols) + times_transpose(grad_up_in, up_cols)
     )
     grad_middle = grad_out + rms_back(grad_hidden_b * (1.0 + scale_b), normed_b, inverse_b)
     grad_gate_a = grad_middle * branch_a
     grad_branch_a = gather_rows((grad_middle * gate_a).astype(BF16))
-    grad_w_out = sum_rows(outer_sum(attended, grad_branch_a))
     grad_attended = (
         times_transpose(grad_branch_a, w_out).astype(BF16).reshape(patches, local_heads, HD)
     )
@@ -222,26 +930,36 @@
     grad_key_raw = rms_back(grad_key_norm * k_gain, key_norm, key_inv)
     grad_project = jnp.stack([grad_query_raw, grad_key_raw, grad_value], axis=1)
     grad_project = grad_project.reshape(patches, 3 * local_heads * HD).astype(BF16)
-    grad_w_qkv = sum_columns(outer_sum(hidden_a, grad_project), 3)
     grad_hidden_a = scatter_rows(times_transpose(grad_project, qkv_cols))
     grad_tokens = grad_middle + rms_back(grad_hidden_a * (1.0 + scale_a), normed_a, inverse_a)
-    grad_mod_rows = jnp.concatenate(
-        [
-            grad_hidden_a,
-            grad_hidden_a * normed_a,
-            grad_gate_a,
-            grad_hidden_b,
-            grad_hidden_b * normed_b,
-            grad_gate_b,
-        ],
-        axis=-1,
+    grad_mod_a = jnp.concatenate(
+        [grad_hidden_a, grad_hidden_a * normed_a, grad_gate_a], axis=-1
     ).astype(BF16)
-    grad_b_mod = jnp.sum(grad_mod_rows, axis=0, dtype=F32)
-    grad_mod_cols = rows_to_columns(grad_mod_rows, 6)
-    grad_w_mod = sum_columns(outer_sum(lifted_full, grad_mod_cols), 6)
-    grad_condition = times_transpose(grad_mod_rows, mod_full) * silu_slope(condition_in)
-    sum_bias = lax.psum_scatter(grad_b_mod, ("dp", "seq"), scatter_dimension=0, tiled=True)
-    sum_q_gain, sum_k_gain = lax.psum((grad_q_gain, grad_k_gain), ("dp", "seq"))
+    grad_mod_b = jnp.concatenate(
+        [grad_hidden_b, grad_hidden_b * normed_b, grad_gate_b], axis=-1
+    ).astype(BF16)
+    half = grad_mod_a.shape[1]
+    grad_condition = (
+        times_transpose(grad_mod_a, mod_full[:, :half])
+        + times_transpose(grad_mod_b, mod_full[:, half:])
+    ) * silu_slope(condition_in)
+    arrays = {
+        "inner": inner,
+        "grad_branch_b": grad_branch_b,
+        "hidden_b": hidden_b,
+        "grad_gate_in": grad_gate_in,
+        "grad_up_in": grad_up_in,
+        "attended": attended,
+        "grad_branch_a": grad_branch_a,
+        "hidden_a": hidden_a,
+        "grad_project": grad_project,
+    }
+    gains = jnp.stack([grad_q_gain, grad_k_gain])
+    shared = [lifted_low, grad_mod_a, grad_mod_b]
+    (grad_w_qkv, grad_w_out, grad_w_gate, grad_w_up, grad_w_down, grad_w_mod, sum_bias, gains) = (
+        all_weight_grads(arrays, shared, gains)
+    )
+    sum_q_gain, sum_k_gain = gains[0], gains[1]
     return (
         block_out[None],
         grad_tokens[None],

time: 973 us -> 586 us (0.60)
  waiting for transfers between devices: 478 us -> 0 us
  Pallas kernels: 0 us -> 385 us
  blocking collectives: 156 us -> 5.29 us
  matrix products: 137 us -> 88.6 us
  local copies, waits for them, and re-layouts: 90.3 us -> 46.9 us
  starting transfers between devices: 39.6 us -> 0 us
  between operations: 17.2 us -> 3.47 us
    pallas_call x0 -> x10, Pallas kernels: none -> 385 us  [the longest x1 171 us: weight_grads(): pl.pallas_call(kernel, out_shape=[jax.ShapeDtypeStruct(shape, F32) for sh...]
    reduce_scatter x9 -> x0, waiting for transfers between devices: 290 us -> none  [the longest x4 124 us: sum_columns(): lax.psum_scatter(partial.astype(BF16), 'dp', scatter_dimension=0, tiled=T...]
    all_gather x6 -> x0, waiting for transfers between devices: 128 us -> none  [gather_rows(): return lax.all_gather(values, 'seq', axis=0, tiled=True)]
    unnamed x2 -> x0, blocking collectives: 73 us -> none
    all_to_all x7 -> x0, waiting for transfers between devices: 57.2 us -> none  [the longest x3 44.2 us: rows_to_columns(): lax.all_to_all(values, 'seq', split_axis=2, concat_axis=0, tiled=True)]
    all_to_all x1 -> x0, blocking collectives: 43.8 us -> none  [rows_to_columns(): lax.all_to_all(values, 'seq', split_axis=2, concat_axis=0, tiled=True)]
    dot_general x6 -> x0, matrix products: 35.1 us -> none  [outer_sum(): return jnp.einsum('ra,rb->ab', left, right, preferred_element_type=F32)]
    all_gather x1, blocking collectives: 38.9 us -> 5.29 us  [shards(): all_positions = lax.all_gather(positions[:, 0], 'seq', axis=1, tiled=True)]
  transfers between devices with their start and end apart: 26 -> 0, of which waited for: 16 -> 0; matrix products, arithmetic and copies ran while one was open for 19% -> 0% of each run, Pallas kernels for 0% -> 0%
where the time goes in v2:
time: 586 us; the launch traced here: 579 us
  Pallas kernels  385 us (66%)
  matrix products  88.6 us (15%)
  other arithmetic  49.4 us (8%)
  local copies, waits for them, and re-layouts  46.9 us (8%)
    pallas_call x1, Pallas kernels, weight_grads(): pl.pallas_call(kernel, out_shape=[jax.ShapeDtypeStruct(shape, F32) for sh...  171 us
    pallas_call x1, Pallas kernels, gather_weights(): pl.pallas_call(weights_kernel, out_shape=[jax.ShapeDtypeStruct((4,) + sha...  77.6 us
    pallas_call x4, Pallas kernels, scatter_rows(): pl.pallas_call(scatter_kernel, out_shape=jax.ShapeDtypeStruct((rows, colu...  68.9 us
    pallas_call x4, Pallas kernels, gather_rows(): pl.pallas_call(gather_kernel, out_shape=jax.ShapeDtypeStruct((4, rows, co...  67.5 us
    dot_general x7, matrix products, times_transpose(): return jnp.einsum('rb,ab->ra', left, right, preferred_element_type=F32)  28.2 us
    dot_general x6, matrix products, matmul(): return jnp.dot(left, right, preferred_element_type=F32)  27.9 us
    unnamed x133, local copies, waits for them, and re-layouts  15.4 us
    dot_general x1, matrix products, shards(): jnp.einsum('qhd,khd->hqk', grad_attended, value_rows, preferred_element_t...  13.9 us

profile of v2, /device:TPU:0, one launch (start us, length us, event | category | flops | bytes accessed | tf_op | source)
XLA Modules:
  0.0 579.0 jit_solution(16889949379853477635)
XLA Ops:
  0.7 4.8 reshape.320
  5.4 7.1 %copy.46 = bf16[288,3,4,288]{0,3,1,2:T(8,128)(2,1)} copy(bf16[288,3,4,288]{3,2,1,0:T(4,128)(2,1)} %reshape.320) | data formatting | bytes 3981312 | tf_op jit(solution)/shard_map/reshape | solution.py:340
  12.5 3.1 copy.47
  15.6 1.7 pad.8.refs_1_
  17.4 77.6 %gather_weights.1 = (bf16[4,288,6912]{2,1,0:T(8,128)(2,1)}, bf16[4,288,1024]{2,1,0:T(8,128)(2,1)}, bf16[4,288,768]{2,1,0:T(8,128)(2,1)}, bf16[4,288,768]{2,1,0:T(8,128)(2,1)}) custom-call(bf16[288,6912]{1,0:T(8,128)(2,1)} %refs_0_.1, bf16[4,288,1024]{2,1,0:T(8,128)(2,1)} %pad.8.refs_1_, bf16[288,3072]{1,0:T(8,128)(2,1)} %refs_2_.1, bf16[288,3072]{1,0:T(8,128)(2,1)} %refs_3_.1), custom_call_target="tpu_custom_call" | custom-call | tf_op jit(solution)/shard_map/gather_weights/pallas_call | solution.py:349
  95.8 12.4 %convolution_add_fusion = f32[256,6912]{1,0:T(8,128)} fusion(bf16[1152,6912]{1,0:T(8,128)(2,1)} %bitcast.201, f32[6912]{0:T(1024)S(1)} %copy-done.54, bf16[1,256,1152]{2,1,0:T(8,128)(2,1)S(1)} %copy-done.35, f32[1152]{0:T(1024)S(1)} %maximum_reduce_fusion), kind=kOutput, calls=%fused_computation.5 | convolution fusion | flops 4080697344 | bytes 23625216 | tf_op jit(solution)/shard_map/dot_general | solution.py:60
  109.1 1.9 fusion.51.own_ref
  111.0 17.0 %gather_rows.4 = bf16[4,256,1152]{2,1,0:T(8,128)(2,1)S(1)} custom-call(bf16[256,1152]{1,0:T(8,128)(2,1)S(1)} %fusion.51.own_ref), custom_call_target="tpu_custom_call" | custom-call | tf_op jit(solution)/shard_map/gather_rows/pallas_call | solution.py:131
  128.0 1.7 slice_bitcast_fusion
  129.7 4.1 copy.48
  133.8 4.1 fusion.92
  140.1 5.3 all-gather
  145.5 1.9 broadcast_multiply_fusion.3
  148.1 2.9 fusion.1
  151.0 3.1 fusion.27
  154.2 2.6 copy-done.6
  158.3 17.3 %scatter_rows.4 = f32[256,1152]{1,0:T(8,128)S(1)} custom-call(bf16[2,2,256,1152]{3,2,1,0:T(8,128)(2,1)S(1)} %bitcast.184), custom_call_target="tpu_custom_call" | custom-call | tf_op jit(solution)/shard_map/scatter_rows/pallas_call | solution.py:191
  175.7 2.5 multiply_reduce_fusion.6
  181.0 2.7 fusion.64
  183.7 16.9 %gather_rows.5 = bf16[4,256,1152]{2,1,0:T(8,128)(2,1)S(1)} custom-call(bf16[256,1152]{1,0:T(8,128)(2,1)S(1)} %get-tuple-element.60.own_ref), custom_call_target="tpu_custom_call" | custom-call | tf_op jit(solution)/shard_map/gather_rows/pallas_call | solution.py:131
  200.6 3.9 fusion.94
  204.5 3.9 fusion.93
  208.4 16.9 %gather_rows.6 = bf16[4,256,1152]{2,1,0:T(8,128)(2,1)S(1)} custom-call(bf16[256,1152]{1,0:T(8,128)(2,1)S(1)} %get-tuple-element.59.own_ref), custom_call_target="tpu_custom_call" | custom-call | tf_op jit(solution)/shard_map/gather_rows/pallas_call | solution.py:131
  225.3 6.4 %multiply_convert_fusion.1 = (bf16[1024,768]{1,0:T(8,128)(2,1)S(1)}, bf16[1024,768]{1,0:T(8,128)(2,1)S(1)}, bf16[1024,768]{1,0:T(8,128)(2,1)S(1)}) fusion(f32[1024,768]{1,0:T(8,128)} %fusion.93, f32[1024,768]{1,0:T(8,128)} %fusion.94, bf16[1024,1152]{1,0:T(8,128)(2,1)S(1)} %bitcast.178, bf16[768,1152]{1,0:T(8,128)(2,1)S(1)} %copy-done.51), kind=kOutput, calls=%fused_computation.18 | convolution fusion | flops 1823735808 | bytes 15138816 | tf_op jit(solution)/shard_map/rb,ab->ra/dot_general | solution.py:68
  231.8 2.2 fusion.95
  234.0 2.3 add_convert_fusion
  236.3 17.3 %scatter_rows.6 = f32[256,1152]{1,0:T(8,128)S(1)} custom-call(bf16[2,2,256,1152]{3,2,1,0:T(8,128)(2,1)S(1)} %bitcast.182), custom_call_target="tpu_custom_call" | custom-call | tf_op jit(solution)/shard_map/scatter_rows/pallas_call | solution.py:191
  255.3 2.2 convolution_convert_fusion.1
  257.5 16.9 %scatter_rows.5 = f32[256,1152]{1,0:T(8,128)S(1)} custom-call(bf16[2,2,256,1152]{3,2,1,0:T(8,128)(2,1)S(1)} %bitcast.185), custom_call_target="tpu_custom_call" | custom-call | tf_op jit(solution)/shard_map/scatter_rows/pallas_call | solution.py:191
  274.4 3.9 multiply_convert_fusion.5
  280.7 16.7 %gather_rows.7 = bf16[4,256,1152]{2,1,0:T(8,128)(2,1)S(1)} custom-call(bf16[256,1152]{1,0:T(8,128)(2,1)S(1)} %multiply_convert_fusion.8.own_ref), custom_call_target="tpu_custom_call" | custom-call | tf_op jit(solution)/shard_map/gather_rows/pallas_call | solution.py:131
  298.9 13.9 %multiply_reduce_fusion = (f32[4,1024]{1,0:T(4,128)S(1)}, f32[4,1024,1024]{1,2,0:T(8,128)}) fusion(f32[4,1024]{1,0:T(4,128)S(1)} %get-tuple-element.104, f32[4,1024,1024]{1,2,0:T(8,128)} %copy-done.6, bf16[1024,4,72]{0,2,1:T(8,128)(2,1)S(1)} %bitcast.209, f32[1024,3,4,72]{0,3,2,1:T(8,128)} %copy-done.8), kind=kOutput, calls=%fused_computation.1 | convolution fusion | flops 620752896 | bytes 34766848 | tf_op jit(solution)/shard_map/qhd,khd->hqk/dot_general | solution.py:913
  312.8 1.8 slice-done.2
  315.9 8.2 %multiply_convert_fusion = bf16[4,1024,1024]{1,2,0:T(8,128)(2,1)S(1)} fusion(f32[4,1024,1024]{1,2,0:T(8,128)} %get-tuple-element.107, f32[4,1024]{1,0:T(4,128)S(1)} %get-tuple-element.106, f32[4,1024]{1,0:T(4,128)S(1)} %get-tuple-element.104, f32[4,1024,1024]{1,2,0:T(8,128)S(1)} %bitcast.187), kind=kLoop, calls=%fused_computation | loop fusion | flops 20971520 | bytes 41975808 | tf_op jit(solution)/shard_map/convert_element_type | solution.py:915
  327.3 6.1 %broadcast_multiply_fusion = (f32[1024,4,72]{0,2,1:T(8,128)S(1)}, f32[1024,4,72]{0,2,1:T(8,128)S(1)}, f32[1024,4,72]{0,2,1:T(8,128)S(1)}) fusion(f32[1024,72]{0,1:T(8,128)S(1)} %copy-done.34, f32[1024,4,72]{0,2,1:T(8,128)S(1)} %convolution_bitcast_fusion.1, bf16[1024,4,72]{0,2,1:T(8,128)(2,1)S(1)} %copy-done.19, bf16[4,1024,1024]{1,2,0:T(8,128)(2,1)} %copy-done.7), kind=kOutput, calls=%fused_computation.118 | convolution fusion | flops 604569600 | bytes 13991936 | tf_op jit(solution)/shard_map/hqk,qhd->khd/dot_general | solution.py:920
  336.4 2.9 multiply_reduce_fusion.2
  340.1 2.7 pad_maximum_fusion.2.refs_11_
  343.5 5.0 fusion.33
  350.3 3.2 convolution_convert_fusion
  353.6 17.3 %scatter_rows.7 = f32[256,1152]{1,0:T(8,128)S(1)} custom-call(bf16[2,2,256,1152]{3,2,1,0:T(8,128)(2,1)S(1)} %bitcast.183), custom_call_target="tpu_custom_call" | custom-call | tf_op jit(solution)/shard_map/scatter_rows/pallas_call | solution.py:191
  370.9 1.7 fusion.52
  372.7 2.8 fusion.57
  377.7 2.5 copy.54.refs_8_
  380.2 2.3 copy.53.refs_5_
  383.7 171.3 %weight_grads.1 = (f32[96,1152]{1,0:T(8,128)}, f32[36,3072]{1,0:T(8,128)}, f32[36,3072]{1,0:T(8,128)}, f32[36,1152]{1,0:T(8,128)}, f32[4,36,864]{2,1,0:T(8,128)}...) custom-call(bf16[1024,768]{1,0:T(8,128)(2,1)} %copy-done.33, bf16[1024,1152]{1,0:T(8,128)(2,1)} %bitcast.179, ...), custom_call_target="tpu_custom_call" | custom-call | tf_op jit(solution)/shard_map/weight_grads/pallas_call | solution.py:724
  556.6 2.3 pad_maximum_fusion.3
  562.3 6.1 %fusion.2 = f32[256,1152]{1,0:T(8,128)S(1)} fusion(bf16[1152,6912]{1,0:T(8,128)(2,1)} %bitcast.202, bf16[256,1152]{1,0:T(8,128)(2,1)S(1)} %copy-done.22, bf16[256,1152]{1,0:T(8,128)(2,1)S(1)} %copy-done.21, bf16[256,1152]{1,0:T(8,128)(2,1)} %get-tuple-element.73), kind=kOutput, calls=%fused_computation.6 | convolution fusion | flops 2043740160 | bytes 10911744 | tf_op jit(solution)/shard_map/rb,ab->ra/dot_general | solution.py:68
  568.5 7.0 %fusion.17 = f32[1,256,1152]{2,1,0:T(8,128)} fusion(f32[256,1152]{1,0:T(8,128)S(1)} %fusion.2, bf16[1152,6912]{1,0:T(8,128)(2,1)} %bitcast.203, bf16[1,256,1152]{2,1,0:T(8,128)(2,1)S(1)} %copy-done.37, f32[1152]{0:T(1024)S(1)} %copy-done.45, bf16[256,1152]{1,0:T(8,128)(2,1)S(1)} %copy-done.20, bf16[256,1152]{1,0:T(8,128)(2,1)S(1)} %copy-done.24, ...), kind=kOutput, calls=%fused_computation.25 | convolution fusion | flops 2046984192 | bytes 12685824 | tf_op jit(solution)/shard_map/rb,ab->ra/dot_general | solution.py:68
  (184 shorter events, 35.1 us)
Async XLA Ops:
  0.6 156.1 %copy-start = (bf16[288,1152]{1,0:T(8,128)(2,1)S(1)}, bf16[288,1152]{1,0:T(8,128)(2,1)}, u32[]{:S(2)}) copy-start(bf16[288,1152]{1,0:T(8,128)(2,1)} %param.19) | copy-start | bytes 1990660
  17.4 78.4 %copy-start.35 = (bf16[1,256,1152]{2,1,0:T(8,128)(2,1)S(1)}, bf16[1,256,1152]{2,1,0:T(8,128)(2,1)}, u32[]{:S(2)}) copy-start(bf16[1,256,1152]{2,1,0:T(8,128)(2,1)} %param.16) | copy-start | bytes 1769476
  17.4 78.4 %copy-start.54 = (f32[6912]{0:T(1024)S(1)}, f32[6912]{0:T(1024)}, u32[]{:S(2)}) copy-start(f32[6912]{0:T(1024)} %param.24) | copy-start | bytes 82948
  95.8 12.5 %copy-start.44 = (f32[1152]{0:T(1024)}, f32[1152]{0:T(1024)S(1)}, u32[]{:S(2)}) copy-start(f32[1152]{0:T(1024)S(1)} %maximum_reduce_fusion) | copy-start | bytes 13828
  95.8 12.5 %copy-start.11 = (bf16[1,256,1152]{2,1,0:T(8,128)(2,1)S(1)}, bf16[1,256,1152]{2,1,0:T(8,128)(2,1)}, u32[]{:S(2)}) copy-start(bf16[1,256,1152]{2,1,0:T(8,128)(2,1)} %param.15) | copy-start | bytes 1769476
  111.0 17.0 %copy-start.29 = (bf16[4,288,1024]{2,1,0:T(8,128)(2,1)S(1)}, bf16[4,288,1024]{2,1,0:T(8,128)(2,1)}, u32[]{:S(2)}) copy-start(bf16[4,288,1024]{2,1,0:T(8,128)(2,1)} %get-tuple-element.25) | copy-start | bytes 7077892
  128.0 5.8 %copy-start.2 = (bf16[4,256,1152]{2,1,0:T(8,128)(2,1)}, bf16[4,256,1152]{2,1,0:T(8,128)(2,1)S(1)}, u32[]{:S(2)}) copy-start(bf16[4,256,1152]{2,1,0:T(8,128)(2,1)S(1)} %gather_rows.4) | copy-start | bytes 7077892
  137.9 13.2 %copy-start.8 = (f32[1024,3,4,72]{0,3,2,1:T(8,128)}, f32[1024,3,4,72]{0,3,2,1:T(8,128)S(1)}, u32[]{:S(2)}) copy-start(f32[1024,3,4,72]{0,3,2,1:T(8,128)S(1)} %fusion.92) | copy-start | bytes 10616836
  148.1 2.9 copy-start.16
  148.1 2.9 copy-start.18
  151.0 5.7 copy-start.6
  158.3 17.4 %copy-start.12 = (bf16[1,256,1152]{2,1,0:T(8,128)(2,1)S(1)}, bf16[1,256,1152]{2,1,0:T(8,128)(2,1)}, u32[]{:S(2)}) copy-start(bf16[1,256,1152]{2,1,0:T(8,128)(2,1)} %param.15) | copy-start | bytes 1769476
  175.7 2.6 copy-start.55
  175.7 5.3 copy-start.27
  183.7 16.9 %copy-start.52 = (bf16[4,288,768]{2,1,0:T(8,128)(2,1)S(1)}, bf16[4,288,768]{2,1,0:T(8,128)(2,1)}, u32[]{:S(2)}) copy-start(bf16[4,288,768]{2,1,0:T(8,128)(2,1)} %get-tuple-element.27) | copy-start | bytes 5308420
  200.6 3.9 copy-start.3
  200.6 3.9 copy-start.53
  208.4 17.0 %copy-start.51 = (bf16[768,1152]{1,0:T(8,128)(2,1)S(1)}, bf16[768,1152]{1,0:T(8,128)(2,1)}, u32[]{:S(2)}) copy-start(bf16[768,1152]{1,0:T(8,128)(2,1)} %param.22) | copy-start | bytes 5308420
  225.3 6.4 %copy-start.4 = (bf16[4,256,1152]{2,1,0:T(8,128)(2,1)}, bf16[4,256,1152]{2,1,0:T(8,128)(2,1)S(1)}, u32[]{:S(2)}) copy-start(bf16[4,256,1152]{2,1,0:T(8,128)(2,1)S(1)} %gather_rows.6) | copy-start | bytes 7077892
  231.7 2.3 copy-start.32
  231.8 2.3 copy-start.31
  231.8 23.5 %copy-start.33 = (bf16[1024,768]{1,0:T(8,128)(2,1)}, bf16[1024,768]{1,0:T(8,128)(2,1)S(1)}, u32[]{:S(2)}) copy-start(bf16[1024,768]{1,0:T(8,128)(2,1)S(1)} %get-tuple-element.63.refs_0_) | copy-start | bytes 4718596
  236.3 17.4 %copy-start.10 = (f32[256,1152]{1,0:T(8,128)S(1)}, f32[256,1152]{1,0:T(8,128)}, u32[]{:S(2)}) copy-start(f32[256,1152]{1,0:T(8,128)} %get-tuple-element.57) | copy-start | bytes 3538948
  257.5 16.9 %copy-start.28 = (bf16[1,256,1152]{2,1,0:T(8,128)(2,1)S(1)}, bf16[1,256,1152]{2,1,0:T(8,128)(2,1)}, u32[]{:S(2)}) copy-start(bf16[1,256,1152]{2,1,0:T(8,128)(2,1)} %param.17) | copy-start | bytes 1769476
  298.9 13.9 %copy-start.56 = (bf16[1024,288]{0,1:T(8,128)(2,1)}, bf16[1024,288]{0,1:T(8,128)(2,1)S(1)}, u32[]{:S(2)}) copy-start(bf16[1024,288]{0,1:T(8,128)(2,1)S(1)} %convolution_convert_fusion.3) | copy-start | bytes 1769476
  298.9 13.9 %slice-start = ((s8[16777216]{0:T(1024)(128)(4,1)}), s8[4194304]{0:T(1024)(128)(4,1)S(1)}, s32[]{:S(2)}) async-start(s8[16777216]{0:T(1024)(128)(4,1)} %bitcast.186), calls=%async_computation | async-start | bytes 8388608
  298.9 13.9 %slice-start.1 = ((s8[16777216]{0:T(1024)(128)(4,1)}), s8[4194304]{0:T(1024)(128)(4,1)S(1)}, s32[]{:S(2)}) async-start(s8[16777216]{0:T(1024)(128)(4,1)} %bitcast.186), calls=%async_computation.1 | async-start | bytes 8388608
  298.9 15.8 %slice-start.2 = ((s8[16777216]{0:T(1024)(128)(4,1)}), s8[4194304]{0:T(1024)(128)(4,1)S(1)}, s32[]{:S(2)}) async-start(s8[16777216]{0:T(1024)(128)(4,1)} %bitcast.186), calls=%async_computation.2 | async-start | bytes 8388608
  298.9 17.0 %slice-start.3 = ((s8[16777216]{0:T(1024)(128)(4,1)}), s8[4194304]{0:T(1024)(128)(4,1)S(1)}, s32[]{:S(2)}) async-start(s8[16777216]{0:T(1024)(128)(4,1)} %bitcast.186), calls=%async_computation.3 | async-start | bytes 8388608
  315.9 8.2 %copy-start.17 = (bf16[1024,4,72]{0,2,1:T(8,128)(2,1)S(1)}, bf16[1024,4,72]{0,2,1:T(8,128)(2,1)}, u32[]{:S(2)}) copy-start(bf16[1024,4,72]{0,2,1:T(8,128)(2,1)} %copy-done.16) | copy-start | bytes 1769476
  324.0 3.2 copy-start.7
  324.0 3.2 copy-start.19
  324.1 3.2 copy-start.34
  333.4 3.0 copy-start.9
  353.5 17.4 %copy-start.13 = (bf16[1,256,1152]{2,1,0:T(8,128)(2,1)S(1)}, bf16[1,256,1152]{2,1,0:T(8,128)(2,1)}, u32[]{:S(2)}) copy-start(bf16[1,256,1152]{2,1,0:T(8,128)(2,1)} %param.15) | copy-start | bytes 1769476
  353.5 17.4 %copy-start.47 = (f32[256]{0:T(256)S(1)}, f32[256]{0:T(256)}, u32[]{:S(2)}) copy-start(f32[256]{0:T(256)} %copy-done.46) | copy-start | bytes 3076
  372.7 3.6 copy-start.20
  380.2 2.3 copy-start.36
  380.2 2.3 copy-start.45
  555.8 3.1 copy-start.39
  559.6 2.6 copy-start.21
  559.8 2.4 copy-start.22
  562.2 6.2 %copy-start.24 = (bf16[256,1152]{1,0:T(8,128)(2,1)S(1)}, bf16[256,1152]{1,0:T(8,128)(2,1)}, u32[]{:S(2)}) copy-start(bf16[256,1152]{1,0:T(8,128)(2,1)} %copy-done.23) | copy-start | bytes 1769476
  562.2 6.2 %copy-start.26 = (bf16[256,1152]{1,0:T(8,128)(2,1)S(1)}, bf16[256,1152]{1,0:T(8,128)(2,1)}, u32[]{:S(2)}) copy-start(bf16[256,1152]{1,0:T(8,128)(2,1)} %copy-done.25) | copy-start | bytes 1769476
  562.3 6.2 %copy-start.37 = (bf16[1,256,1152]{2,1,0:T(8,128)(2,1)S(1)}, bf16[1,256,1152]{2,1,0:T(8,128)(2,1)}, u32[]{:S(2)}) copy-start(bf16[1,256,1152]{2,1,0:T(8,128)(2,1)} %param.16) | copy-start | bytes 1769476
  568.4 7.0 %copy-start.43 = (f32[36,1152]{1,0:T(8,128)S(1)}, f32[36,1152]{1,0:T(8,128)}, u32[]{:S(2)}) copy-start(f32[36,1152]{1,0:T(8,128)} %get-tuple-element.127) | copy-start | bytes 497668
  568.4 7.7 %copy-start.41 = (f32[36,3072]{1,0:T(8,128)S(1)}, f32[36,3072]{1,0:T(8,128)}, u32[]{:S(2)}) copy-start(f32[36,3072]{1,0:T(8,128)} %get-tuple-element.128) | copy-start | bytes 1327108
  576.1 2.3 copy-start.1
  (13 other events, 17.0 us)

commit v3 on v1

v3 whole, which is shorter than its diff:
```python
import math

import jax
import jax.numpy as jnp
from jax import lax
from jax.experimental import pallas as pl
from jax.experimental.pallas import tpu as pltpu
from jax.sharding import PartitionSpec as P

HEADS = 16
HD = 72
EPSILON = 1e-06
BF16 = jnp.bfloat16
F32 = jnp.float32


def inverse_rms(values):
    return lax.rsqrt(jnp.mean(values * values, axis=-1, keepdims=True) + EPSILON)


def rms_back(grad_in, normed, inverse):
    return inverse * (grad_in - normed * jnp.mean(grad_in * normed, axis=-1, keepdims=True))


def silu_slope(values):
    logistic = jax.nn.sigmoid(values)
    return logistic * (1.0 + values * (1.0 - logistic))


def time_embed(steps, width):
    half_width = width // 2
    frequency = jnp.exp(-math.log(10000.0) * jnp.arange(half_width, dtype=F32) / half_width)
    angles = steps.astype(F32)[:, None] * frequency[None, :]
    return jnp.concatenate([jnp.cos(angles), jnp.sin(angles)], axis=-1)


def rope_tables(positions, head_size):
    quarter = head_size // 4
    frequency = jnp.exp(-math.log(10000.0) * jnp.arange(quarter, dtype=F32) / quarter)
    along_rows = positions[0].astype(F32)[..., None] * frequency
    along_cols = positions[1].astype(F32)[..., None] * frequency
    angles = jnp.concatenate([along_rows, along_rows, along_cols, along_cols], axis=-1)
    return (jnp.cos(angles)[..., None, :], jnp.sin(angles)[..., None, :])


def quarter_turn(values):
    first, second, third, fourth = jnp.split(values, 4, axis=-1)
    return jnp.concatenate([-second, first, -fourth, third], axis=-1)


def rotate_heads(values, cosine, sine):
    return values * cosine + quarter_turn(values) * sine


def unrotate(grad_in, cosine, sine):
    return grad_in * cosine - quarter_turn(grad_in * sine)


def matmul(left, right):
    return jnp.dot(left, right, preferred_element_type=F32)


def outer_sum(left, right):
    return jnp.einsum("ra,rb->ab", left, right, preferred_element_type=F32)


def times_transpose(left, right):
    return jnp.einsum("rb,ab->ra", left, right, preferred_element_type=F32)


MESH = pl.DeviceIdType.MESH
SUM_ID, GATHER_ID, SCATTER_ID, WEIGHT_ID, ATTEND_ID, BACK_ID = 1, 2, 3, 4, 5, 6


def greet(partners):
    barrier = pltpu.get_barrier_semaphore()
    for partner in partners:
        pl.semaphore_signal(barrier, inc=1, device_id=partner, device_id_type=MESH)
    pl.semaphore_wait(barrier, len(partners))


def group_partners():
    item, column = lax.axis_index("dp"), lax.axis_index("seq")
    core = lax.rem(column, 2)
    return (item, column + 1 - 2 * core), (item, lax.rem(column + 2, 4))


GATHER_PIECES = 4


def gather_kernel(own_ref, out_ref, local_sem, send_sem, recv_sem):
    column = lax.axis_index("seq")
    sibling, across = group_partners()
    greet([sibling, across])
    local = pltpu.make_async_copy(own_ref, out_ref.at[column], local_sem)
    local.start()
    rows = own_ref.shape[0] // GATHER_PIECES

    def remote(source, place, piece, kind, target):
        part = pl.ds(piece * rows, rows)
        return pltpu.make_async_remote_copy(
            src_ref=source.at[part],
            dst_ref=out_ref.at[place, part],
            send_sem=send_sem.at[kind, piece],
            recv_sem=recv_sem.at[kind, piece],
            device_id=target,
            device_id_type=MESH,
        )

    far = lax.rem(column + 2, 4)
    pieces = range(GATHER_PIECES)
    over = [remote(own_ref, column, piece, 0, across) for piece in pieces]
    beside = [remote(own_ref, column, piece, 1, sibling) for piece in pieces]
    onward = [remote(out_ref.at[far], far, piece, 2, sibling) for piece in pieces]
    for copy in over:
        copy.start()
    for copy in beside:
        copy.start()
    for piece in pieces:
        over[piece].wait_recv()
        onward[piece].start()
    for piece in pieces:
        over[piece].wait_send()
        beside[piece].wait()
        onward[piece].wait()
    local.wait()


def gather_rows(values):
    rows, columns = values.shape
    gathered = pl.pallas_call(
        gather_kernel,
        out_shape=jax.ShapeDtypeStruct((4, rows, columns), values.dtype),
        in_specs=[pl.BlockSpec(memory_space=pltpu.VMEM)],
        out_specs=pl.BlockSpec(memory_space=pltpu.VMEM),
        scratch_shapes=[
            pltpu.SemaphoreType.DMA,
            pltpu.SemaphoreType.DMA((3, GATHER_PIECES)),
            pltpu.SemaphoreType.DMA((3, GATHER_PIECES)),
        ],
        compiler_params=pltpu.CompilerParams(
            collective_id=GATHER_ID, has_side_effects=True, vmem_limit_bytes=48 * 2**20
        ),
        name="gather_rows",
    )(values)
    return gathered.reshape(4 * rows, columns)


def scatter_kernel(parts_ref, out_ref, near, low, far, send_sem, recv_sem):
    column = lax.axis_index("seq")
    core, chip = lax.rem(column, 2), column // 2
    sibling, across = group_partners()
    greet([sibling, across])
    rows = out_ref.shape[0] // 2

    def remote(source, target_ref, index, target):
        return pltpu.make_async_remote_copy(
            src_ref=source,
            dst_ref=target_ref,
            send_sem=send_sem.at[index],
            recv_sem=recv_sem.at[index],
            device_id=target,
            device_id_type=MESH,
        )

    parts = [pl.ds(piece * rows, rows) for piece in range(2)]
    beside = [
        remote(parts_ref.at[1 - chip, 1 - core, part], near.at[0, part], i, sibling)
        for i, part in enumerate(parts)
    ]
    beside.append(remote(parts_ref.at[chip, 1 - core], near.at[1], 2, sibling))
    for copy in beside:
        copy.start()
    over = [remote(low.at[part], far.at[part], 3 + i, across) for i, part in enumerate(parts)]
    for i, part in enumerate(parts):
        beside[i].wait_recv()
        pair = parts_ref[1 - chip, core, part].astype(F32) + near[0, part].astype(F32)
        low[part] = pair.astype(BF16)
        over[i].start()
    beside[2].wait_recv()
    out_ref[...] = parts_ref[chip, core].astype(F32) + near[1].astype(F32)
    for i, part in enumerate(parts):
        over[i].wait()
        out_ref[part] += far[part].astype(F32)
    for copy in beside:
        copy.wait_send()


def scatter_rows(partial):
    rows, columns = partial.shape[0] // 4, partial.shape[1]
    return pl.pallas_call(
        scatter_kernel,
        out_shape=jax.ShapeDtypeStruct((rows, columns), F32),
        in_specs=[pl.BlockSpec(memory_space=pltpu.VMEM)],
        out_specs=pl.BlockSpec(memory_space=pltpu.VMEM),
        scratch_shapes=[
            pltpu.VMEM((2, rows, columns), BF16),
            pltpu.VMEM((rows, columns), BF16),
            pltpu.VMEM((rows, columns), BF16),
            pltpu.SemaphoreType.DMA((5,)),
            pltpu.SemaphoreType.DMA((5,)),
        ],
        compiler_params=pltpu.CompilerParams(
            collective_id=SCATTER_ID, has_side_effects=True, vmem_limit_bytes=48 * 2**20
        ),
        name="scatter_rows",
    )(partial.astype(BF16).reshape(2, 2, rows, columns))


TILE = 128
LANES = 128
QUARTER = HD // 4
FIRST_ROWS = 80


class WeightImport:
    def __init__(self, blocks, base):
        self.blocks, self.base = blocks, base
        self.arrays = sorted({block[0] for block in blocks})

    def scratch(self):
        count = len(self.blocks)
        return [
            pltpu.SemaphoreType.DMA((4,)),
            pltpu.SemaphoreType.DMA((count, 7)),
            pltpu.SemaphoreType.DMA((count, 7)),
        ]

    def bind(self, ins, outs, scratch):
        self.ins, self.outs = ins, outs
        self.own_sem, self.send_sem, self.recv_sem = scratch
        item, column = lax.axis_index("dp"), lax.axis_index("seq")
        core, chip = lax.rem(column, 2), column // 2
        self.item, self.column = item, column
        self.y_bit, self.z_bit = lax.rem(item, 2), lax.rem(item // 2, 2)
        self.sibling = (item, column + 1 - 2 * core)
        self.y_near = (item + 1 - 2 * self.y_bit, column)
        self.z_near = (item + 2 - 4 * self.z_bit, column)
        self.far = [(1 - chip) * 2 + k for k in (core, 1 - core)]
        self.half_rows = ins[0].shape[0] // 2

    def partners(self):
        across = [(self.item, place) for place in self.far]
        return across + [self.sibling, self.y_near, self.z_near]

    def copy(self, source, target_ref, block, kind, target):
        return pltpu.make_async_remote_copy(
            src_ref=source,
            dst_ref=target_ref,
            send_sem=self.send_sem.at[block, kind],
            recv_sem=self.recv_sem.at[block, kind],
            device_id=target,
            device_id_type=MESH,
        )

    def piece(self, ref, block, y_pick, z_pick, first_row=0, rows=None, base=0):
        _, _, start, columns = self.blocks[block]
        rows = self.half_rows if rows is None else rows
        return ref.at[
            pl.ds(pl.multiple_of(z_pick * self.half_rows + first_row, 16), rows),
            pl.ds(pl.multiple_of(base + start + y_pick * columns, TILE), columns),
        ]

    def mine_for(self, array, place):
        ref = self.ins[array]
        if len(ref.shape) == 3:
            return ref.at[place], 0
        return ref, self.base if array == 0 else place * self.outs[array].shape[2]

    def whole(self, array, place):
        ref, base = self.mine_for(array, place)
        columns = self.outs[array].shape[2]
        if ref.shape[-1] == columns:
            return ref
        return ref.at[:, pl.ds(pl.multiple_of(base, TILE), columns)]

    def over(self, block):
        array, offset, _, _ = self.blocks[block]
        goal = self.far[offset or 0]
        ref, base = self.mine_for(array, goal)
        source = self.piece(ref, block, self.y_bit, self.z_bit, base=base)
        target = self.piece(self.outs[array].at[self.column], block, self.y_bit, self.z_bit)
        return self.copy(source, target, block, 0, (self.item, goal))

    def onward(self, block, kind):
        array, offset, _, _ = self.blocks[block]
        ref = self.outs[array].at[self.far[offset or 0]]
        if kind == 1:
            part, target = self.piece(ref, block, self.y_bit, self.z_bit), self.y_near
        elif kind == 2:
            part, target = self.piece(ref, block, self.y_bit, self.z_bit), self.z_near
        elif kind == 3:
            part = self.piece(ref, block, 1 - self.y_bit, self.z_bit, 0, FIRST_ROWS)
            target = self.z_near
        else:
            rest = self.half_rows - FIRST_ROWS
            part = self.piece(ref, block, self.y_bit, 1 - self.z_bit, FIRST_ROWS, rest)
            target = self.y_near
        return self.copy(part, part, block, kind, target)

    def share(self, block):
        _, _, start, columns = self.blocks[block]
        part = self.outs[0].at[self.far[0], :, pl.ds(start, 2 * columns)]
        return self.copy(part, part, block, 5, self.sibling)

    def beside(self, array):
        source = self.whole(array, self.sibling[1])
        index = self.arrays.index(array)
        return self.copy(source, self.outs[array].at[self.column], index, 6, self.sibling)

    def own(self, array):
        source = self.whole(array, self.column)
        return pltpu.make_async_copy(source, self.outs[array].at[self.column], self.own_sem.at[array])

    def steps(self):
        count = len(self.blocks)
        todo = []
        for step in range(count + 3):
            if step < count:
                todo.append(lambda step=step: self.arrive(step))
            if 0 <= step - 1 < count:
                todo.append(lambda step=step: self.pass_on(step - 1))
            if 0 <= step - 2 < count:
                todo.append(lambda step=step: self.complete(step - 2))
        return todo

    def arrive(self, step):
        self.over(step).wait_recv()
        self.onward(step, 1).start()
        self.onward(step, 2).start()

    def pass_on(self, step):
        self.onward(step, 1).wait_recv()
        self.onward(step, 3).start()
        self.onward(step, 2).wait_recv()
        self.onward(step, 4).start()

    def complete(self, step):
        self.onward(step, 3).wait_recv()
        self.onward(step, 4).wait_recv()
        if self.blocks[step][0] == 0:
            self.share(step).start()

    def end(self):
        for block in range(len(self.blocks)):
            self.over(block).wait_send()
            for kind in range(1, 5):
                self.onward(block, kind).wait_send()
            if self.blocks[block][0] == 0:
                self.share(block).wait_send()


class RowGather:
    def __init__(self, own, everyone, local_sem, send_sem, recv_sem):
        self.own, self.everyone = own, everyone
        self.local_sem, self.send_sem, self.recv_sem = local_sem, send_sem, recv_sem
        self.column = lax.axis_index("seq")
        self.far = lax.rem(self.column + 2, 4)
        self.sibling, self.across = group_partners()

    def remote(self, source, place, piece, kind, target):
        rows = self.own.shape[0] // GATHER_PIECES
        part = pl.ds(piece * rows, rows)
        return pltpu.make_async_remote_copy(
            src_ref=source.at[part],
            dst_ref=self.everyone.at[place, part],
            send_sem=self.send_sem.at[kind, piece],
            recv_sem=self.recv_sem.at[kind, piece],
            device_id=target,
            device_id_type=MESH,
        )

    def over(self, piece):
        return self.remote(self.own, self.column, piece, 0, self.across)

    def beside(self, piece):
        return self.remote(self.own, self.column, piece, 1, self.sibling)

    def onward(self, piece):
        return self.remote(self.everyone.at[self.far], self.far, piece, 2, self.sibling)

    def local(self):
        return pltpu.make_async_copy(self.own, self.everyone.at[self.column], self.local_sem)

    def start(self):
        for piece in range(GATHER_PIECES):
            self.over(piece).start()
        for piece in range(GATHER_PIECES):
            self.beside(piece).start()
        self.local().start()

    def pass_on(self):
        for piece in range(GATHER_PIECES):
            self.over(piece).wait_recv()
            self.onward(piece).start()

    def end(self):
        for piece in range(GATHER_PIECES):
            self.over(piece).wait_send()
            self.beside(piece).wait()
            self.onward(piece).wait()
        self.local().wait()

    @staticmethod
    def scratch():
        return [
            pltpu.SemaphoreType.DMA,
            pltpu.SemaphoreType.DMA((3, GATHER_PIECES)),
            pltpu.SemaphoreType.DMA((3, GATHER_PIECES)),
        ]


MOD_BLOCK = 2304


def first_import():
    wide = 3 * HEADS // 4 * LANES
    return WeightImport([(0, None, 0, MOD_BLOCK // 2), (1, 0, 0, wide // 2), (1, 1, 0, wide // 2)], 0)


def second_import(ff):
    blocks = [(0, None, 0, MOD_BLOCK // 2)]
    blocks += [(k, j, 0, ff // 2) for k in (2, 3) for j in (0, 1)]
    return WeightImport(blocks + [(0, None, MOD_BLOCK, MOD_BLOCK // 2)], MOD_BLOCK)


def spread_heads(w_ref, lanes_ref):
    rows = w_ref.shape[0]
    valid = lax.broadcasted_iota(jnp.int32, (rows, LANES), 1) < HD
    for head in range(3 * HEADS):
        kind, device, place = head // HEADS, head % HEADS // 4, head % 4
        start = head * HD // LANES * LANES
        stop = min(start + 2 * LANES, w_ref.shape[1])
        window = w_ref[:, start:stop].astype(F32)
        shift = head * HD - start
        if shift:
            window = pltpu.roll(window, window.shape[1] - shift, 1)
        target = (kind * 4 + place) * LANES
        lanes_ref[device, :, target : target + LANES] = jnp.where(
            valid, window[:, :LANES], 0.0
        ).astype(BF16)


def first_kernel(imports, *refs):
    (w_mod, w_qkv, condition, tokens, embed, bias, positions), refs = refs[:7], refs[7:]
    (mod_out, qkv_out, modulation_out, hidden_all, lifted, positions_all), refs = refs[:6], refs[6:]
    (mod_all, lanes, hidden, mod_sem, spot_send, spot_recv), refs = refs[:6], refs[6:]
    imports.bind({0: w_mod, 1: lanes}, {0: mod_all, 1: qkv_out}, refs[:3])
    gather = RowGather(hidden, hidden_all, *refs[3:6])
    item, column = lax.axis_index("dp"), lax.axis_index("seq")
    greet(imports.partners())
    imports.over(0).start()
    imports.own(0).start()
    imports.beside(0).start()
    peers = [(item, lax.rem(column + k, 4)) for k in range(1, 4)]
    spot_copies = [
        pltpu.make_async_remote_copy(
            src_ref=positions,
            dst_ref=positions_all.at[column],
            send_sem=spot_send.at[k],
            recv_sem=spot_recv.at[k],
            device_id=peer,
            device_id_type=MESH,
        )
        for k, peer in enumerate(peers)
    ]
    for copy in spot_copies:
        copy.start()
    positions_all[column] = positions[...]
    spread_heads(w_qkv, lanes)
    imports.over(1).start()
    imports.over(2).start()
    imports.own(1).start()
    imports.beside(1).start()
    values = condition[...].astype(F32) + embed[...]
    lifted[...] = (values * jax.nn.sigmoid(values)).astype(BF16)
    todo = imports.steps()
    for step in todo[:5]:
        step()
    imports.complete(0)
    imports.own(0).wait()
    imports.beside(0).wait_recv()
    imports.share(0).wait_recv()
    store = pltpu.make_async_copy(mod_all, mod_out, mod_sem)
    store.start()
    weights = mod_all[...].reshape(-1, mod_all.shape[2])
    modulation = jnp.dot(lifted[...], weights, preferred_element_type=F32)
    modulation = modulation + bias[:, : mod_all.shape[2]]
    modulation_out[...] = modulation
    width = tokens.shape[1]
    values = tokens[...].astype(F32)
    normed = values * inverse_rms(values)
    hidden[...] = (normed * (1.0 + modulation[:, width:]) + modulation[:, :width]).astype(BF16)
    gather.start()
    for step in todo[6:]:
        step()
    gather.pass_on()
    imports.end()
    imports.beside(0).wait_send()
    imports.beside(1).wait()
    imports.own(1).wait()
    gather.end()
    for copy in spot_copies:
        copy.wait()
    store.wait()


def first_stage(w_mod, w_qkv, condition, tokens, embed, bias, positions):
    rows, width = tokens.shape
    depth, lanes = w_mod.shape[0], 3 * HEADS // 4 * LANES
    imports = first_import()
    vmem, anywhere = pl.BlockSpec(memory_space=pltpu.VMEM), pl.BlockSpec(memory_space=pl.ANY)

    def kernel(*refs):
        first_kernel(imports, *refs)

    return pl.pallas_call(
        kernel,
        out_shape=[
            jax.ShapeDtypeStruct((4, depth, MOD_BLOCK), BF16),
            jax.ShapeDtypeStruct((4, depth, lanes), BF16),
            jax.ShapeDtypeStruct((rows, MOD_BLOCK), F32),
            jax.ShapeDtypeStruct((4, rows, width), BF16),
            jax.ShapeDtypeStruct((rows, width), BF16),
            jax.ShapeDtypeStruct((4,) + positions.shape, jnp.int32),
        ],
        in_specs=[anywhere] + [vmem] * 6,
        out_specs=[anywhere, anywhere] + [vmem] * 4,
        scratch_shapes=[
            pltpu.VMEM((4, depth, MOD_BLOCK), BF16),
            pltpu.VMEM((4, depth, lanes), BF16),
            pltpu.VMEM((rows, width), BF16),
            pltpu.SemaphoreType.DMA,
            pltpu.SemaphoreType.DMA((3,)),
            pltpu.SemaphoreType.DMA((3,)),
        ]
        + imports.scratch()
        + RowGather.scratch(),
        compiler_params=pltpu.CompilerParams(
            collective_id=WEIGHT_ID, has_side_effects=True, vmem_limit_bytes=60 * 2**20
        ),
        name="first_stage",
    )(w_mod, w_qkv, condition, tokens, embed, bias, positions)


def rotated(values, tables, sign):
    cosine, ahead, behind = tables
    turned = pltpu.roll(values, LANES - QUARTER, 1) * ahead + pltpu.roll(values, QUARTER, 1) * behind
    return values * cosine + turned if sign > 0 else values * cosine - turned


def lane_tables(positions):
    cosine, sine = rope_tables(positions, HD)
    cosine, sine = cosine[:, 0], sine[:, 0]
    takes_ahead = (jnp.arange(HD) // QUARTER % 2 == 0)[None, :]
    tables = (cosine, jnp.where(takes_ahead, -sine, 0.0), jnp.where(takes_ahead, 0.0, sine))
    return [jnp.pad(table, ((0, 0), (0, LANES - HD))) for table in tables]


def head_inverse(values):
    return lax.rsqrt(jnp.sum(values * values, axis=-1, keepdims=True) * (1.0 / HD) + EPSILON)


def over_rows(left, right):
    return lax.dot_general(left, right, (((1,), (1,)), ((), ())), preferred_element_type=F32)


def over_first(left, right):
    return lax.dot_general(left, right, (((0,), (0,)), ((), ())), preferred_element_type=F32)


class RowSums:
    def __init__(self, blocks, near, low, far, send_sem, recv_sem):
        column = lax.axis_index("seq")
        self.column = column
        self.core, self.chip = lax.rem(column, 2), column // 2
        self.sibling, self.across = group_partners()
        self.blocks, self.near, self.low, self.far = blocks, near, low, far
        self.send_sem, self.recv_sem = send_sem, recv_sem
        self.order = [
            (1 - self.chip) * 2 + 1 - self.core,
            (1 - self.chip) * 2 + self.core,
            self.chip * 2 + 1 - self.core,
            column,
        ]

    def copy(self, source, target_ref, index, target):
        return pltpu.make_async_remote_copy(
            src_ref=source,
            dst_ref=target_ref,
            send_sem=self.send_sem.at[index],
            recv_sem=self.recv_sem.at[index],
            device_id=target,
            device_id_type=MESH,
        )

    def beside(self, index):
        return self.copy(self.blocks.at[index], self.near.at[index], index, self.sibling)

    def over(self):
        return self.copy(self.low, self.far, 2, self.across)

    def put(self, index, values):
        if index == 0 or index == 2:
            self.blocks[index // 2] = values.astype(BF16)
            self.beside(index // 2).start()
        elif index == 1:
            self.beside(0).wait_recv()
            self.low[...] = (values + self.near[0].astype(F32)).astype(BF16)
            self.over().start()
        else:
            self.own = values

    def sums(self):
        self.beside(1).wait_recv()
        total = self.own + self.near[1].astype(F32)
        self.over().wait()
        total = total + self.far[...].astype(F32)
        self.beside(0).wait_send()
        self.beside(1).wait_send()
        return total

    @staticmethod
    def scratch(rows, columns):
        return [
            pltpu.VMEM((2, rows, columns), BF16),
            pltpu.VMEM((2, rows, columns), BF16),
            pltpu.VMEM((rows, columns), BF16),
            pltpu.VMEM((rows, columns), BF16),
            pltpu.SemaphoreType.DMA((3,)),
            pltpu.SemaphoreType.DMA((3,)),
        ]


def attend_kernel(imports, *refs):
    (hidden, w_qkv, w_out, cosine, ahead, behind, q_gain, k_gain), refs = refs[:8], refs[8:]
    (w_mod, w_gate, w_up, lifted, bias), refs = refs[:5], refs[5:]
    (heads_out, rows_out, attended_out, branch_out), refs = refs[:4], refs[4:]
    (mod_out, gate_out, up_out, modulation_out), refs = refs[:4], refs[4:]
    (mod_all, gate_own, up_own, mod_sem, load_sem), refs = refs[:5], refs[5:]
    sums = RowSums(*refs[:6])
    imports.bind({0: w_mod, 2: w_gate, 3: w_up}, {0: mod_all, 2: gate_out, 3: up_out}, refs[6:])
    greet(imports.partners())
    for block in range(len(imports.blocks)):
        imports.over(block).start()
    imports.own(0).start()
    loads = [
        pltpu.make_async_copy(imports.whole(k, sums.column), ref, load_sem.at[k - 2])
        for k, ref in ((2, gate_own), (3, up_own))
    ]
    stores = [
        pltpu.make_async_copy(ref, imports.outs[k].at[sums.column], load_sem.at[k])
        for k, ref in ((2, gate_own), (3, up_own))
    ]
    for copy in loads:
        copy.start()
    for array in imports.arrays:
        imports.beside(array).start()
    todo = imports.steps()

    def aside(number):
        for _ in range(min(number, len(todo))):
            todo.pop(0)()

    factor = HD ** (-0.5)
    rows = branch_out.shape[0]
    heads = attended_out.shape[1] // LANES
    tables = cosine[...], ahead[...], behind[...]
    for pair in range(3 * heads // 2):
        span = slice(pair * 2 * LANES, (pair + 1) * 2 * LANES)
        projected = jnp.dot(hidden[...], w_qkv[:, span], preferred_element_type=F32)
        if pair >= heads:
            rows_out[:, span] = projected.astype(BF16)
            continue
        heads_out[:, span] = projected
        gain = (q_gain if pair < heads // 2 else k_gain)[...]
        for half in range(2):
            values = projected[:, half * LANES : (half + 1) * LANES]
            values = values * head_inverse(values) * gain
            start = pair * 2 * LANES + half * LANES
            rows_out[:, start : start + LANES] = rotated(values, tables, 1).astype(BF16)
        if pair == heads - 1:
            aside(1)
    aside(1)
    for copy in loads:
        copy.wait()
    for copy in stores:
        copy.start()
    for index in range(4):
        block = pl.ds(pl.multiple_of(sums.order[index] * rows, rows), rows)
        for head in range(heads):
            spans = [slice((k * heads + head) * LANES, (k * heads + head + 1) * LANES) for k in range(3)]
            exp_scores = jnp.exp(over_rows(rows_out[block, spans[0]], rows_out[:, spans[1]]) * factor)
            scale = 1.0 / jnp.sum(exp_scores, axis=1, keepdims=True)
            mixed = jnp.dot(
                (exp_scores * scale).astype(BF16),
                rows_out[:, spans[2]],
                preferred_element_type=F32,
            )
            attended_out[block, spans[0]] = mixed.astype(BF16)
            aside(1)
        sums.put(index, jnp.dot(attended_out[block, :], w_out[...], preferred_element_type=F32))
    aside(6)
    imports.own(0).wait()
    imports.beside(0).wait_recv()
    arrays = [block[0] for block in imports.blocks]
    mod_blocks = [index for index, array in enumerate(arrays) if array == 0]

    def modulate(number):
        imports.share(mod_blocks[number]).wait_recv()
        span = slice(number * MOD_BLOCK, (number + 1) * MOD_BLOCK)
        weights = mod_all[:, :, span].reshape(-1, MOD_BLOCK)
        modulation = jnp.dot(lifted[...], weights, preferred_element_type=F32)
        start = imports.base + number * MOD_BLOCK
        modulation_out[:, span] = modulation + bias[:, start : start + MOD_BLOCK]

    modulate(0)
    aside(len(todo))
    branch_out[...] = sums.sums()
    modulate(1)
    store = pltpu.make_async_copy(mod_all, mod_out, mod_sem)
    store.start()
    imports.end()
    imports.beside(0).wait_send()
    for array in imports.arrays[1:]:
        imports.beside(array).wait()
    for copy in stores:
        copy.wait()
    store.wait()


def attend(hidden, w_qkv, w_out, tables, q_gain, k_gain, w_mod, w_gate, w_up, lifted, bias):
    patches, wide = hidden.shape[0], w_qkv.shape[1]
    rows, width = patches // 4, hidden.shape[1]
    depth, ff = w_mod.shape[0], w_gate.shape[1] // 4
    rest = w_mod.shape[1] - MOD_BLOCK
    imports = second_import(ff)
    vmem, anywhere = pl.BlockSpec(memory_space=pltpu.VMEM), pl.BlockSpec(memory_space=pl.ANY)

    def kernel(*refs):
        attend_kernel(imports, *refs)

    return pl.pallas_call(
        kernel,
        out_shape=[
            jax.ShapeDtypeStruct((patches, wide * 2 // 3), F32),
            jax.ShapeDtypeStruct((patches, wide), BF16),
            jax.ShapeDtypeStruct((patches, wide // 3), BF16),
            jax.ShapeDtypeStruct((rows, width), F32),
            jax.ShapeDtypeStruct((4, depth, rest), BF16),
            jax.ShapeDtypeStruct((4, depth, ff), BF16),
            jax.ShapeDtypeStruct((4, depth, ff), BF16),
            jax.ShapeDtypeStruct((rows, rest), F32),
        ],
        in_specs=[vmem] * 8 + [anywhere] * 3 + [vmem] * 2,
        out_specs=[vmem] * 4 + [anywhere] * 3 + [vmem],
        scratch_shapes=[
            pltpu.VMEM((4, depth, rest), BF16),
            pltpu.VMEM((depth, ff), BF16),
            pltpu.VMEM((depth, ff), BF16),
            pltpu.SemaphoreType.DMA,
            pltpu.SemaphoreType.DMA((4,)),
        ]
        + RowSums.scratch(rows, width)
        + imports.scratch(),
        compiler_params=pltpu.CompilerParams(
            collective_id=ATTEND_ID, has_side_effects=True, vmem_limit_bytes=63 * 2**20
        ),
        name="attend",
    )(hidden, w_qkv, w_out, *tables, q_gain, k_gain, w_mod, w_gate, w_up, lifted, bias)


def rows_to_columns(values, blocks):
    rows, columns = values.shape
    ways = lax.axis_size("seq")
    values = values.reshape(rows, blocks, ways, columns // (blocks * ways))
    moved = lax.all_to_all(values, "seq", split_axis=2, concat_axis=0, tiled=True)
    return moved.reshape(rows * ways, columns // ways)


def columns_to_rows(values, blocks):
    rows, columns = values.shape
    ways = lax.axis_size("seq")
    values = values.reshape(rows, blocks, 1, columns // blocks)
    moved = lax.all_to_all(values, "seq", split_axis=0, concat_axis=2, tiled=True)
    return moved.reshape(rows // ways, columns * ways)


def first_tile(place, tiles):
    return (tiles * place) // 4


def padded_rows(rows):
    return -(-rows // 16) * 16


class Part:
    def __init__(self, left, right, rows, span, out, order, by_rows=False, in_lanes=False, bias=False):
        self.left, self.right, self.rows = left, right, rows
        self.start, self.columns, self.out = span[0], span[1] - span[0], out
        self.order, self.by_rows, self.in_lanes, self.bias = order, by_rows, in_lanes, bias
        self.slab = padded_rows(rows)


def split_part(left, right, rows, columns, out, order, **kinds):
    middle = -(-columns // (2 * TILE)) * TILE
    return [
        Part(left, right, rows, span, out, order, **kinds)
        for span in ((0, middle), (middle, columns))
    ]


class GradSums:
    def __init__(self, parts, names, shared_shapes, small_shape):
        self.parts, self.names = parts, names
        self.shared_shapes, self.small_shape = shared_shapes, small_shape
        self.has_rows = any(part.by_rows for part in parts)

    def spread(self, group):
        rows, columns, whole = self.shared_shapes[group]
        return rows, columns if whole else -(-columns // (4 * TILE)) * TILE

    def scratch(self, array_shapes):
        parts, count, groups = self.parts, len(self.parts), len(self.shared_shapes)
        shapes = [pltpu.VMEM(shape, BF16) for shape in array_shapes]
        shapes += [pltpu.VMEM((4,) + self.spread(group), BF16) for group in range(groups)]
        for lead in ((2, 2, 2), (2, 2), (2,), ()):
            shapes += [pltpu.VMEM(lead + (part.slab, part.columns), BF16) for part in parts]
        for _ in range(2):
            for part in parts:
                if part.by_rows:
                    shapes.append(pltpu.VMEM((part.slab, part.columns), BF16))
                else:
                    shapes.append(pltpu.VMEM((4, padded_rows(part.rows // 4), part.columns), BF16))
        widest = max(part.columns for part in parts)
        tallest = max(4 * LANES if part.in_lanes else part.rows for part in parts)
        return shapes + [
            pltpu.VMEM((tallest, widest), F32),
            pltpu.VMEM((4,) + self.small_shape, F32),
            pltpu.VMEM((3,) + self.small_shape, F32),
            pltpu.SemaphoreType.DMA((len(self.names),)),
            pltpu.SemaphoreType.DMA((groups, 3)),
            pltpu.SemaphoreType.DMA((groups, 3)),
            pltpu.SemaphoreType.DMA((groups,)),
            pltpu.SemaphoreType.DMA((count, 3)),
            pltpu.SemaphoreType.DMA((count, 3)),
            pltpu.SemaphoreType.DMA((count, 3)),
            pltpu.SemaphoreType.DMA((count, 3)),
            pltpu.SemaphoreType.DMA((6,)),
            pltpu.SemaphoreType.DMA((6,)),
        ]

    def bind(self, ins, shared, small_in, outs, small_out, scratch):
        count, groups, names = len(self.parts), len(self.shared_shapes), self.names
        refs = list(scratch)

        def take(number):
            taken = refs[:number]
            del refs[:number]
            return taken

        self.shared, self.small_in, self.outs, self.small_out = shared, small_in, outs, small_out
        self.held = dict(zip(names, take(len(names)), strict=True))
        self.gathered = take(groups)
        self.own, self.first_in = take(count), take(count)
        self.second_in, self.third_in = take(count), take(count)
        self.slabs, self.slab_in = take(count), take(count)
        self.total, self.small, self.small_came = take(3)
        load_sem, self.share_send, self.share_recv, own_sem, self.send_sem, self.recv_sem = take(6)
        self.last_send, self.last_recv, self.small_send, self.small_recv = take(4)
        item, column = lax.axis_index("dp"), lax.axis_index("seq")
        self.column = column
        self.bits = [lax.rem(item, 2), lax.rem(item // 2, 2), item // 4]
        self.partners = [(item + (1 - 2 * self.bits[k]) * (1 << k), column) for k in range(3)]
        self.peers = [(item, lax.rem(column + k, 4)) for k in range(1, 4)]
        self.owner = (2 * column + item // 4, lax.rem(item, 4))
        self.feeder = (4 * lax.rem(item, 2) + column, item // 2)
        self.elsewhere = jnp.logical_or(self.owner[0] != item, self.owner[1] != column)
        self.loads = {
            name: pltpu.make_async_copy(ins[i], self.held[name], load_sem.at[i])
            for i, name in enumerate(names)
        }
        self.own_shares = [
            pltpu.make_async_copy(
                self.columns_of(g, column), self.gathered[g].at[column], own_sem.at[g]
            )
            for g in range(groups)
        ]
        self.ready = set()
        self.others = {}

    def greet(self):
        barrier = pltpu.get_barrier_semaphore()
        for partner in self.partners + self.peers:
            pl.semaphore_signal(barrier, inc=1, device_id=partner, device_id_type=MESH)
        waits = 6
        if self.has_rows:
            waits = 6 + self.elsewhere.astype(jnp.int32)

            @pl.when(self.elsewhere)
            def _():
                pl.semaphore_signal(barrier, inc=1, device_id=self.feeder, device_id_type=MESH)

        pl.semaphore_wait(barrier, waits)

    def load(self):
        for name in self.names:
            self.loads[name].start()

    def remote(self, source, target_ref, send, recv, target):
        return pltpu.make_async_remote_copy(
            src_ref=source,
            dst_ref=target_ref,
            send_sem=send,
            recv_sem=recv,
            device_id=target,
            device_id_type=MESH,
        )

    def columns_of(self, group, place):
        wide, narrow = self.shared_shapes[group][1], self.spread(group)[1]
        if wide == narrow:
            return self.shared[group]
        start = first_tile(place, wide // TILE) * TILE
        return self.shared[group].at[:, pl.ds(pl.multiple_of(start, TILE), narrow)]

    def shares(self, group):
        return [
            self.remote(
                self.columns_of(group, peer[1]),
                self.gathered[group].at[self.column],
                self.share_send.at[group, k],
                self.share_recv.at[group, k],
                peer,
            )
            for k, peer in enumerate(self.peers)
        ]

    def share(self):
        for group in range(len(self.shared_shapes)):
            self.own_shares[group].start()
            for copy in self.shares(group):
                copy.start()

    def operand(self, name):
        if isinstance(name, int):
            if name not in self.ready:
                self.own_shares[name].wait()
                for copy in self.shares(name):
                    copy.wait()
            self.ready.add(name)
            ref = self.gathered[name]
            return ref[...].reshape(4 * ref.shape[1], ref.shape[2])
        first = name not in self.ready
        self.ready.add(name)
        if name in self.others:
            ref, wait = self.others[name]
            if first:
                wait()
            return ref[...].reshape(4 * ref.shape[1], ref.shape[2])
        if first:
            self.loads[name].wait()
        return self.held[name][...]

    def multiply(self, index):
        part = self.parts[index]
        left, right = self.operand(part.left), self.operand(part.right)
        right = right[:, part.start : part.start + part.columns]
        if part.bias:
            sums = jnp.sum(right.astype(F32), axis=0, keepdims=True)
            for tile in range(part.columns // TILE):
                row = part.start // TILE + tile
                self.small[0, row : row + 1] = sums[:, tile * TILE : (tile + 1) * TILE]
        own, rows = self.own[index], part.rows
        if part.in_lanes:
            self.total[: left.shape[1], : part.columns] = over_first(left, right)
            for d in range(8):
                start = d // 2 * LANES + d % 2 * rows
                own[d // 4, d // 2 % 2, d % 2] = self.cut(start, rows, part.slab, part.columns)
            return
        step = 3 * TILE
        for start in range(0, left.shape[1], step):
            product = over_first(left[:, start : start + step], right).astype(BF16)
            for d in range(8):
                low, high = max(start, d * rows), min(start + step, (d + 1) * rows)
                if low < high:
                    place = slice(low - d * rows, high - d * rows)
                    own[d // 4, d // 2 % 2, d % 2, place] = product[low - start : high - start]

    def cut(self, start, rows, padded, columns):
        values = self.total[start : start + rows, :columns]
        if padded > rows:
            values = jnp.concatenate([values, jnp.zeros((padded - rows, columns), F32)], axis=0)
        return values.astype(BF16)

    def place(self, index, high, low):
        if self.parts[index].order == 0:
            return (high, low, self.bits[0])
        return (high, self.bits[1], low)

    def stage(self, index, step):
        order = self.parts[index].order
        other = 1 - order
        sems = self.send_sem.at[index, step], self.recv_sem.at[index, step]
        own = self.own[index]
        if step == 0:
            pick = 1 - self.bits[order]
            half = (slice(None), slice(None), pick) if order == 0 else (slice(None), pick)
            return self.remote(own.at[half], self.first_in[index], *sems, self.partners[order])
        if step == 1:
            place = self.place(index, slice(None), 1 - self.bits[other])
            return self.remote(own.at[place], self.second_in[index], *sems, self.partners[other])
        place = self.place(index, 1 - self.bits[2], self.bits[other])
        return self.remote(own.at[place], self.third_in[index], *sems, self.partners[2])

    def begin(self, index):
        self.multiply(index)
        self.stage(index, 0).start()

    def end_first(self, index):
        self.stage(index, 0).wait()
        for high in range(2):
            for low in range(2):
                place = self.place(index, high, low)
                came = self.first_in[index][high, low].astype(F32)
                self.own[index][place] = (self.own[index][place].astype(F32) + came).astype(BF16)
        self.stage(index, 1).start()

    def end_second(self, index):
        self.stage(index, 1).wait()
        for high in range(2):
            place = self.place(index, high, self.bits[1 - self.parts[index].order])
            came = self.second_in[index][high].astype(F32)
            self.own[index][place] = (self.own[index][place].astype(F32) + came).astype(BF16)
        self.stage(index, 2).start()

    def last(self, index):
        if self.parts[index].by_rows:
            sems = self.last_send.at[index, 0], self.last_recv.at[index, 0]
            return [self.remote(self.slabs[index], self.slab_in[index], *sems, self.owner)]
        return [
            self.remote(
                self.slabs[index].at[peer[1]],
                self.slab_in[index].at[self.column],
                self.last_send.at[index, k],
                self.last_recv.at[index, k],
                peer,
            )
            for k, peer in enumerate(self.peers)
        ]

    def end_third(self, index):
        part = self.parts[index]
        self.stage(index, 2).wait()
        place = self.place(index, self.bits[2], self.bits[1 - part.order])
        sums = self.own[index][place].astype(F32) + self.third_in[index][...].astype(F32)
        if part.by_rows:
            self.slabs[index][...] = sums.astype(BF16)

            @pl.when(self.elsewhere)
            def _():
                self.last(index)[0].start()

            @pl.when(jnp.logical_not(self.elsewhere))
            def _():
                self.slab_in[index][...] = self.slabs[index][...]

            return
        self.total[: part.rows, : part.columns] = sums
        rows = part.rows // 4
        for k in range(4):
            self.slabs[index][k] = self.cut(k * rows, rows, padded_rows(rows), part.columns)
        for copy in self.last(index):
            copy.start()
        self.slab_in[index][self.column] = self.slabs[index][self.column]

    def end_last(self, index):
        part = self.parts[index]
        out, stop = self.outs[part.out], part.start + part.columns
        if part.by_rows:

            @pl.when(self.elsewhere)
            def _():
                self.last(index)[0].wait()

            out[:, part.start : stop] = self.slab_in[index][...].astype(F32)[: part.rows]
            return
        for copy in self.last(index):
            copy.wait()
        rows = part.rows // 4
        wide = out.shape[-1]
        for k in range(4):
            values = self.slab_in[index][k].astype(F32)[:rows]
            if len(out.shape) == 3:
                out[k, :, part.start : stop] = values
            else:
                start = first_tile(k, wide // TILE) * TILE
                out[:, start + part.start : start + stop] = values

    def small_step(self, step):
        if step < 3:
            sems = self.small_send.at[step], self.small_recv.at[step]
            return [
                self.remote(self.small.at[step], self.small_came.at[step], *sems, self.partners[step])
            ]
        return [
            self.remote(
                self.small.at[3],
                self.small_out.at[self.column],
                self.small_send.at[3 + k],
                self.small_recv.at[3 + k],
                peer,
            )
            for k, peer in enumerate(self.peers)
        ]

    def end_small(self, at):
        self.small_step(at - 1)[0].wait()
        self.small[at] = self.small[at - 1] + self.small_came[at - 1]
        for copy in self.small_step(at):
            copy.start()

    def steps(self, ahead=2):
        count = len(self.parts)
        todo = [lambda: self.small.__setitem__(0, self.small_in[...])]
        todo += [lambda index=index: self.begin(index) for index in range(min(ahead, count))]
        for step in range(count + 3):
            if step < count:
                todo.append(lambda step=step: self.end_first(step))
                if step + ahead < count:
                    todo.append(lambda step=step: self.begin(step + ahead))
            if 0 <= step - 1 < count:
                todo.append(lambda step=step: self.end_second(step - 1))
            if 0 <= step - 2 < count:
                todo.append(lambda step=step: self.end_third(step - 2))
            if 0 <= step - 3 < count:
                todo.append(lambda step=step: self.end_last(step - 3))
            at = step - max(count - ahead, 0)
            if at == 0:
                todo.append(lambda: self.small_step(0)[0].start())
            if 1 <= at <= 3:
                todo.append(lambda at=at: self.end_small(at))
        todo.append(self.end)
        return todo

    def end(self):
        self.small_out[self.column] = self.small[3]
        for copy in self.small_step(3):
            copy.wait()


def split(refs, *counts):
    groups, start = [], 0
    for number in counts:
        groups.append(refs[start : start + number])
        start += number
    return groups + [refs[start:]]


def weight_grads(parts, arrays, shared, small, out_shapes):
    names = tuple(arrays)
    sums = GradSums(parts, names, [value.shape + (whole,) for value, whole in shared], small.shape)
    count = len(out_shapes)

    def kernel(*refs):
        ins, given, (small_in,), outs, (small_out,), scratch = split(
            refs, len(names), len(shared), 1, count, 1
        )
        sums.bind(ins, given, small_in, outs, small_out, scratch)
        sums.load()
        sums.greet()
        sums.share()
        for step in sums.steps(ahead=3):
            step()

    return pl.pallas_call(
        kernel,
        out_shape=[jax.ShapeDtypeStruct(shape, F32) for shape in out_shapes]
        + [jax.ShapeDtypeStruct((4,) + small.shape, F32)],
        in_specs=[pl.BlockSpec(memory_space=pl.ANY)] * (len(names) + len(shared))
        + [pl.BlockSpec(memory_space=pltpu.VMEM)],
        out_specs=[pl.BlockSpec(memory_space=pltpu.VMEM)] * (count + 1),
        scratch_shapes=sums.scratch([value.shape for value in arrays.values()]),
        compiler_params=pltpu.CompilerParams(
            collective_id=SUM_ID, has_side_effects=True, vmem_limit_bytes=63 * 2**20
        ),
        name="weight_grads",
    )(*arrays.values(), *[value for value, _ in shared], small)


BACK_INPUTS = ("rows", "heads", "w_qkv", "w_out", "cosine", "ahead", "behind", "q_gain", "k_gain")


def back_kernel(sums, grad_in, lifted, given, lifted_all, project_out, hidden_out, gains_out, refs):
    branch_in, loads_into, pieces, scratch = split(refs, 1, 4, 1)
    (branch_all,), (rows, heads, w_qkv, w_out), (grad_heads,) = branch_in, loads_into, pieces
    load_sem = scratch[0]
    gather, gather_lifted = RowGather(grad_in, branch_all, *scratch[1:4]), RowGather(lifted, lifted_all, *scratch[4:7])
    row_sums = RowSums(*scratch[7:])
    cosine, ahead, behind, q_gain, k_gain = given[4:]
    local_rows = grad_in.shape[0]
    count = grad_heads.shape[1] // LANES
    factor = HD ** (-0.5)
    loads = [
        pltpu.make_async_copy(source, target, load_sem.at[k])
        for k, (source, target) in enumerate(zip(given[:4], (rows, heads, w_qkv, w_out), strict=True))
    ]
    for k in (3, 0, 1, 2):
        loads[k].start()
    sums.load()
    sums.greet()

    gather.start()
    gather_lifted.start()
    sums.share()

    def lifted_ready():
        gather_lifted.pass_on()
        gather_lifted.end()

    sums.others["lifted"] = (lifted_all, lifted_ready)
    todo = sums.steps(ahead=3)

    def aside(number):
        for _ in range(min(number, len(todo))):
            todo.pop(0)()

    aside(4)
    gather.pass_on()
    gather.end()
    loads[3].wait()
    grad_branch = branch_all[...].reshape(4 * local_rows, branch_all.shape[2])
    grad_heads[...] = over_rows(grad_branch, w_out[...]).astype(BF16)
    loads[0].wait()
    loads[1].wait()
    tables = cosine[...], ahead[...], behind[...]
    block = 256
    gain_sums = [jnp.zeros((1, LANES), F32), jnp.zeros((1, LANES), F32)]
    counts = (1, 3, 3, 3)
    for head in range(count):
        spans = [slice((k * count + head) * LANES, (k * count + head + 1) * LANES) for k in range(3)]
        keys, values = rows[:, spans[1]], rows[:, spans[2]]
        grad_query, grad_key, grad_value = [], None, None
        for start in range(0, rows.shape[0], block):
            queries = rows[start : start + block, spans[0]]
            grads = grad_heads[start : start + block, spans[0]]
            exp_scores = jnp.exp(over_rows(keys, queries) * factor)
            probs = exp_scores * (1.0 / jnp.sum(exp_scores, axis=0, keepdims=True))
            grad_probs = over_rows(values, grads)
            inner = jnp.sum(probs * grad_probs, axis=0, keepdims=True)
            grad_scores = (probs * (grad_probs - inner)).astype(BF16)
            grad_query.append(over_first(grad_scores, keys))
            key_term = jnp.dot(grad_scores, queries, preferred_element_type=F32)
            value_term = jnp.dot(probs.astype(BF16), grads, preferred_element_type=F32)
            grad_key = key_term if grad_key is None else grad_key + key_term
            grad_value = value_term if grad_value is None else grad_value + value_term
        project_out[:, spans[2]] = grad_value.astype(BF16)
        terms = (jnp.concatenate(grad_query, axis=0) * factor, grad_key * factor)
        for k, (term, gain) in enumerate(zip(terms, (q_gain, k_gain), strict=True)):
            raw = heads[:, spans[k]]
            inverse = head_inverse(raw)
            normed = raw * inverse
            back = rotated(term, tables, -1)
            gain_sums[k] = gain_sums[k] + jnp.sum(back * normed, axis=0, keepdims=True)
            back = back * gain[...]
            mean = jnp.sum(back * normed, axis=-1, keepdims=True) * (1.0 / HD)
            project_out[:, spans[k]] = (inverse * (back - normed * mean)).astype(BF16)
        aside(counts[head])
    gains_out[...] = jnp.concatenate(gain_sums + [jnp.zeros((6, LANES), F32)], axis=0)
    loads[2].wait()
    for index in range(4):
        part = pl.ds(pl.multiple_of(row_sums.order[index] * local_rows, local_rows), local_rows)
        row_sums.put(index, over_rows(project_out[part, :], w_qkv[...]))
        if index == 1:
            aside(1)
    aside(3)
    hidden_out[...] = row_sums.sums()
    aside(len(todo))


def attention_back(grad_in, lifted, given, parts, arrays, shared, small, out_shapes):
    names = tuple(arrays)
    sums = GradSums(parts, names, [value.shape + (whole,) for value, whole in shared], small.shape)
    count = len(out_shapes)
    rows, width = grad_in.shape
    kept, heads, w_qkv, w_out = given[:4]
    vmem, anywhere = pl.BlockSpec(memory_space=pltpu.VMEM), pl.BlockSpec(memory_space=pl.ANY)

    def kernel(*refs):
        ins, exchanged, (small_in, grad, low), held, outs, (small_out, low_all), results, refs = split(
            refs, len(names), len(shared), 3, len(given), count, 2, 4
        )
        own, scratch = split(refs, OWN_SCRATCH)
        sums.bind(ins, exchanged, small_in, outs, small_out, scratch)
        branch_all, project, hidden, gains = results
        back_kernel(sums, grad, low, held, low_all, project, hidden, gains, [branch_all] + list(own))

    own_scratch = [
        pltpu.VMEM(kept.shape, BF16),
        pltpu.VMEM(heads.shape, F32),
        pltpu.VMEM(w_qkv.shape, BF16),
        pltpu.VMEM(w_out.shape, BF16),
        pltpu.VMEM((4 * rows, w_out.shape[0]), BF16),
        pltpu.SemaphoreType.DMA((4,)),
        *RowGather.scratch(),
        *RowGather.scratch(),
    ] + RowSums.scratch(rows, width)
    return pl.pallas_call(
        kernel,
        out_shape=[jax.ShapeDtypeStruct(shape, F32) for shape in out_shapes]
        + [
            jax.ShapeDtypeStruct((4,) + small.shape, F32),
            jax.ShapeDtypeStruct((4, rows, width), BF16),
            jax.ShapeDtypeStruct((4, rows, width), BF16),
            jax.ShapeDtypeStruct(kept.shape, BF16),
            jax.ShapeDtypeStruct((rows, width), F32),
            jax.ShapeDtypeStruct((8, LANES), F32),
        ],
        in_specs=[anywhere] * (len(names) + len(shared)) + [vmem] * 3 + [anywhere] * 4 + [vmem] * 5,
        out_specs=[vmem] * (count + 6),
        scratch_shapes=own_scratch + sums.scratch([value.shape for value in arrays.values()]),
        compiler_params=pltpu.CompilerParams(
            collective_id=BACK_ID, has_side_effects=True, vmem_limit_bytes=63 * 2**20
        ),
        name="attention_back",
    )(*arrays.values(), *[value for value, _ in shared], small, grad_in, lifted, *given)


OWN_SCRATCH = 18


def to_owners(rows):
    n_dp, n_seq = lax.axis_size("dp"), lax.axis_size("seq")
    pairs = []
    for d in range(n_dp):
        for s in range(n_seq):
            pairs.append((d * n_seq + s, s * n_dp + d))
    return lax.ppermute(rows, ("dp", "seq"), pairs)


def plain_sums(left, right, blocks):
    mine = lax.psum_scatter(outer_sum(left, right).astype(BF16), "dp", scatter_dimension=0, tiled=True)
    return (columns_to_rows(mine, blocks) if blocks else to_owners(mine)).astype(F32)


def padded_small(values):
    values = jnp.pad(values, ((0, 8 - values.shape[0]), (0, TILE - values.shape[1])))
    return jnp.concatenate([jnp.zeros((8, TILE), F32), values])


def bias_columns(small, tiles):
    edges = [first_tile(k, tiles) for k in range(4)] + [tiles]
    sums = small[:, :8].reshape(4, 8 * TILE)
    return [sums[k, : (edges[k + 1] - edges[k]) * TILE] for k in range(4)]


def in_lanes(values, axis):
    shape = values.shape
    values = values.reshape(shape[:axis] + (shape[axis] // HD, HD) + shape[axis + 1 :])
    pads = [(0, 0)] * len(values.shape)
    pads[axis + 1] = (0, LANES - HD)
    return jnp.pad(values, pads).reshape(shape[:axis] + (-1,) + shape[axis + 1 :])


def out_of_lanes(values):
    return values.reshape(values.shape[0], -1, LANES)[:, :, :HD]


def plain_back(grad_branch_a, given):
    kept, projected, w_qkv, w_out, cosine, ahead, behind, q_gain, k_gain = given
    patches, count = kept.shape[0], w_out.shape[0] // LANES
    factor = HD ** (-0.5)
    tables = [table[:, None, :] for table in (cosine, ahead, behind)]

    def turn(values):
        turned = jnp.roll(values, -QUARTER, -1) * tables[1] + jnp.roll(values, QUARTER, -1) * tables[2]
        return values * tables[0] - turned

    query, key, value = jnp.split(kept.reshape(patches, 3 * count, LANES), 3, axis=1)
    grads = times_transpose(grad_branch_a, w_out).astype(BF16).reshape(patches, count, LANES)
    scores = jnp.einsum("qhd,khd->hqk", query, key, preferred_element_type=F32) * factor
    exp_scores = jnp.exp(scores)
    probs = exp_scores / jnp.sum(exp_scores, axis=-1, keepdims=True)
    grad_probs = jnp.einsum("qhd,khd->hqk", grads, value, preferred_element_type=F32)
    inner = jnp.sum(probs * grad_probs, axis=-1, keepdims=True)
    grad_scores = (probs * (grad_probs - inner)).astype(BF16)
    terms = (
        jnp.einsum("hqk,khd->qhd", grad_scores, key, preferred_element_type=F32) * factor,
        jnp.einsum("hqk,qhd->khd", grad_scores, query, preferred_element_type=F32) * factor,
    )
    grad_value = jnp.einsum("hqk,qhd->khd", probs.astype(BF16), grads, preferred_element_type=F32)
    raws = jnp.split(projected.reshape(patches, 2 * count, LANES), 2, axis=1)
    results, gains = [], []
    for term, raw, gain in zip(terms, raws, (q_gain, k_gain), strict=True):
        inverse = head_inverse(raw)
        normed = raw * inverse
        back = turn(term)
        gains.append(jnp.sum(back * normed, axis=(0, 1)))
        back = back * gain[0]
        mean = jnp.sum(back * normed, axis=-1, keepdims=True) * (1.0 / HD)
        results.append(inverse * (back - normed * mean))
    grad_lanes = jnp.concatenate(results + [grad_value], axis=1).reshape(kept.shape).astype(BF16)
    return grad_lanes, times_transpose(grad_lanes, w_qkv), jnp.stack(gains)


def shards(
    tokens,
    condition,
    cotangent,
    w_qkv,
    w_out,
    w_gate,
    w_up,
    w_down,
    w_mod,
    b_mod,
    q_gain,
    k_gain,
    noise_counts,
    time_steps,
    positions,
):
    local_rows, width = tokens.shape[1:]
    ways = lax.axis_size("seq")
    patches = local_rows * ways
    local_heads = HEADS // ways
    item = lax.axis_index("dp")
    running = jnp.cumsum(noise_counts)
    image_id = jnp.sum((running <= item).astype(jnp.int32))
    chosen = jnp.arange(noise_counts.shape[0], dtype=jnp.int32) == image_id
    share = 1.0 / jnp.sum(jnp.where(chosen, noise_counts, 0)).astype(F32)

    embed = time_embed(time_steps, width)
    condition_in = condition[0].astype(F32) + embed
    bias_row = b_mod[None]
    mod_first, w_qkv_lanes, modulation_first, hidden_a, lifted_low, all_positions = first_stage(
        w_mod, w_qkv, condition[0], tokens[0], embed, bias_row, positions[:, 0]
    )
    shift_a, scale_a = jnp.split(modulation_first, 2, axis=-1)
    hidden_a = hidden_a.reshape(patches, width)
    w_qkv_lanes = w_qkv_lanes.reshape(width, w_qkv_lanes.shape[2])
    tables = lane_tables(jnp.transpose(all_positions, (1, 0, 2)).reshape(2, patches))
    w_out_lanes = in_lanes(w_out, 0)
    gain_lanes = [jnp.pad(gain, (0, LANES - HD))[None] for gain in (q_gain, k_gain)]
    (
        projected_lanes,
        rows_lanes,
        attended_lanes,
        branch_a,
        mod_rest,
        gate_cols,
        up_cols,
        modulation_rest,
    ) = attend(
        hidden_a, w_qkv_lanes, w_out_lanes, tables, *gain_lanes, w_mod, w_gate, w_up, lifted_low, bias_row
    )
    gate_a, shift_b, scale_b, gate_b = jnp.split(modulation_rest, 4, axis=-1)
    mod_first, mod_rest = mod_first.reshape(width, -1), mod_rest.reshape(width, -1)
    gate_cols, up_cols = gate_cols.reshape(width, -1), up_cols.reshape(width, -1)
    tokens_f = tokens[0].astype(F32)
    inverse_a = inverse_rms(tokens_f)
    normed_a = tokens_f * inverse_a
    grad_out = cotangent[0].astype(F32) * share
    grad_branch_b = gather_rows((grad_out * gate_b).astype(BF16))

    middle = tokens_f + gate_a * branch_a
    inverse_b = inverse_rms(middle)
    normed_b = middle * inverse_b
    hidden_b = gather_rows((normed_b * (1.0 + scale_b) + shift_b).astype(BF16))
    gate_in = matmul(hidden_b, gate_cols)
    up_in = matmul(hidden_b, up_cols)
    activated = jax.nn.silu(gate_in)
    inner = (activated * up_in).astype(BF16)
    branch_b = scatter_rows(matmul(inner, w_down))
    block_out = (middle + gate_b * branch_b).astype(BF16)

    grad_gate_b = grad_out * branch_b
    grad_inner = times_transpose(grad_branch_b, w_down)
    grad_gate_in = (grad_inner * up_in * silu_slope(gate_in)).astype(BF16)
    grad_up_in = (grad_inner * activated).astype(BF16)
    grad_hidden_b = scatter_rows(
        times_transpose(grad_gate_in, gate_cols) + times_transpose(grad_up_in, up_cols)
    )
    grad_middle = grad_out + rms_back(grad_hidden_b * (1.0 + scale_b), normed_b, inverse_b)
    grad_gate_a = grad_middle * branch_a
    own_branch_a = (grad_middle * gate_a).astype(BF16)
    grad_mod_b = jnp.concatenate(
        [grad_hidden_b, grad_hidden_b * normed_b, grad_gate_b], axis=-1
    ).astype(BF16)
    wide = grad_mod_b.shape[1]
    ff, heads_wide, own_rows = gate_cols.shape[1], local_heads * HD, width // 8
    mod_cols = -(-wide // (4 * TILE)) * TILE
    pieces = lax.axis_size("dp") == 8
    parts_b, arrays_b, shared_b, shapes_b = [], {}, [], []
    if pieces:
        parts_b = [
            *split_part("inner", "grad_branch_b", ff // 8, width, 0, 0, by_rows=True),
            *split_part("hidden_b", "grad_gate_in", own_rows, ff, 1, 1),
            *split_part("hidden_b", "grad_up_in", own_rows, ff, 2, 0),
            *split_part("lifted", 0, own_rows, mod_cols, 3, 0, bias=True),
        ]
        parts_b = [parts_b[k] for k in (0, 2, 1, 3, 4, 5, 6, 7)]
        arrays_b = {
            "inner": inner,
            "grad_branch_b": grad_branch_b,
            "hidden_b": hidden_b,
            "grad_gate_in": grad_gate_in,
            "grad_up_in": grad_up_in,
        }
        shared_b = [(grad_mod_b, False)]
        shapes_b = [
            (ff // 8, width),
            (own_rows // 4, 4 * ff),
            (own_rows // 4, 4 * ff),
            (own_rows // 4, wide),
        ]
    given = [rows_lanes, projected_lanes, w_qkv_lanes, w_out_lanes, *tables, *gain_lanes]
    empty = jnp.zeros((16, TILE), F32)
    if pieces:
        (*sums_b, small_b, lifted_full, grad_branch_a, grad_lanes, grad_hidden_a, gain_sums) = (
            attention_back(own_branch_a, lifted_low, given, parts_b, arrays_b, shared_b, empty, shapes_b)
        )
        grad_branch_a = grad_branch_a.reshape(patches, width)
        lifted_full = lifted_full.reshape(patches, width)
    else:
        grad_branch_a = gather_rows(own_branch_a)
        grad_lanes, partial, gain_sums = plain_back(grad_branch_a, given)
        grad_hidden_a = scatter_rows(partial)
    grad_tokens = grad_middle + rms_back(grad_hidden_a * (1.0 + scale_a), normed_a, inverse_a)
    grad_mod_a = jnp.concatenate(
        [grad_hidden_a, grad_hidden_a * normed_a, grad_gate_a], axis=-1
    ).astype(BF16)
    first = mod_first.shape[1]
    grad_condition = (
        times_transpose(grad_mod_a[:, :first], mod_first)
        + times_transpose(
            jnp.concatenate([grad_mod_a[:, first:], grad_mod_b], axis=1), mod_rest
        )
    ) * silu_slope(condition_in)
    grad_project = out_of_lanes(grad_lanes).reshape(patches, 3 * heads_wide)
    gain_sums = gain_sums[:2, :HD]
    if pieces:
        parts_a = [
            *split_part("hidden_a", "grad_project", own_rows, 3 * heads_wide, 0, 0),
            Part(
                "attended", "grad_branch_a", heads_wide // 8, (0, width), 1, 1, by_rows=True, in_lanes=True
            ),
            *split_part("lifted", 0, own_rows, mod_cols, 2, 0, bias=True),
        ]
        parts_a = [parts_a[k] for k in (0, 2, 1, 3, 4)]
        arrays_a = {
            "hidden_a": hidden_a,
            "grad_project": grad_project,
            "attended": attended_lanes,
            "grad_branch_a": grad_branch_a,
            "lifted": lifted_full,
        }
        shapes_a = [
            (4, own_rows // 4, 3 * heads_wide),
            (heads_wide // 8, width),
            (own_rows // 4, wide),
        ]
        qkv_sum, grad_w_out, mod_a, small_a = weight_grads(
            parts_a, arrays_a, [(grad_mod_a, False)], padded_small(gain_sums), shapes_a
        )
        grad_w_down, grad_w_gate, grad_w_up, mod_b = sums_b
        grad_w_qkv = jnp.transpose(
            qkv_sum.reshape(4, own_rows // 4, 3, heads_wide), (1, 2, 0, 3)
        ).reshape(own_rows // 4, 3 * width)
        grad_w_mod = jnp.concatenate([mod_a, mod_b], axis=1)
        tiles = wide // TILE
        bias = jnp.concatenate(bias_columns(small_a, tiles) + bias_columns(small_b, tiles))
        own_bias = bias.shape[0] // (8 * ways)
        sum_bias = lax.dynamic_slice(
            bias, ((item * ways + lax.axis_index("seq")) * own_bias,), (own_bias,)
        )
        gains = jnp.sum(small_a[:, 8:10, :HD], axis=0)
    else:
        mod_rows = jnp.concatenate([grad_mod_a, grad_mod_b], axis=1)
        grad_w_down = plain_sums(inner, grad_branch_b, 0)
        grad_w_gate = plain_sums(hidden_b, grad_gate_in, 1)
        grad_w_up = plain_sums(hidden_b, grad_up_in, 1)
        grad_w_qkv = plain_sums(hidden_a, grad_project, 3)
        attended = out_of_lanes(attended_lanes).reshape(patches, heads_wide)
        grad_w_out = plain_sums(attended, grad_branch_a, 0)
        grad_w_mod = plain_sums(gather_rows(lifted_low), rows_to_columns(mod_rows, 6), 6)
        bias_rows = jnp.sum(mod_rows, axis=0, dtype=F32)
        sum_bias = lax.psum_scatter(bias_rows, ("dp", "seq"), scatter_dimension=0, tiled=True)
        gains = lax.psum(gain_sums, ("dp", "seq"))
    sum_q_gain, sum_k_gain = gains[0], gains[1]
    return (
        block_out[None],
        grad_tokens[None],
        grad_condition[None],
        grad_w_qkv,
        grad_w_out,
        grad_w_gate,
        grad_w_up,
        grad_w_down,
        grad_w_mod,
        sum_bias,
        sum_q_gain,
        sum_k_gain,
    )


def solution(mesh):
    placed = (
        P("dp", "seq", None),
        P("dp", "seq", None),
        P("dp", "seq", None),
        P("seq", None),
        P("seq", None),
        P("seq", None),
        P("seq", None),
        P("seq", None),
        P("seq", None),
        P(),
        P(),
        P(),
        P(),
        P("dp"),
        P(None, "dp", "seq"),
    )
    return jax.shard_map(
        shards,
        mesh=mesh,
        in_specs=placed,
        out_specs=(
            P("dp", "seq", None),
            P("dp", "seq", None),
            P("dp", "seq", None),
            P(("dp", "seq"), None),
            P(("dp", "seq"), None),
            P(("dp", "seq"), None),
            P(("dp", "seq"), None),
            P(("dp", "seq"), None),
            P(("dp", "seq"), None),
            P(("dp", "seq")),
            P(),
            P(),
        ),
        check_vma=False,
    )
```

time: 973 us -> 485 us (0.50)
  waiting for transfers between devices: 478 us -> 0 us
  Pallas kernels: 0 us -> 392 us
  blocking collectives: 156 us -> 0 us
  matrix products: 137 us -> 33.3 us
  local copies, waits for them, and re-layouts: 90.3 us -> 26.4 us
  starting transfers between devices: 39.6 us -> 0 us
  other arithmetic: 49.1 us -> 25.1 us
  between operations: 17.2 us -> 2.95 us
    pallas_call x0 -> x8, Pallas kernels: none -> 392 us  [the longest x1 122 us: attention_back(): pl.pallas_call(kernel, out_shape=[jax.ShapeDtypeStruct(shape, F32) for sh...]
    reduce_scatter x9 -> x0, waiting for transfers between devices: 290 us -> none  [the longest x4 124 us: sum_columns(): lax.psum_scatter(partial.astype(BF16), 'dp', scatter_dimension=0, tiled=T...]
    all_gather x6 -> x0, waiting for transfers between devices: 128 us -> none  [gather_rows(): return lax.all_gather(values, 'seq', axis=0, tiled=True)]
    unnamed x2 -> x0, blocking collectives: 73 us -> none
    dot_general x12 -> x0, matrix products: 66.1 us -> none  [the longest x6 35.1 us: outer_sum(): return jnp.einsum('ra,rb->ab', left, right, preferred_element_type=F32)]
    all_to_all x7 -> x0, waiting for transfers between devices: 57.2 us -> none  [the longest x3 44.2 us: rows_to_columns(): lax.all_to_all(values, 'seq', split_axis=2, concat_axis=0, tiled=True)]
    all_to_all x1 -> x0, blocking collectives: 43.8 us -> none  [rows_to_columns(): lax.all_to_all(values, 'seq', split_axis=2, concat_axis=0, tiled=True)]
    all_gather x1 -> x0, blocking collectives: 38.9 us -> none  [shards(): all_positions = lax.all_gather(positions[:, 0], 'seq', axis=1, tiled=True)]
  transfers between devices with their start and end apart: 26 -> 0, of which waited for: 16 -> 0; matrix products, arithmetic and copies ran while one was open for 19% -> 0% of each run, Pallas kernels for 0% -> 0%
where the time goes in v3:
time: 485 us; the launch traced here: 480 us
  Pallas kernels  392 us (81%)
  matrix products  33.3 us (7%)
  local copies, waits for them, and re-layouts  26.4 us (5%)
  other arithmetic  25.1 us (5%)
    pallas_call x1, Pallas kernels, attention_back(): pl.pallas_call(kernel, out_shape=[jax.ShapeDtypeStruct(shape, F32) for sh...  122 us
    pallas_call x1, Pallas kernels, weight_grads(): pl.pallas_call(kernel, out_shape=[jax.ShapeDtypeStruct(shape, F32) for sh...  79.3 us
    pallas_call x1, Pallas kernels, attend(): pl.pallas_call(kernel, out_shape=[jax.ShapeDtypeStruct((patches, wide * 2...  68.4 us
    pallas_call x1, Pallas kernels, first_stage(): pl.pallas_call(kernel, out_shape=[jax.ShapeDtypeStruct((4, depth, MOD_BLO...  54.2 us
    pallas_call x2, Pallas kernels, scatter_rows(): pl.pallas_call(scatter_kernel, out_shape=jax.ShapeDtypeStruct((rows, colu...  34.2 us
    pallas_call x2, Pallas kernels, gather_rows(): pl.pallas_call(gather_kernel, out_shape=jax.ShapeDtypeStruct((4, rows, co...  34 us
    dot_general x5, matrix products, times_transpose(): return jnp.einsum('rb,ab->ra', left, right, preferred_element_type=F32)  23.4 us
    dot_general x3, matrix products, matmul(): return jnp.dot(left, right, preferred_element_type=F32)  9.92 us

profile of v3, /device:TPU:0, one launch (start us, length us, event | category | flops | bytes accessed | tf_op | source)
XLA Modules:
  0.0 479.9 jit_solution(2333374270923515649)
XLA Ops:
  1.4 0.7 fusion.38
  2.1 1.4 broadcast_in_dim.59.refs_5_.refs_12_
  3.4 1.3 copy.43
  4.7 54.2 %first_stage.1 = (bf16[4,288,2304]{2,1,0:T(8,128)(2,1)}, bf16[4,288,1536]{2,1,0:T(8,128)(2,1)}, f32[256,2304]{1,0:T(8,128)}, bf16[4,256,1152]{2,1,0:T(8,128)(2,1...) custom-call(bf16[288,6912]{1,0:T(8,128)(2,1)} %refs_8_.1, bf16[288,3456]{1,0:T(8,128)(2,1)} %refs_1_.1, ...), custom_call_target="tpu_custom_call" | custom-call | tf_op jit(solution)/shard_map/first_stage/pallas_call | solution.py:517
  58.9 0.8 slice_convert_fusion.1
  60.1 2.9 broadcast_select_fusion
  63.0 0.8 pad.27.refs_3_.refs_13_
  63.8 0.9 pad.28.refs_4_.refs_14_
  64.7 0.8 pad.29.refs_5_.refs_15_
  66.1 1.1 pad.26
  67.2 68.4 %attend.1 = (f32[1024,1024]{1,0:T(8,128)}, bf16[1024,1536]{1,0:T(8,128)(2,1)}, bf16[1024,512]{1,0:T(8,128)(2,1)}, f32[256,1152]{1,0:T(8,128)}, bf16[4,288,4608]{...) custom-call(bf16[1024,1152]{1,0:T(8,128)(2,1)} %bitcast.97, ...), custom_call_target="tpu_custom_call" | custom-call | tf_op jit(solution)/shard_map/attend/pallas_call | solution.py:743
  135.6 2.0 multiply_reduce_fusion.1
  138.5 1.3 fusion.34
  140.5 2.3 fusion.24
  142.8 17.0 %gather_rows.2 = bf16[4,256,1152]{2,1,0:T(8,128)(2,1)S(1)} custom-call(bf16[256,1152]{1,0:T(8,128)(2,1)S(1)} %get-tuple-element.85.own_ref), custom_call_target="tpu_custom_call" | custom-call | tf_op jit(solution)/shard_map/gather_rows/pallas_call | solution.py:131
  159.9 3.9 fusion.40
  163.8 3.8 fusion.39
  167.6 16.9 %gather_rows.3 = bf16[4,256,1152]{2,1,0:T(8,128)(2,1)S(1)} custom-call(bf16[256,1152]{1,0:T(8,128)(2,1)S(1)} %get-tuple-element.84.own_ref), custom_call_target="tpu_custom_call" | custom-call | tf_op jit(solution)/shard_map/gather_rows/pallas_call | solution.py:131
  184.6 6.0 %multiply_convert_fusion = (bf16[1024,768]{1,0:T(8,128)(2,1)S(1)}, bf16[1024,768]{1,0:T(8,128)(2,1)S(1)}, bf16[1024,768]{1,0:T(8,128)(2,1)S(1)}) fusion(f32[1024,768]{1,0:T(8,128)} %fusion.39, f32[1024,768]{1,0:T(8,128)} %fusion.40, bf16[1024,1152]{1,0:T(8,128)(2,1)S(1)} %bitcast.86, bf16[768,1152]{1,0:T(8,128)(2,1)S(1)} %copy-done.35), kind=kOutput, calls=%fused_computation.2 | convolution fusion | flops 1823735808 | bytes 15138816 | tf_op jit(solution)/shard_map/rb,ab->ra/dot_general | solution.py:68
  190.7 2.2 fusion.41
  193.4 2.3 add_convert_fusion
  195.8 17.3 %scatter_rows.3 = f32[256,1152]{1,0:T(8,128)S(1)} custom-call(bf16[2,2,256,1152]{3,2,1,0:T(8,128)(2,1)S(1)} %bitcast.88), custom_call_target="tpu_custom_call" | custom-call | tf_op jit(solution)/shard_map/scatter_rows/pallas_call | solution.py:191
  213.5 1.1 copy-done.36
  214.6 2.2 convolution_convert_fusion
  216.9 16.9 %scatter_rows.2 = f32[256,1152]{1,0:T(8,128)S(1)} custom-call(bf16[2,2,256,1152]{3,2,1,0:T(8,128)(2,1)S(1)} %bitcast.89), custom_call_target="tpu_custom_call" | custom-call | tf_op jit(solution)/shard_map/scatter_rows/pallas_call | solution.py:191
  233.8 1.8 multiply_convert_fusion.3
  235.6 1.0 multiply_convert_fusion.4.refs_7_
  236.7 1.4 pad_maximum_fusion.refs_5_
  238.6 122.1 %attention_back.1 = (f32[96,1152]{1,0:T(8,128)}, f32[36,3072]{1,0:T(8,128)}, f32[36,3072]{1,0:T(8,128)}, f32[36,3456]{1,0:T(8,128)}, f32[4,16,128]{2,1,0:T(8,128...) custom-call(bf16[1024,768]{1,0:T(8,128)(2,1)} %copy-done.23, ...), custom_call_target="tpu_custom_call" | custom-call | tf_op jit(solution)/shard_map/attention_back/pallas_call | solution.py:1308
  360.8 2.1 fusion.13
  363.1 2.8 fusion.18
  365.9 1.4 pad_maximum_fusion.1.refs_5_
  367.5 3.2 copy.31
  370.7 1.4 slice.78
  372.2 3.8 copy.32.refs_1_
  376.0 0.7 slice.62
  377.2 79.3 %weight_grads.1 = (f32[4,36,864]{2,1,0:T(8,128)}, f32[36,1152]{1,0:T(8,128)}, f32[36,3456]{1,0:T(8,128)}, f32[4,16,128]{2,1,0:T(8,128)}) custom-call(bf16[1024,1152]{1,0:T(8,128)(2,1)} %bitcast.98, bf16[1024,864]{1,0:T(8,128)(2,1)} %copy.32.refs_1_, bf16[1024,512]{1,0:T(8,128)(2,1)} %get-tuple-element.55.refs_2_, bf16[1024,1152]{1,0:T(8,128)(2,1)} %bitcast.103, ...), custom_call_target="tpu_custom_call" | custom-call | tf_op jit(solution)/shard_map/weight_grads/pallas_call | solution.py:1176
  456.5 0.8 slice_bitcast_fusion.1
  457.6 0.6 dynamic_slice.3
  458.2 2.1 pad_maximum_fusion.2
  461.3 1.2 reshape.229
  462.4 0.7 slice_reduce_fusion
  463.7 4.4 fusion.20
  468.2 8.4 %fusion.2 = f32[1,256,1152]{2,1,0:T(8,128)} fusion(f32[256,1152]{1,0:T(8,128)S(1)} %fusion.20, bf16[1152,4608]{1,0:T(8,128)(2,1)} %bitcast.114, bf16[256,1152]{1,0:T(8,128)(2,1)S(1)} %copy-done.12, bf16[256,1152]{1,0:T(8,128)(2,1)S(1)} %copy-done.10, bf16[256,1152]{1,0:T(8,128)(2,1)S(1)} %copy-done.14, bf16[256,1152]{1,0:T(8,128)(2,1)S(1)} %copy-done.8, ...), kind=kOutput, calls=%fused_computation.9 | convolution fusion | flops 2730590208 | bytes 15929856 | tf_op jit(solution)/shard_map/rb,ab->ra/dot_general | solution.py:68
  476.7 0.7 copy.57
  477.3 0.8 copy.58
  478.1 0.8 copy.59
  478.9 0.8 copy.60
  (122 shorter events, 5.9 us)
Async XLA Ops:
  63.0 2.6 copy-start.33
  63.0 2.6 copy-start.34
  63.0 3.1 copy-start.24
  67.2 68.4 %copy-start.4 = (bf16[1,256,1152]{2,1,0:T(8,128)(2,1)S(1)}, bf16[1,256,1152]{2,1,0:T(8,128)(2,1)}, u32[]{:S(2)}) copy-start(bf16[1,256,1152]{2,1,0:T(8,128)(2,1)} %param.15) | copy-start | bytes 1769476
  135.6 2.1 copy-start.41
  135.6 4.9 %copy-start.19 = (bf16[1,256,1152]{2,1,0:T(8,128)(2,1)S(1)}, bf16[1,256,1152]{2,1,0:T(8,128)(2,1)}, u32[]{:S(2)}) copy-start(bf16[1,256,1152]{2,1,0:T(8,128)(2,1)} %param.17) | copy-start | bytes 1769476
  142.8 17.1 %copy-start.37 = (bf16[4,288,768]{2,1,0:T(8,128)(2,1)S(1)}, bf16[4,288,768]{2,1,0:T(8,128)(2,1)}, u32[]{:S(2)}) copy-start(bf16[4,288,768]{2,1,0:T(8,128)(2,1)} %get-tuple-element.47) | copy-start | bytes 5308420
  159.9 3.9 copy-start
  159.9 3.9 copy-start.39
  167.6 17.0 %copy-start.35 = (bf16[768,1152]{1,0:T(8,128)(2,1)S(1)}, bf16[768,1152]{1,0:T(8,128)(2,1)}, u32[]{:S(2)}) copy-start(bf16[768,1152]{1,0:T(8,128)(2,1)} %param.22) | copy-start | bytes 5308420
  184.6 6.0 %copy-start.1 = (bf16[4,256,1152]{2,1,0:T(8,128)(2,1)}, bf16[4,256,1152]{2,1,0:T(8,128)(2,1)S(1)}, u32[]{:S(2)}) copy-start(bf16[4,256,1152]{2,1,0:T(8,128)(2,1)S(1)} %gather_rows.3) | copy-start | bytes 7077892
  184.6 6.1 %copy-start.40 = (bf16[4,288,768]{2,1,0:T(8,128)(2,1)S(1)}, bf16[4,288,768]{2,1,0:T(8,128)(2,1)}, u32[]{:S(2)}) copy-start(bf16[4,288,768]{2,1,0:T(8,128)(2,1)} %get-tuple-element.46) | copy-start | bytes 5308420
  190.6 2.3 copy-start.22
  190.6 2.3 copy-start.21
  190.6 22.9 %copy-start.23 = (bf16[1024,768]{1,0:T(8,128)(2,1)}, bf16[1024,768]{1,0:T(8,128)(2,1)S(1)}, u32[]{:S(2)}) copy-start(bf16[1024,768]{1,0:T(8,128)(2,1)S(1)} %get-tuple-element.82.refs_0_) | copy-start | bytes 4718596
  190.6 2.8 copy-start.38
  190.6 22.5 %slice-start = ((s8[4718592]{0:T(1024)(128)(4,1)}), s8[4194304]{0:T(1024)(128)(4,1)S(1)}, s32[]{:S(2)}) async-start(s8[4718592]{0:T(1024)(128)(4,1)} %bitcast.90), calls=%async_computation | async-start | bytes 8388608
  193.4 19.7 %slice-start.1 = ((s8[4718592]{0:T(1024)(128)(4,1)}), s8[524288]{0:T(1024)(128)(4,1)S(1)}, s32[]{:S(2)}) async-start(s8[4718592]{0:T(1024)(128)(4,1)} %bitcast.90), calls=%async_computation.1 | async-start | bytes 1048576
  213.2 1.5 copy-start.36
  216.9 16.9 %copy-start.5 = (f32[256,1152]{1,0:T(8,128)S(1)}, f32[256,1152]{1,0:T(8,128)}, u32[]{:S(2)}) copy-start(f32[256,1152]{1,0:T(8,128)} %get-tuple-element.45) | copy-start | bytes 3538948
  216.9 16.9 %copy-start.20 = (bf16[1,256,1152]{2,1,0:T(8,128)(2,1)S(1)}, bf16[1,256,1152]{2,1,0:T(8,128)(2,1)}, u32[]{:S(2)}) copy-start(bf16[1,256,1152]{2,1,0:T(8,128)(2,1)} %param.17) | copy-start | bytes 1769476
  235.6 2.4 copy-start.2
  235.6 2.4 copy-start.9
  235.6 2.4 copy-start.11
  235.6 2.4 copy-start.13
  360.8 2.2 copy-start.3
  360.8 2.3 copy-start.6
  363.1 2.8 copy-start.7
  365.9 1.4 copy-start.15
  365.9 1.6 copy-start.17
  377.2 80.2 %copy-start.32 = (f32[4,16,128]{2,1,0:T(8,128)S(1)}, f32[4,16,128]{2,1,0:T(8,128)}, u32[]{:S(2)}) copy-start(f32[4,16,128]{2,1,0:T(8,128)} %get-tuple-element.67) | copy-start | bytes 98308
  377.2 81.0 %copy-start.27 = (f32[36,3456]{1,0:T(8,128)S(1)}, f32[36,3456]{1,0:T(8,128)}, u32[]{:S(2)}) copy-start(f32[36,3456]{1,0:T(8,128)} %get-tuple-element.65) | copy-start | bytes 1492996
  456.5 3.8 copy-start.26
  461.1 2.6 copy-start.16
  461.1 2.6 copy-start.18
  463.7 4.5 copy-start.8
  463.7 4.5 copy-start.10
  463.7 4.5 copy-start.12
  463.7 4.5 copy-start.14
  463.7 4.5 copy-start.25
  468.2 8.5 %copy-start.31 = (f32[36,1152]{1,0:T(8,128)S(1)}, f32[36,1152]{1,0:T(8,128)}, u32[]{:S(2)}) copy-start(f32[36,1152]{1,0:T(8,128)} %get-tuple-element.122) | copy-start | bytes 497668
  468.2 9.1 %copy-start.29 = (f32[36,3072]{1,0:T(8,128)S(1)}, f32[36,3072]{1,0:T(8,128)}, u32[]{:S(2)}) copy-start(f32[36,3072]{1,0:T(8,128)} %get-tuple-element.123) | copy-start | bytes 1327108
  476.7 1.5 copy-start.28
  476.7 2.2 copy-start.30

commit v4 on v3

--- a/solution.py
+++ b/solution.py
@@ -69,7 +69,7 @@
 
 
 MESH = pl.DeviceIdType.MESH
-SUM_ID, GATHER_ID, SCATTER_ID, WEIGHT_ID, ATTEND_ID, BACK_ID = 1, 2, 3, 4, 5, 6
+SUM_ID, GATHER_ID, SCATTER_ID, WEIGHT_ID, ATTEND_ID, BACK_ID, MLP_ID = 1, 2, 3, 4, 5, 6, 7
 
 
 def greet(partners):
@@ -214,14 +214,14 @@
 
 
 class WeightImport:
-    def __init__(self, blocks, base):
-        self.blocks, self.base = blocks, base
+    def __init__(self, blocks, ranges):
+        self.blocks, self.ranges = blocks, ranges
         self.arrays = sorted({block[0] for block in blocks})
 
     def scratch(self):
         count = len(self.blocks)
         return [
-            pltpu.SemaphoreType.DMA((4,)),
+            pltpu.SemaphoreType.DMA((8,)),
             pltpu.SemaphoreType.DMA((count, 7)),
             pltpu.SemaphoreType.DMA((count, 7)),
         ]
@@ -253,19 +253,29 @@
             device_id_type=MESH,
         )
 
-    def piece(self, ref, block, y_pick, z_pick, first_row=0, rows=None, base=0):
-        _, _, start, columns = self.blocks[block]
+    def source_column(self, column):
+        for start, stop in self.ranges:
+            if column < stop - start:
+                return start + column
+            column -= stop - start
+
+    def piece(self, ref, block, y_pick, z_pick, first_row=0, rows=None, base=0, outside=False):
+        array, _, start, columns = self.blocks[block]
+        step = columns
+        if array == 0 and outside:
+            step = self.source_column(start + columns) - self.source_column(start)
+            start = self.source_column(start)
         rows = self.half_rows if rows is None else rows
         return ref.at[
             pl.ds(pl.multiple_of(z_pick * self.half_rows + first_row, 16), rows),
-            pl.ds(pl.multiple_of(base + start + y_pick * columns, TILE), columns),
+            pl.ds(pl.multiple_of(base + start + y_pick * step, TILE), columns),
         ]
 
     def mine_for(self, array, place):
         ref = self.ins[array]
         if len(ref.shape) == 3:
             return ref.at[place], 0
-        return ref, self.base if array == 0 else place * self.outs[array].shape[2]
+        return ref, 0 if array == 0 else place * self.outs[array].shape[2]
 
     def whole(self, array, place):
         ref, base = self.mine_for(array, place)
@@ -278,7 +288,7 @@
         array, offset, _, _ = self.blocks[block]
         goal = self.far[offset or 0]
         ref, base = self.mine_for(array, goal)
-        source = self.piece(ref, block, self.y_bit, self.z_bit, base=base)
+        source = self.piece(ref, block, self.y_bit, self.z_bit, base=base, outside=True)
         target = self.piece(self.outs[array].at[self.column], block, self.y_bit, self.z_bit)
         return self.copy(source, target, block, 0, (self.item, goal))
 
@@ -303,14 +313,29 @@
         part = self.outs[0].at[self.far[0], :, pl.ds(start, 2 * columns)]
         return self.copy(part, part, block, 5, self.sibling)
 
+    def spans(self, array, place):
+        target = self.outs[array].at[self.column]
+        if array:
+            return [(self.whole(array, place), target)]
+        pairs, at = [], 0
+        for start, stop in self.ranges:
+            columns = stop - start
+            pairs.append((self.ins[0].at[:, pl.ds(start, columns)], target.at[:, pl.ds(at, columns)]))
+            at += columns
+        return pairs
+
     def beside(self, array):
-        source = self.whole(array, self.sibling[1])
         index = self.arrays.index(array)
-        return self.copy(source, self.outs[array].at[self.column], index, 6, self.sibling)
+        return [
+            self.copy(source, target, index + 2 * k, 6, self.sibling)
+            for k, (source, target) in enumerate(self.spans(array, self.sibling[1]))
+        ]
 
     def own(self, array):
-        source = self.whole(array, self.column)
-        return pltpu.make_async_copy(source, self.outs[array].at[self.column], self.own_sem.at[array])
+        return [
+            pltpu.make_async_copy(source, target, self.own_sem.at[array + 4 * k])
+            for k, (source, target) in enumerate(self.spans(array, self.column))
+        ]
 
     def steps(self):
         count = len(self.blocks)
@@ -410,18 +435,15 @@
         ]
 
 
-MOD_BLOCK = 2304
-
-
-def first_import():
+def first_import(width):
     wide = 3 * HEADS // 4 * LANES
-    return WeightImport([(0, None, 0, MOD_BLOCK // 2), (1, 0, 0, wide // 2), (1, 1, 0, wide // 2)], 0)
-
-
-def second_import(ff):
-    blocks = [(0, None, 0, MOD_BLOCK // 2)]
-    blocks += [(k, j, 0, ff // 2) for k in (2, 3) for j in (0, 1)]
-    return WeightImport(blocks + [(0, None, MOD_BLOCK, MOD_BLOCK // 2)], MOD_BLOCK)
+    blocks = [(0, None, 0, width), (0, None, 2 * width, width), (1, 0, 0, wide // 2), (1, 1, 0, wide // 2)]
+    return WeightImport(blocks, [(0, 3 * width), (5 * width, 6 * width)])
+
+
+def second_import(width, ff):
+    blocks = [(0, None, 0, width)] + [(k, j, 0, ff // 2) for k in (2, 3) for j in (0, 1)]
+    return WeightImport(blocks, [(3 * width, 5 * width)])
 
 
 def spread_heads(w_ref, lanes_ref):
@@ -441,17 +463,30 @@
         ).astype(BF16)
 
 
+def start_all(copies):
+    for copy in copies:
+        copy.start()
+
+
+def wait_all(copies):
+    for copy in copies:
+        copy.wait()
+
+
 def first_kernel(imports, *refs):
-    (w_mod, w_qkv, condition, tokens, embed, bias, positions), refs = refs[:7], refs[7:]
-    (mod_out, qkv_out, modulation_out, hidden_all, lifted, positions_all), refs = refs[:6], refs[6:]
+    (w_mod, w_qkv, condition, tokens, cotangent, embed, share, bias, positions), refs = refs[:9], refs[9:]
+    (mod_out, qkv_out, scale_a, gate_a, gate_b), refs = refs[:5], refs[5:]
+    (hidden_all, lifted_all, grads, lifted, positions_all), refs = refs[:5], refs[5:]
     (mod_all, lanes, hidden, mod_sem, spot_send, spot_recv), refs = refs[:6], refs[6:]
     imports.bind({0: w_mod, 1: lanes}, {0: mod_all, 1: qkv_out}, refs[:3])
     gather = RowGather(hidden, hidden_all, *refs[3:6])
+    gather_lifted = RowGather(lifted, lifted_all, *refs[6:9])
     item, column = lax.axis_index("dp"), lax.axis_index("seq")
+    width = tokens.shape[1]
     greet(imports.partners())
     imports.over(0).start()
-    imports.own(0).start()
-    imports.beside(0).start()
+    start_all(imports.own(0))
+    start_all(imports.beside(0))
     peers = [(item, lax.rem(column + k, 4)) for k in range(1, 4)]
     spot_copies = [
         pltpu.make_async_remote_copy(
@@ -464,51 +499,71 @@
         )
         for k, peer in enumerate(peers)
     ]
-    for copy in spot_copies:
-        copy.start()
+    start_all(spot_copies)
     positions_all[column] = positions[...]
     spread_heads(w_qkv, lanes)
-    imports.over(1).start()
-    imports.over(2).start()
-    imports.own(1).start()
-    imports.beside(1).start()
+    for block in range(1, len(imports.blocks)):
+        imports.over(block).start()
+    start_all(imports.own(1))
+    start_all(imports.beside(1))
     values = condition[...].astype(F32) + embed[...]
     lifted[...] = (values * jax.nn.sigmoid(values)).astype(BF16)
-    todo = imports.steps()
-    for step in todo[:5]:
-        step()
+    imports.arrive(0)
+    imports.pass_on(0)
+    imports.arrive(1)
     imports.complete(0)
-    imports.own(0).wait()
-    imports.beside(0).wait_recv()
-    imports.share(0).wait_recv()
-    store = pltpu.make_async_copy(mod_all, mod_out, mod_sem)
-    store.start()
-    weights = mod_all[...].reshape(-1, mod_all.shape[2])
-    modulation = jnp.dot(lifted[...], weights, preferred_element_type=F32)
-    modulation = modulation + bias[:, : mod_all.shape[2]]
-    modulation_out[...] = modulation
-    width = tokens.shape[1]
+    wait_all(imports.own(0))
+    for copy in imports.beside(0):
+        copy.wait_recv()
+
+    def modulate(block):
+        imports.share(block).wait_recv()
+        start = imports.blocks[block][2]
+        weights = mod_all[:, :, start : start + 2 * width].reshape(-1, 2 * width)
+        modulation = jnp.dot(lifted[...], weights, preferred_element_type=F32)
+        return [
+            modulation[:, k * width : (k + 1) * width]
+            + bias[:, pl.ds(imports.source_column(start + k * width), width)]
+            for k in range(2)
+        ]
+
+    shift, scale = modulate(0)
+    scale_a[...] = scale
     values = tokens[...].astype(F32)
     normed = values * inverse_rms(values)
-    hidden[...] = (normed * (1.0 + modulation[:, width:]) + modulation[:, :width]).astype(BF16)
+    hidden[...] = (normed * (1.0 + scale) + shift).astype(BF16)
     gather.start()
-    for step in todo[6:]:
-        step()
+    gather_lifted.start()
+    imports.pass_on(1)
+    imports.arrive(2)
+    imports.complete(1)
+    imports.arrive(3)
+    store = pltpu.make_async_copy(mod_all, mod_out, mod_sem)
+    gate_a[...], gate = modulate(1)
+    store.start()
+    gate_b[...] = gate
+    grads[...] = (cotangent[...].astype(F32) * share[...] * gate).astype(BF16)
+    imports.pass_on(2)
+    imports.pass_on(3)
     gather.pass_on()
+    imports.complete(2)
+    imports.complete(3)
+    gather_lifted.pass_on()
     imports.end()
-    imports.beside(0).wait_send()
-    imports.beside(1).wait()
-    imports.own(1).wait()
+    for copy in imports.beside(0):
+        copy.wait_send()
+    wait_all(imports.beside(1))
+    wait_all(imports.own(1))
     gather.end()
-    for copy in spot_copies:
-        copy.wait()
+    gather_lifted.end()
+    wait_all(spot_copies)
     store.wait()
 
 
-def first_stage(w_mod, w_qkv, condition, tokens, embed, bias, positions):
+def first_stage(w_mod, w_qkv, condition, tokens, cotangent, embed, share, bias, positions):
     rows, width = tokens.shape
     depth, lanes = w_mod.shape[0], 3 * HEADS // 4 * LANES
-    imports = first_import()
+    imports = first_import(width)
     vmem, anywhere = pl.BlockSpec(memory_space=pltpu.VMEM), pl.BlockSpec(memory_space=pl.ANY)
 
     def kernel(*refs):
@@ -517,17 +572,21 @@
     return pl.pallas_call(
         kernel,
         out_shape=[
-            jax.ShapeDtypeStruct((4, depth, MOD_BLOCK), BF16),
+            jax.ShapeDtypeStruct((4, depth, 4 * width), BF16),
             jax.ShapeDtypeStruct((4, depth, lanes), BF16),
-            jax.ShapeDtypeStruct((rows, MOD_BLOCK), F32),
+            jax.ShapeDtypeStruct((rows, width), F32),
+            jax.ShapeDtypeStruct((rows, width), F32),
+            jax.ShapeDtypeStruct((rows, width), F32),
             jax.ShapeDtypeStruct((4, rows, width), BF16),
+            jax.ShapeDtypeStruct((4, rows, width), BF16),
+            jax.ShapeDtypeStruct((rows, width), BF16),
             jax.ShapeDtypeStruct((rows, width), BF16),
             jax.ShapeDtypeStruct((4,) + positions.shape, jnp.int32),
         ],
-        in_specs=[anywhere] + [vmem] * 6,
-        out_specs=[anywhere, anywhere] + [vmem] * 4,
+        in_specs=[anywhere] + [vmem] * 8,
+        out_specs=[anywhere, anywhere] + [vmem] * 8,
         scratch_shapes=[
-            pltpu.VMEM((4, depth, MOD_BLOCK), BF16),
+            pltpu.VMEM((4, depth, 4 * width), BF16),
             pltpu.VMEM((4, depth, lanes), BF16),
             pltpu.VMEM((rows, width), BF16),
             pltpu.SemaphoreType.DMA,
@@ -535,12 +594,12 @@
             pltpu.SemaphoreType.DMA((3,)),
         ]
         + imports.scratch()
-        + RowGather.scratch(),
+        + RowGather.scratch() * 2,
         compiler_params=pltpu.CompilerParams(
             collective_id=WEIGHT_ID, has_side_effects=True, vmem_limit_bytes=60 * 2**20
         ),
         name="first_stage",
-    )(w_mod, w_qkv, condition, tokens, embed, bias, positions)
+    )(w_mod, w_qkv, condition, tokens, cotangent, embed, share, bias, positions)
 
 
 def rotated(values, tables, sign):
@@ -634,16 +693,17 @@
 
 def attend_kernel(imports, *refs):
     (hidden, w_qkv, w_out, cosine, ahead, behind, q_gain, k_gain), refs = refs[:8], refs[8:]
-    (w_mod, w_gate, w_up, lifted, bias), refs = refs[:5], refs[5:]
+    (w_mod, w_gate, w_up, lifted, bias, tokens, gate_a, grads), refs = refs[:8], refs[8:]
     (heads_out, rows_out, attended_out, branch_out), refs = refs[:4], refs[4:]
-    (mod_out, gate_out, up_out, modulation_out), refs = refs[:4], refs[4:]
+    (mod_out, gate_out, up_out, scale_out, middle_out, hidden_out, grads_all), refs = refs[:7], refs[7:]
     (mod_all, gate_own, up_own, mod_sem, load_sem), refs = refs[:5], refs[5:]
     sums = RowSums(*refs[:6])
-    imports.bind({0: w_mod, 2: w_gate, 3: w_up}, {0: mod_all, 2: gate_out, 3: up_out}, refs[6:])
+    imports.bind({0: w_mod, 2: w_gate, 3: w_up}, {0: mod_all, 2: gate_out, 3: up_out}, refs[6:9])
+    gather = RowGather(grads, grads_all, *refs[9:])
     greet(imports.partners())
     for block in range(len(imports.blocks)):
         imports.over(block).start()
-    imports.own(0).start()
+    start_all(imports.own(0))
     loads = [
         pltpu.make_async_copy(imports.whole(k, sums.column), ref, load_sem.at[k - 2])
         for k, ref in ((2, gate_own), (3, up_own))
@@ -655,7 +715,8 @@
     for copy in loads:
         copy.start()
     for array in imports.arrays:
-        imports.beside(array).start()
+        start_all(imports.beside(array))
+    gather.start()
     todo = imports.steps()
 
     def aside(number):
@@ -679,8 +740,6 @@
             values = values * head_inverse(values) * gain
             start = pair * 2 * LANES + half * LANES
             rows_out[:, start : start + LANES] = rotated(values, tables, 1).astype(BF16)
-        if pair == heads - 1:
-            aside(1)
     aside(1)
     for copy in loads:
         copy.wait()
@@ -698,43 +757,42 @@
                 preferred_element_type=F32,
             )
             attended_out[block, spans[0]] = mixed.astype(BF16)
-            aside(1)
         sums.put(index, jnp.dot(attended_out[block, :], w_out[...], preferred_element_type=F32))
-    aside(6)
-    imports.own(0).wait()
-    imports.beside(0).wait_recv()
-    arrays = [block[0] for block in imports.blocks]
-    mod_blocks = [index for index, array in enumerate(arrays) if array == 0]
-
-    def modulate(number):
-        imports.share(mod_blocks[number]).wait_recv()
-        span = slice(number * MOD_BLOCK, (number + 1) * MOD_BLOCK)
-        weights = mod_all[:, :, span].reshape(-1, MOD_BLOCK)
-        modulation = jnp.dot(lifted[...], weights, preferred_element_type=F32)
-        start = imports.base + number * MOD_BLOCK
-        modulation_out[:, span] = modulation + bias[:, start : start + MOD_BLOCK]
-
-    modulate(0)
-    aside(len(todo))
-    branch_out[...] = sums.sums()
-    modulate(1)
+        aside((1, 3, 4, len(todo))[index])
+    gather.pass_on()
+    wait_all(imports.own(0))
+    for copy in imports.beside(0):
+        copy.wait_recv()
+    imports.share(0).wait_recv()
     store = pltpu.make_async_copy(mod_all, mod_out, mod_sem)
     store.start()
+    width = tokens.shape[1]
+    weights = mod_all[...].reshape(-1, 2 * width)
+    modulation = jnp.dot(lifted[...], weights, preferred_element_type=F32)
+    modulation = modulation + bias[:, pl.ds(imports.source_column(0), 2 * width)]
+    scale = modulation[:, width:]
+    scale_out[...] = scale
+    branch = sums.sums()
+    branch_out[...] = branch
+    middle = tokens[...].astype(F32) + gate_a[...] * branch
+    middle_out[...] = middle
+    hidden_out[...] = (middle * inverse_rms(middle) * (1.0 + scale) + modulation[:, :width]).astype(BF16)
     imports.end()
-    imports.beside(0).wait_send()
+    for copy in imports.beside(0):
+        copy.wait_send()
     for array in imports.arrays[1:]:
-        imports.beside(array).wait()
+        wait_all(imports.beside(array))
+    gather.end()
     for copy in stores:
         copy.wait()
     store.wait()
 
 
-def attend(hidden, w_qkv, w_out, tables, q_gain, k_gain, w_mod, w_gate, w_up, lifted, bias):
+def attend(hidden, w_qkv, w_out, tables, q_gain, k_gain, w_mod, w_gate, w_up, lifted, bias, tokens, gate_a, grads):
     patches, wide = hidden.shape[0], w_qkv.shape[1]
     rows, width = patches // 4, hidden.shape[1]
     depth, ff = w_mod.shape[0], w_gate.shape[1] // 4
-    rest = w_mod.shape[1] - MOD_BLOCK
-    imports = second_import(ff)
+    imports = second_import(width, ff)
     vmem, anywhere = pl.BlockSpec(memory_space=pltpu.VMEM), pl.BlockSpec(memory_space=pl.ANY)
 
     def kernel(*refs):
@@ -747,27 +805,192 @@
             jax.ShapeDtypeStruct((patches, wide), BF16),
             jax.ShapeDtypeStruct((patches, wide // 3), BF16),
             jax.ShapeDtypeStruct((rows, width), F32),
-            jax.ShapeDtypeStruct((4, depth, rest), BF16),
+            jax.ShapeDtypeStruct((4, depth, 2 * width), BF16),
             jax.ShapeDtypeStruct((4, depth, ff), BF16),
             jax.ShapeDtypeStruct((4, depth, ff), BF16),
-            jax.ShapeDtypeStruct((rows, rest), F32),
+            jax.ShapeDtypeStruct((rows, width), F32),
+            jax.ShapeDtypeStruct((rows, width), F32),
+            jax.ShapeDtypeStruct((rows, width), BF16),
+            jax.ShapeDtypeStruct((4, rows, width), BF16),
         ],
-        in_specs=[vmem] * 8 + [anywhere] * 3 + [vmem] * 2,
-        out_specs=[vmem] * 4 + [anywhere] * 3 + [vmem],
+        in_specs=[vmem] * 8 + [anywhere] * 3 + [vmem] * 5,
+        out_specs=[vmem] * 4 + [anywhere] * 3 + [vmem] * 4,
         scratch_shapes=[
-            pltpu.VMEM((4, depth, rest), BF16),
+            pltpu.VMEM((4, depth, 2 * width), BF16),
             pltpu.VMEM((depth, ff), BF16),
             pltpu.VMEM((depth, ff), BF16),
             pltpu.SemaphoreType.DMA,
             pltpu.SemaphoreType.DMA((4,)),
         ]
         + RowSums.scratch(rows, width)
-        + imports.scratch(),
+        + imports.scratch()
+        + RowGather.scratch(),
         compiler_params=pltpu.CompilerParams(
             collective_id=ATTEND_ID, has_side_effects=True, vmem_limit_bytes=63 * 2**20
         ),
         name="attend",
-    )(hidden, w_qkv, w_out, *tables, q_gain, k_gain, w_mod, w_gate, w_up, lifted, bias)
+    )(hidden, w_qkv, w_out, *tables, q_gain, k_gain, w_mod, w_gate, w_up, lifted, bias, tokens, gate_a, grads)
+
+
+def mlp_kernel(sums, *refs):
+    (hidden, grads_all, w_gate, w_up, w_down), refs = refs[:5], refs[5:]
+    (middle, scale, gate_a, gate_b, branch_a, cotangent, share), refs = refs[:7], refs[7:]
+    (hidden_all, inner, grad_gate, grad_up), refs = refs[:4], refs[4:]
+    (block_out, middle_out, branch_grad_out, mod_out), refs = refs[:4], refs[4:]
+    handed_out, refs = refs[: len(sums.leaving)], refs[len(sums.leaving) :]
+    if sums.parts:
+        sums.bind([], [], None, [], None, [], handed_out, refs[30:])
+    sums.others = {
+        "inner": (inner, lambda: None),
+        "grad_branch_b": (grads_all, lambda: None),
+        "hidden_b": (hidden_all, lambda: None),
+        "grad_gate_in": (grad_gate, lambda: None),
+    }
+    gather = RowGather(hidden, hidden_all, *refs[:3])
+    halves = [RowSums(*refs[3 + 6 * k : 9 + 6 * k]) for k in range(4)]
+    sums_grad, sums_branch = halves[:2], halves[2:]
+    first = sums_grad[0]
+    greet([first.sibling, first.across] + (sums.partners[:2] if sums.parts else []))
+    gather.start()
+    rows, width = hidden.shape
+    near, far = first.chip * 2, (1 - first.chip) * 2
+    depth = w_gate.shape[0] * w_gate.shape[1]
+    gate_weights, up_weights = (ref[...].reshape(depth, ref.shape[2]) for ref in (w_gate, w_up))
+
+    def block(ref, pair, start, count):
+        return jnp.concatenate([ref[pair + k, start : start + count] for k in range(2)], axis=0)
+
+    def process(pair, start, count):
+        values = block(hidden_all, pair, start, count)
+        gate_in = jnp.dot(values, gate_weights, preferred_element_type=F32)
+        up_in = jnp.dot(values, up_weights, preferred_element_type=F32)
+        grad_inner = over_rows(block(grads_all, pair, start, count), w_down[...])
+        logistic = jax.nn.sigmoid(gate_in)
+        activated = gate_in * logistic
+        slope = logistic * (1.0 + gate_in * (1.0 - logistic))
+        results = (
+            (activated * up_in).astype(BF16),
+            (grad_inner * up_in * slope).astype(BF16),
+            (grad_inner * activated).astype(BF16),
+        )
+        for ref, result in zip((inner, grad_gate, grad_up), results, strict=True):
+            for k in range(2):
+                at = pl.multiple_of((pair + k) * rows + start, 16)
+                ref[pl.ds(at, count), :] = result[k * count : (k + 1) * count]
+        return over_rows(results[1], gate_weights) + over_rows(results[2], up_weights)
+
+    def put(sums, partial, count, far_rows):
+        @pl.when(first.core == 0)
+        def _():
+            held[0, :count], held[1, :count] = partial[count:], partial[:count]
+
+        @pl.when(first.core == 1)
+        def _():
+            held[0, :count], held[1, :count] = partial[:count], partial[count:]
+
+        if far_rows:
+            sums.put(0, held[0, :count])
+            sums.put(1, held[1, :count])
+        else:
+            sums.put(2, held[0, :count])
+            return held[1, :count]
+
+    held, own_grad, own_branch = refs[27:30]
+    half = rows // 2
+    for piece in range(GATHER_PIECES):
+        gather.beside(piece).wait_recv()
+    gather.local().wait()
+    partial = process(near, 0, rows)
+    for k in range(2):
+        part = slice(k * half, (k + 1) * half)
+        both = jnp.concatenate([partial[part], partial[rows + k * half : rows + (k + 1) * half]], axis=0)
+        own_grad[part] = put(sums_grad[k], both, half, False)
+    for k in range(2):
+        pieces = range(k * GATHER_PIECES // 2, (k + 1) * GATHER_PIECES // 2)
+        for piece in pieces:
+            gather.over(piece).wait_recv()
+            gather.onward(piece).start()
+        for piece in pieces:
+            gather.onward(piece).wait_recv()
+        put(sums_grad[k], process(far, k * half, half), half, True)
+    sums.do(*["b0", "b1"][: len(sums.parts)])
+    for k in range(2):
+        at = [pl.ds(pl.multiple_of((far + j) * rows + k * half, 16), half) for j in range(2)]
+        values = jnp.concatenate([inner[part, :] for part in at], axis=0)
+        put(sums_branch[k], jnp.dot(values, w_down[...], preferred_element_type=F32), half, True)
+    sums.do(*["b2", "b3"][: len(sums.parts)])
+    for k in range(2):
+        at = [pl.ds(pl.multiple_of((near + j) * rows + k * half, 16), half) for j in range(2)]
+        values = jnp.concatenate([inner[part, :] for part in at], axis=0)
+        partial = jnp.dot(values, w_down[...], preferred_element_type=F32)
+        own_branch[k * half : (k + 1) * half] = put(sums_branch[k], partial, half, False)
+    sums.do(*["f0", "f1"][: len(sums.parts)])
+    for k in range(2):
+        part = slice(k * half, (k + 1) * half)
+        sums_grad[k].put(3, own_grad[part])
+        grad_hidden = sums_grad[k].sums()
+        values = middle[part]
+        inverse = inverse_rms(values)
+        normed = values * inverse
+        grad_out = cotangent[part].astype(F32) * share[...]
+        grad_middle = grad_out + rms_back(grad_hidden * (1.0 + scale[part]), normed, inverse)
+        middle_out[part] = grad_middle
+        branch_grad_out[part] = (grad_middle * gate_a[part]).astype(BF16)
+        mod_out[part, :width] = (grad_middle * branch_a[part]).astype(BF16)
+        mod_out[part, width : 2 * width] = grad_hidden.astype(BF16)
+        mod_out[part, 2 * width : 3 * width] = (grad_hidden * normed).astype(BF16)
+    sums.do(*["f2", "f3"][: len(sums.parts)])
+    for k in range(2):
+        part = slice(k * half, (k + 1) * half)
+        sums_branch[k].put(3, own_branch[part])
+        branch = sums_branch[k].sums()
+        block_out[part] = (middle[part] + gate_b[part] * branch).astype(BF16)
+        grad_out = cotangent[part].astype(F32) * share[...]
+        mod_out[part, 3 * width :] = (grad_out * branch).astype(BF16)
+    for piece in range(GATHER_PIECES):
+        gather.over(piece).wait_send()
+        gather.beside(piece).wait_send()
+        gather.onward(piece).wait_send()
+    sums.end()
+
+
+def mlp(hidden, grads_all, w_gate, w_up, w_down, rest, parts):
+    rows, width = hidden.shape
+    ff = w_down.shape[0]
+    sums = GradSums(parts, (), [], (16, LANES))
+    vmem, anywhere = pl.BlockSpec(memory_space=pltpu.VMEM), pl.BlockSpec(memory_space=pl.ANY)
+
+    def kernel(*refs):
+        mlp_kernel(sums, *refs)
+
+    return pl.pallas_call(
+        kernel,
+        out_shape=[
+            jax.ShapeDtypeStruct((4, rows, width), BF16),
+            jax.ShapeDtypeStruct((4 * rows, ff), BF16),
+            jax.ShapeDtypeStruct((4 * rows, ff), BF16),
+            jax.ShapeDtypeStruct((4 * rows, ff), BF16),
+            jax.ShapeDtypeStruct((rows, width), BF16),
+            jax.ShapeDtypeStruct((rows, width), F32),
+            jax.ShapeDtypeStruct((rows, width), BF16),
+            jax.ShapeDtypeStruct((rows, 4 * width), BF16),
+        ]
+        + [jax.ShapeDtypeStruct(part.handed(), BF16) for part in parts],
+        in_specs=[vmem] * 12,
+        out_specs=[vmem] * 8 + [anywhere] * len(parts),
+        scratch_shapes=RowGather.scratch()
+        + RowSums.scratch(rows // 2, width) * 4
+        + [
+            pltpu.VMEM((2, rows // 2, width), F32),
+            pltpu.VMEM((rows, width), F32),
+            pltpu.VMEM((rows, width), F32),
+        ]
+        + (sums.scratch([]) if parts else []),
+        compiler_params=pltpu.CompilerParams(
+            collective_id=MLP_ID, has_side_effects=True, vmem_limit_bytes=63 * 2**20
+        ),
+        name="mlp",
+    )(hidden, grads_all, w_gate, w_up, w_down, *rest)
 
 
 def rows_to_columns(values, blocks):
@@ -795,11 +1018,17 @@
 
 
 class Part:
-    def __init__(self, left, right, rows, span, out, order, by_rows=False, in_lanes=False, bias=False):
+    def __init__(self, left, right, rows, span, out, order, at=None, **kinds):
         self.left, self.right, self.rows = left, right, rows
         self.start, self.columns, self.out = span[0], span[1] - span[0], out
-        self.order, self.by_rows, self.in_lanes, self.bias = order, by_rows, in_lanes, bias
+        self.at = self.start if at is None else at
+        self.order = order
+        for kind in ("by_rows", "in_lanes", "bias", "enter", "leave"):
+            setattr(self, kind, kinds.get(kind, False))
         self.slab = padded_rows(rows)
+
+    def handed(self):
+        return (2, 2, self.slab, self.columns)
 
 
 def split_part(left, right, rows, columns, out, order, **kinds):
@@ -811,24 +1040,38 @@
 
 
 class GradSums:
-    def __init__(self, parts, names, shared_shapes, small_shape):
+    def __init__(self, parts, names, shared_shapes, small_shape, after=()):
         self.parts, self.names = parts, names
+        self.after = dict(after)
         self.shared_shapes, self.small_shape = shared_shapes, small_shape
-        self.has_rows = any(part.by_rows for part in parts)
-
-    def spread(self, group):
-        rows, columns, whole = self.shared_shapes[group]
-        return rows, columns if whole else -(-columns // (4 * TILE)) * TILE
+        self.has_rows = any(part.by_rows and not part.leave for part in parts)
+        self.entering = [index for index, part in enumerate(parts) if part.enter]
+        self.leaving = [index for index, part in enumerate(parts) if part.leave]
 
     def scratch(self, array_shapes):
         parts, count, groups = self.parts, len(self.parts), len(self.shared_shapes)
-        shapes = [pltpu.VMEM(shape, BF16) for shape in array_shapes]
-        shapes += [pltpu.VMEM((4,) + self.spread(group), BF16) for group in range(groups)]
-        for lead in ((2, 2, 2), (2, 2), (2,), ()):
-            shapes += [pltpu.VMEM(lead + (part.slab, part.columns), BF16) for part in parts]
+        none = pltpu.VMEM((16, LANES), BF16)
+        shapes = [
+            none if name in self.after else pltpu.VMEM(shape, BF16)
+            for name, shape in zip(self.names, array_shapes, strict=True)
+        ]
+        shapes += [pltpu.VMEM((4, rows, columns), BF16) for rows, _, _, columns in self.shared_shapes]
+
+        def each(lead, needed):
+            return [
+                pltpu.VMEM(lead(part) + (part.slab, part.columns), BF16) if needed(part) else none
+                for part in parts
+            ]
+
+        shapes += each(lambda part: (2, 2) if part.enter else (2, 2, 2), lambda part: True)
+        shapes += each(lambda part: (2, 2), lambda part: not part.enter)
+        shapes += each(lambda part: (2,), lambda part: not part.leave)
+        shapes += each(lambda part: (), lambda part: not part.leave)
         for _ in range(2):
             for part in parts:
-                if part.by_rows:
+                if part.leave:
+                    shapes.append(none)
+                elif part.by_rows:
                     shapes.append(pltpu.VMEM((part.slab, part.columns), BF16))
                 else:
                     shapes.append(pltpu.VMEM((4, padded_rows(part.rows // 4), part.columns), BF16))
@@ -838,10 +1081,11 @@
             pltpu.VMEM((tallest, widest), F32),
             pltpu.VMEM((4,) + self.small_shape, F32),
             pltpu.VMEM((3,) + self.small_shape, F32),
-            pltpu.SemaphoreType.DMA((len(self.names),)),
-            pltpu.SemaphoreType.DMA((groups, 3)),
-            pltpu.SemaphoreType.DMA((groups, 3)),
-            pltpu.SemaphoreType.DMA((groups,)),
+            pltpu.SemaphoreType.DMA((max(len(self.names), 1),)),
+            pltpu.SemaphoreType.DMA((max(groups, 1), 3)),
+            pltpu.SemaphoreType.DMA((max(groups, 1), 3)),
+            pltpu.SemaphoreType.DMA((max(groups, 1),)),
+            pltpu.SemaphoreType.DMA((count,)),
             pltpu.SemaphoreType.DMA((count, 3)),
             pltpu.SemaphoreType.DMA((count, 3)),
             pltpu.SemaphoreType.DMA((count, 3)),
@@ -850,7 +1094,7 @@
             pltpu.SemaphoreType.DMA((6,)),
         ]
 
-    def bind(self, ins, shared, small_in, outs, small_out, scratch):
+    def bind(self, ins, shared, small_in, outs, small_out, handed_in, handed_out, scratch):
         count, groups, names = len(self.parts), len(self.shared_shapes), self.names
         refs = list(scratch)
 
@@ -861,12 +1105,15 @@
 
         self.shared, self.small_in, self.outs, self.small_out = shared, small_in, outs, small_out
         self.held = dict(zip(names, take(len(names)), strict=True))
+        for name, place in self.after.items():
+            self.held[name] = self.held[place]
         self.gathered = take(groups)
         self.own, self.first_in = take(count), take(count)
         self.second_in, self.third_in = take(count), take(count)
         self.slabs, self.slab_in = take(count), take(count)
         self.total, self.small, self.small_came = take(3)
-        load_sem, self.share_send, self.share_recv, own_sem, self.send_sem, self.recv_sem = take(6)
+        load_sem, self.share_send, self.share_recv, own_sem, hand_sem = take(5)
+        self.send_sem, self.recv_sem = take(2)
         self.last_send, self.last_recv, self.small_send, self.small_recv = take(4)
         item, column = lax.axis_index("dp"), lax.axis_index("seq")
         self.column = column
@@ -888,6 +1135,13 @@
         ]
         self.ready = set()
         self.others = {}
+        self.handing = {
+            index: pltpu.make_async_copy(ref, self.own[index], hand_sem.at[index])
+            for index, ref in zip(self.entering, handed_in, strict=True)
+        }
+        for index, ref in zip(self.leaving, handed_out, strict=True):
+            half = self.own[index].at[self.half(index, True)]
+            self.handing[index] = pltpu.make_async_copy(half, ref, hand_sem.at[index])
 
     def greet(self):
         barrier = pltpu.get_barrier_semaphore()
@@ -904,8 +1158,11 @@
         pl.semaphore_wait(barrier, waits)
 
     def load(self):
+        for index in self.entering:
+            self.handing[index].start()
         for name in self.names:
-            self.loads[name].start()
+            if name not in self.after:
+                self.loads[name].start()
 
     def remote(self, source, target_ref, send, recv, target):
         return pltpu.make_async_remote_copy(
@@ -918,10 +1175,8 @@
         )
 
     def columns_of(self, group, place):
-        wide, narrow = self.shared_shapes[group][1], self.spread(group)[1]
-        if wide == narrow:
-            return self.shared[group]
-        start = first_tile(place, wide // TILE) * TILE
+        _, wide, first, narrow = self.shared_shapes[group]
+        start = first_tile(place, wide // TILE) * TILE + first
         return self.shared[group].at[:, pl.ds(pl.multiple_of(start, TILE), narrow)]
 
     def shares(self, group):
@@ -957,7 +1212,7 @@
             ref, wait = self.others[name]
             if first:
                 wait()
-            return ref[...].reshape(4 * ref.shape[1], ref.shape[2])
+            return ref[...].reshape(-1, ref.shape[-1])
         if first:
             self.loads[name].wait()
         return self.held[name][...]
@@ -969,7 +1224,7 @@
         if part.bias:
             sums = jnp.sum(right.astype(F32), axis=0, keepdims=True)
             for tile in range(part.columns // TILE):
-                row = part.start // TILE + tile
+                row = part.at // TILE + tile
                 self.small[0, row : row + 1] = sums[:, tile * TILE : (tile + 1) * TILE]
         own, rows = self.own[index], part.rows
         if part.in_lanes:
@@ -993,7 +1248,14 @@
             values = jnp.concatenate([values, jnp.zeros((padded - rows, columns), F32)], axis=0)
         return values.astype(BF16)
 
+    def half(self, index, mine):
+        order = self.parts[index].order
+        pick = self.bits[order] if mine else 1 - self.bits[order]
+        return (slice(None), slice(None), pick) if order == 0 else (slice(None), pick)
+
     def place(self, index, high, low):
+        if self.parts[index].enter:
+            return (high, low)
         if self.parts[index].order == 0:
             return (high, low, self.bits[0])
         return (high, self.bits[1], low)
@@ -1004,9 +1266,8 @@
         sems = self.send_sem.at[index, step], self.recv_sem.at[index, step]
         own = self.own[index]
         if step == 0:
-            pick = 1 - self.bits[order]
-            half = (slice(None), slice(None), pick) if order == 0 else (slice(None), pick)
-            return self.remote(own.at[half], self.first_in[index], *sems, self.partners[order])
+            source = own.at[self.half(index, False)]
+            return self.remote(source, self.first_in[index], *sems, self.partners[order])
         if step == 1:
             place = self.place(index, slice(None), 1 - self.bits[other])
             return self.remote(own.at[place], self.second_in[index], *sems, self.partners[other])
@@ -1014,6 +1275,10 @@
         return self.remote(own.at[place], self.third_in[index], *sems, self.partners[2])
 
     def begin(self, index):
+        if self.parts[index].enter:
+            self.handing[index].wait()
+            self.stage(index, 1).start()
+            return
         self.multiply(index)
         self.stage(index, 0).start()
 
@@ -1024,7 +1289,10 @@
                 place = self.place(index, high, low)
                 came = self.first_in[index][high, low].astype(F32)
                 self.own[index][place] = (self.own[index][place].astype(F32) + came).astype(BF16)
-        self.stage(index, 1).start()
+        if self.parts[index].leave:
+            self.handing[index].start()
+        else:
+            self.stage(index, 1).start()
 
     def end_second(self, index):
         self.stage(index, 1).wait()
@@ -1076,14 +1344,14 @@
 
     def end_last(self, index):
         part = self.parts[index]
-        out, stop = self.outs[part.out], part.start + part.columns
+        out, stop = self.outs[part.out], part.at + part.columns
         if part.by_rows:
 
             @pl.when(self.elsewhere)
             def _():
                 self.last(index)[0].wait()
 
-            out[:, part.start : stop] = self.slab_in[index][...].astype(F32)[: part.rows]
+            out[:, part.at : stop] = self.slab_in[index][...].astype(F32)[: part.rows]
             return
         for copy in self.last(index):
             copy.wait()
@@ -1092,10 +1360,10 @@
         for k in range(4):
             values = self.slab_in[index][k].astype(F32)[:rows]
             if len(out.shape) == 3:
-                out[k, :, part.start : stop] = values
+                out[k, :, part.at : stop] = values
             else:
                 start = first_tile(k, wide // TILE) * TILE
-                out[:, start + part.start : start + stop] = values
+                out[:, start + part.at : start + stop] = values
 
     def small_step(self, step):
         if step < 3:
@@ -1120,33 +1388,32 @@
         for copy in self.small_step(at):
             copy.start()
 
-    def steps(self, ahead=2):
-        count = len(self.parts)
-        todo = [lambda: self.small.__setitem__(0, self.small_in[...])]
-        todo += [lambda index=index: self.begin(index) for index in range(min(ahead, count))]
-        for step in range(count + 3):
-            if step < count:
-                todo.append(lambda step=step: self.end_first(step))
-                if step + ahead < count:
-                    todo.append(lambda step=step: self.begin(step + ahead))
-            if 0 <= step - 1 < count:
-                todo.append(lambda step=step: self.end_second(step - 1))
-            if 0 <= step - 2 < count:
-                todo.append(lambda step=step: self.end_third(step - 2))
-            if 0 <= step - 3 < count:
-                todo.append(lambda step=step: self.end_last(step - 3))
-            at = step - max(count - ahead, 0)
-            if at == 0:
-                todo.append(lambda: self.small_step(0)[0].start())
-            if 1 <= at <= 3:
-                todo.append(lambda at=at: self.end_small(at))
-        todo.append(self.end)
-        return todo
+    def do(self, *steps):
+        kinds = {
+            "b": self.begin,
+            "f": self.end_first,
+            "s": self.end_second,
+            "t": self.end_third,
+            "l": self.end_last,
+            "x": self.small_exchange,
+            "r": lambda number: self.loads[self.names[number]].start(),
+        }
+        for step in steps:
+            kinds[step[0]](int(step[1:]))
+
+    def small_exchange(self, at):
+        if at == 0:
+            self.small_step(0)[0].start()
+        elif at < 4:
+            self.end_small(at)
+        else:
+            self.small_out[self.column] = self.small[3]
+            for copy in self.small_step(3):
+                copy.wait()
 
     def end(self):
-        self.small_out[self.column] = self.small[3]
-        for copy in self.small_step(3):
-            copy.wait()
+        for index in self.leaving:
+            self.handing[index].wait()
 
 
 def split(refs, *counts):
@@ -1157,88 +1424,169 @@
     return groups + [refs[start:]]
 
 
-def weight_grads(parts, arrays, shared, small, out_shapes):
+LAST_STEPS = (
+    ("b0", "b1", "b2", "b3", "b4"),
+    ("s0", "s3", "s1"),
+    ("b5", "s4", "t0", "s2"),
+    ("t3", "b6", "t1", "f5"),
+    ("t4", "l0", "l3", "t2", "x0", "l1"),
+    ("f6", "x1", "l4", "s5", "l2", "x2", "t5", "x3", "s6", "l5", "t6", "x4", "l6"),
+)
+
+
+def last_grads(parts, arrays, shared, small, handed, out_shapes, condition, embed, rows_a, rows_b, mods):
     names = tuple(arrays)
-    sums = GradSums(parts, names, [value.shape + (whole,) for value, whole in shared], small.shape)
+    shapes = [value.shape + (first, columns) for value, first, columns in shared]
+    sums = GradSums(parts, names, shapes, small.shape)
     count = len(out_shapes)
+    width = condition.shape[1]
 
     def kernel(*refs):
-        ins, given, (small_in,), outs, (small_out,), scratch = split(
-            refs, len(names), len(shared), 1, count, 1
+        ins, given, handed_in, given_mods, (small_in, seen, embed_in, low, high), outs, lasts, refs = split(
+            refs, len(names), len(shared), len(handed), len(mods), 5, count, 2
         )
-        sums.bind(ins, given, small_in, outs, small_out, scratch)
+        (small_out, condition_out), held, (mod_sem,), scratch = lasts, refs[:2], refs[2:3], refs[3:]
+        sums.bind(ins, given, small_in, outs, small_out, handed_in, [], scratch)
         sums.load()
+        loads = [
+            pltpu.make_async_copy(source, target, mod_sem.at[k])
+            for k, (source, target) in enumerate(zip(given_mods, held, strict=True))
+        ]
+        start_all(loads)
         sums.greet()
         sums.share()
-        for step in sums.steps(ahead=3):
-            step()
-
+        sums.small[0] = small_in[...]
+        first, rest = held
+        condition_out[...] = jnp.zeros_like(condition_out)
+        work = [
+            (low, 0, first, 0, 2 * width),
+            (high, 0, first, 2 * width, width),
+            (high, width, rest, 0, 2 * width),
+            (high, 3 * width, first, 3 * width, width),
+        ]
+        for number, steps in enumerate(LAST_STEPS):
+            sums.do(*steps)
+            if number == 0:
+                wait_all(loads)
+            if number < 4:
+                rows, at, weights, start, columns = work[number]
+                condition_out[...] += over_rows(
+                    rows[:, at : at + columns], weights[:, start : start + columns]
+                )
+            if number == 4:
+                values = seen[...].astype(F32) + embed_in[...]
+                condition_out[...] = condition_out[...] * silu_slope(values)
+        sums.end()
+
+    vmem, anywhere = pl.BlockSpec(memory_space=pltpu.VMEM), pl.BlockSpec(memory_space=pl.ANY)
     return pl.pallas_call(
         kernel,
         out_shape=[jax.ShapeDtypeStruct(shape, F32) for shape in out_shapes]
-        + [jax.ShapeDtypeStruct((4,) + small.shape, F32)],
-        in_specs=[pl.BlockSpec(memory_space=pl.ANY)] * (len(names) + len(shared))
-        + [pl.BlockSpec(memory_space=pltpu.VMEM)],
-        out_specs=[pl.BlockSpec(memory_space=pltpu.VMEM)] * (count + 1),
-        scratch_shapes=sums.scratch([value.shape for value in arrays.values()]),
+        + [
+            jax.ShapeDtypeStruct((4,) + small.shape, F32),
+            jax.ShapeDtypeStruct(condition.shape, F32),
+        ],
+        in_specs=[anywhere] * (len(names) + len(shared) + len(handed) + len(mods)) + [vmem] * 5,
+        out_specs=[vmem] * (count + 2),
+        scratch_shapes=[pltpu.VMEM(value.shape, BF16) for value in mods]
+        + [pltpu.SemaphoreType.DMA((len(mods),))]
+        + sums.scratch([value.shape for value in arrays.values()]),
         compiler_params=pltpu.CompilerParams(
             collective_id=SUM_ID, has_side_effects=True, vmem_limit_bytes=63 * 2**20
         ),
-        name="weight_grads",
-    )(*arrays.values(), *[value for value, _ in shared], small)
-
-
-BACK_INPUTS = ("rows", "heads", "w_qkv", "w_out", "cosine", "ahead", "behind", "q_gain", "k_gain")
-
-
-def back_kernel(sums, grad_in, lifted, given, lifted_all, project_out, hidden_out, gains_out, refs):
-    branch_in, loads_into, pieces, scratch = split(refs, 1, 4, 1)
-    (branch_all,), (rows, heads, w_qkv, w_out), (grad_heads,) = branch_in, loads_into, pieces
-    load_sem = scratch[0]
-    gather, gather_lifted = RowGather(grad_in, branch_all, *scratch[1:4]), RowGather(lifted, lifted_all, *scratch[4:7])
-    row_sums = RowSums(*scratch[7:])
-    cosine, ahead, behind, q_gain, k_gain = given[4:]
+        name="last_grads",
+    )(
+        *arrays.values(),
+        *[value for value, _, _ in shared],
+        *handed,
+        *mods,
+        small,
+        condition,
+        embed,
+        rows_a,
+        rows_b,
+    )
+
+
+BACK_STEPS = {
+    "start": ("b0", "b1", "b2", "b3", "b4", "b5", "r3", "s1", "s0", "s3", "t1"),
+    "gathered": ("b6", "b7"),
+    "head0": ("f2", "l1", "t0", "t3"),
+    "head1": ("s2", "s4", "f5", "f6", "l0", "l3"),
+    "head2": ("f7", "t4", "b8", "s5"),
+    "head3": ("b11", "b12", "t2", "l4", "b9"),
+    "put1": ("b10", "s6", "s7", "x0"),
+    "put3": ("t5", "f8", "l2", "x1", "t6", "t7", "l5", "f11", "x2"),
+    "end": ("f9", "x3", "l6", "l7", "f12", "f10", "x4"),
+}
+
+
+def pack_heads(lanes_ref, packed_ref):
+    rows, count = lanes_ref.shape[0], lanes_ref.shape[1] // LANES
+    lane = lax.broadcasted_iota(jnp.int32, (rows, LANES), 1)
+    for tile in range(packed_ref.shape[1] // LANES):
+        values = jnp.zeros((rows, LANES), F32)
+        for head in range(count):
+            start = head * HD - tile * LANES
+            if -HD < start < LANES:
+                one = lanes_ref[:, head * LANES : (head + 1) * LANES].astype(F32)
+                one = pltpu.roll(one, start % LANES, 1) if start else one
+                values = jnp.where(jnp.logical_and(lane >= start, lane < start + HD), one, values)
+        packed_ref[:, tile * LANES : (tile + 1) * LANES] = values.astype(BF16)
+
+
+def back_kernel(sums, own, outs, refs):
+    grad_in, rows_in, heads_in, w_qkv_in, w_out_in, cosine, ahead, behind, q_gain, k_gain = own[:10]
+    grad_middle, tokens, scale = own[10:]
+    tokens_out, mod_out, gains_out = outs
+    (branch_all, rows, heads, w_qkv, w_out, grad_heads, packed, load_sem), refs = refs[:8], refs[8:]
+    gather = RowGather(grad_in, branch_all, *refs[:3])
+    row_sums = RowSums(*refs[3:])
     local_rows = grad_in.shape[0]
     count = grad_heads.shape[1] // LANES
     factor = HD ** (-0.5)
     loads = [
         pltpu.make_async_copy(source, target, load_sem.at[k])
-        for k, (source, target) in enumerate(zip(given[:4], (rows, heads, w_qkv, w_out), strict=True))
+        for k, (source, target) in enumerate(
+            ((rows_in, rows), (w_out_in, w_out), (w_qkv_in, w_qkv))
+        )
     ]
-    for k in (3, 0, 1, 2):
+
+    def load_head(head):
+        return [
+            pltpu.make_async_copy(
+                heads_in.at[:, pl.ds((k * count + head) * LANES, LANES)],
+                heads.at[head % 2, k],
+                load_sem.at[3 + 2 * (head % 2) + k],
+            )
+            for k in range(2)
+        ]
+
+    for k in (1, 0, 2):
         loads[k].start()
+    start_all(load_head(0))
     sums.load()
     sums.greet()
-
     gather.start()
-    gather_lifted.start()
     sums.share()
-
-    def lifted_ready():
-        gather_lifted.pass_on()
-        gather_lifted.end()
-
-    sums.others["lifted"] = (lifted_all, lifted_ready)
-    todo = sums.steps(ahead=3)
-
-    def aside(number):
-        for _ in range(min(number, len(todo))):
-            todo.pop(0)()
-
-    aside(4)
+    sums.small[0] = jnp.zeros_like(sums.small[0])
+    sums.others["grad_branch_a"] = (branch_all, lambda: None)
+    sums.others["grad_project"] = (packed, lambda: None)
+    sums.do(*BACK_STEPS["start"])
     gather.pass_on()
     gather.end()
-    loads[3].wait()
+    loads[1].wait()
     grad_branch = branch_all[...].reshape(4 * local_rows, branch_all.shape[2])
     grad_heads[...] = over_rows(grad_branch, w_out[...]).astype(BF16)
+    sums.do(*BACK_STEPS["gathered"])
     loads[0].wait()
-    loads[1].wait()
     tables = cosine[...], ahead[...], behind[...]
     block = 256
     gain_sums = [jnp.zeros((1, LANES), F32), jnp.zeros((1, LANES), F32)]
-    counts = (1, 3, 3, 3)
     for head in range(count):
         spans = [slice((k * count + head) * LANES, (k * count + head + 1) * LANES) for k in range(3)]
+        if head + 1 < count:
+            start_all(load_head(head + 1))
         keys, values = rows[:, spans[1]], rows[:, spans[2]]
         grad_query, grad_key, grad_value = [], None, None
         for start in range(0, rows.shape[0], block):
@@ -1254,79 +1602,98 @@
             value_term = jnp.dot(probs.astype(BF16), grads, preferred_element_type=F32)
             grad_key = key_term if grad_key is None else grad_key + key_term
             grad_value = value_term if grad_value is None else grad_value + value_term
-        project_out[:, spans[2]] = grad_value.astype(BF16)
+        rows[:, spans[2]] = grad_value.astype(BF16)
         terms = (jnp.concatenate(grad_query, axis=0) * factor, grad_key * factor)
+        wait_all(load_head(head))
         for k, (term, gain) in enumerate(zip(terms, (q_gain, k_gain), strict=True)):
-            raw = heads[:, spans[k]]
+            raw = heads[head % 2, k]
             inverse = head_inverse(raw)
             normed = raw * inverse
             back = rotated(term, tables, -1)
             gain_sums[k] = gain_sums[k] + jnp.sum(back * normed, axis=0, keepdims=True)
             back = back * gain[...]
             mean = jnp.sum(back * normed, axis=-1, keepdims=True) * (1.0 / HD)
-            project_out[:, spans[k]] = (inverse * (back - normed * mean)).astype(BF16)
-        aside(counts[head])
+            rows[:, spans[k]] = (inverse * (back - normed * mean)).astype(BF16)
+        if head == count - 1:
+            pack_heads(rows, packed)
+        sums.do(*BACK_STEPS["head%d" % head])
     gains_out[...] = jnp.concatenate(gain_sums + [jnp.zeros((6, LANES), F32)], axis=0)
     loads[2].wait()
     for index in range(4):
         part = pl.ds(pl.multiple_of(row_sums.order[index] * local_rows, local_rows), local_rows)
-        row_sums.put(index, over_rows(project_out[part, :], w_qkv[...]))
-        if index == 1:
-            aside(1)
-    aside(3)
-    hidden_out[...] = row_sums.sums()
-    aside(len(todo))
-
-
-def attention_back(grad_in, lifted, given, parts, arrays, shared, small, out_shapes):
+        row_sums.put(index, over_rows(rows[part, :], w_qkv[...]))
+        sums.do(*BACK_STEPS.get("put%d" % index, ()))
+    grad_hidden = row_sums.sums()
+    values = tokens[...].astype(F32)
+    inverse = inverse_rms(values)
+    normed = values * inverse
+    tokens_out[...] = grad_middle[...] + rms_back(grad_hidden * (1.0 + scale[...]), normed, inverse)
+    width = values.shape[1]
+    mod_out[:, :width] = grad_hidden.astype(BF16)
+    mod_out[:, width:] = (grad_hidden * normed).astype(BF16)
+    sums.do(*BACK_STEPS["end"])
+    sums.end()
+
+
+def attention_back(own, parts, arrays, shared, small_shape, handed, out_shapes):
     names = tuple(arrays)
-    sums = GradSums(parts, names, [value.shape + (whole,) for value, whole in shared], small.shape)
+    shapes = [value.shape + (first, columns) for value, first, columns in shared]
+    sums = GradSums(parts, names, shapes, small_shape, {"hidden_a": "hidden_b"})
     count = len(out_shapes)
-    rows, width = grad_in.shape
-    kept, heads, w_qkv, w_out = given[:4]
+    rows, width = own[0].shape
+    kept, heads, w_qkv, w_out = own[1:5]
+    leaving = [parts[index].handed() for index in sums.leaving]
     vmem, anywhere = pl.BlockSpec(memory_space=pltpu.VMEM), pl.BlockSpec(memory_space=pl.ANY)
-
-    def kernel(*refs):
-        ins, exchanged, (small_in, grad, low), held, outs, (small_out, low_all), results, refs = split(
-            refs, len(names), len(shared), 3, len(given), count, 2, 4
-        )
-        own, scratch = split(refs, OWN_SCRATCH)
-        sums.bind(ins, exchanged, small_in, outs, small_out, scratch)
-        branch_all, project, hidden, gains = results
-        back_kernel(sums, grad, low, held, low_all, project, hidden, gains, [branch_all] + list(own))
-
     own_scratch = [
+        pltpu.VMEM((4, rows, width), BF16),
         pltpu.VMEM(kept.shape, BF16),
-        pltpu.VMEM(heads.shape, F32),
+        pltpu.VMEM((2, 2, 4 * rows, LANES), F32),
         pltpu.VMEM(w_qkv.shape, BF16),
         pltpu.VMEM(w_out.shape, BF16),
         pltpu.VMEM((4 * rows, w_out.shape[0]), BF16),
-        pltpu.SemaphoreType.DMA((4,)),
+        pltpu.VMEM((4 * rows, -(-3 * width // 4 // LANES) * LANES), BF16),
+        pltpu.SemaphoreType.DMA((7,)),
         *RowGather.scratch(),
-        *RowGather.scratch(),
-    ] + RowSums.scratch(rows, width)
+        *RowSums.scratch(rows, width),
+    ]
+
+    def kernel(*refs):
+        ins, exchanged, handed_in, given, outs, handed_out, (small_out,), results, mine, scratch = split(
+            refs,
+            len(names),
+            len(shared),
+            len(handed),
+            len(own),
+            count,
+            len(leaving),
+            1,
+            3,
+            len(own_scratch),
+        )
+        sums.bind(ins, exchanged, None, outs, small_out, handed_in, handed_out, scratch)
+        back_kernel(sums, given, results, mine)
+
     return pl.pallas_call(
         kernel,
         out_shape=[jax.ShapeDtypeStruct(shape, F32) for shape in out_shapes]
+        + [jax.ShapeDtypeStruct(shape, BF16) for shape in leaving]
         + [
-            jax.ShapeDtypeStruct((4,) + small.shape, F32),
-            jax.ShapeDtypeStruct((4, rows, width), BF16),
-            jax.ShapeDtypeStruct((4, rows, width), BF16),
-            jax.ShapeDtypeStruct(kept.shape, BF16),
+            jax.ShapeDtypeStruct((4,) + small_shape, F32),
             jax.ShapeDtypeStruct((rows, width), F32),
+            jax.ShapeDtypeStruct((rows, 2 * width), BF16),
             jax.ShapeDtypeStruct((8, LANES), F32),
         ],
-        in_specs=[anywhere] * (len(names) + len(shared)) + [vmem] * 3 + [anywhere] * 4 + [vmem] * 5,
-        out_specs=[vmem] * (count + 6),
+        in_specs=[anywhere] * (len(names) + len(shared) + len(handed))
+        + [vmem]
+        + [anywhere] * 4
+        + [vmem] * 8,
+        out_specs=[vmem] * count + [anywhere] * len(leaving) + [vmem] * 4,
         scratch_shapes=own_scratch + sums.scratch([value.shape for value in arrays.values()]),
         compiler_params=pltpu.CompilerParams(
             collective_id=BACK_ID, has_side_effects=True, vmem_limit_bytes=63 * 2**20
         ),
         name="attention_back",
-    )(*arrays.values(), *[value for value, _ in shared], small, grad_in, lifted, *given)
-
-
-OWN_SCRATCH = 18
+    )(*arrays.values(), *[value for value, _, _ in shared], *handed, *own)
 
 
 def to_owners(rows):
@@ -1348,9 +1715,15 @@
     return jnp.concatenate([jnp.zeros((8, TILE), F32), values])
 
 
+def again(part):
+    span = (part.start, part.start + part.columns)
+    kinds = {"by_rows": part.by_rows, "enter": True}
+    return Part(None, None, part.rows, span, part.out, part.order, at=part.at, **kinds)
+
+
 def bias_columns(small, tiles):
     edges = [first_tile(k, tiles) for k in range(4)] + [tiles]
-    sums = small[:, :8].reshape(4, 8 * TILE)
+    sums = small.reshape(4, -1)
     return [sums[k, : (edges[k + 1] - edges[k]) * TILE] for k in range(4)]
 
 
@@ -1431,13 +1804,24 @@
     share = 1.0 / jnp.sum(jnp.where(chosen, noise_counts, 0)).astype(F32)
 
     embed = time_embed(time_steps, width)
-    condition_in = condition[0].astype(F32) + embed
     bias_row = b_mod[None]
-    mod_first, w_qkv_lanes, modulation_first, hidden_a, lifted_low, all_positions = first_stage(
-        w_mod, w_qkv, condition[0], tokens[0], embed, bias_row, positions[:, 0]
+    share_row = jnp.full((1, width), share)
+    (
+        mod_first,
+        w_qkv_lanes,
+        scale_a,
+        gate_a,
+        gate_b,
+        hidden_a,
+        lifted_full,
+        own_branch_b,
+        lifted_low,
+        all_positions,
+    ) = first_stage(
+        w_mod, w_qkv, condition[0], tokens[0], cotangent[0], embed, share_row, bias_row, positions[:, 0]
     )
-    shift_a, scale_a = jnp.split(modulation_first, 2, axis=-1)
     hidden_a = hidden_a.reshape(patches, width)
+    lifted_full = lifted_full.reshape(patches, width)
     w_qkv_lanes = w_qkv_lanes.reshape(width, w_qkv_lanes.shape[2])
     tables = lane_tables(jnp.transpose(all_positions, (1, 0, 2)).reshape(2, patches))
     w_out_lanes = in_lanes(w_out, 0)
@@ -1450,132 +1834,151 @@
         mod_rest,
         gate_cols,
         up_cols,
-        modulation_rest,
+        scale_b,
+        middle,
+        hidden_b,
+        grads_all,
     ) = attend(
-        hidden_a, w_qkv_lanes, w_out_lanes, tables, *gain_lanes, w_mod, w_gate, w_up, lifted_low, bias_row
+        hidden_a,
+        w_qkv_lanes,
+        w_out_lanes,
+        tables,
+        *gain_lanes,
+        w_mod,
+        w_gate,
+        w_up,
+        lifted_low,
+        bias_row,
+        tokens[0],
+        gate_a,
+        own_branch_b,
     )
-    gate_a, shift_b, scale_b, gate_b = jnp.split(modulation_rest, 4, axis=-1)
+    grad_branch_b = grads_all.reshape(patches, width)
+    pieces = lax.axis_size("dp") == 8
+    ff, heads_wide, own_rows = w_down.shape[0], local_heads * HD, width // 8
+    handed_mlp = [
+        split_part("inner", "grad_branch_b", ff // 8, width, 0, 0, by_rows=True, leave=True),
+        split_part("hidden_b", "grad_gate_in", own_rows, ff, 1, 1, leave=True),
+    ]
+    handed_mlp = [handed_mlp[k % 2][k // 2] for k in range(4)] if pieces else []
+    hidden_b, inner, grad_gate_in, grad_up_in, block_out, grad_middle, own_branch_a, grad_mod_b, *handed = mlp(
+        hidden_b,
+        grads_all,
+        gate_cols,
+        up_cols,
+        w_down,
+        (middle, scale_b, gate_a, gate_b, branch_a, cotangent[0], share_row),
+        handed_mlp,
+    )
+    hidden_b = hidden_b.reshape(patches, width)
     mod_first, mod_rest = mod_first.reshape(width, -1), mod_rest.reshape(width, -1)
-    gate_cols, up_cols = gate_cols.reshape(width, -1), up_cols.reshape(width, -1)
-    tokens_f = tokens[0].astype(F32)
-    inverse_a = inverse_rms(tokens_f)
-    normed_a = tokens_f * inverse_a
-    grad_out = cotangent[0].astype(F32) * share
-    grad_branch_b = gather_rows((grad_out * gate_b).astype(BF16))
-
-    middle = tokens_f + gate_a * branch_a
-    inverse_b = inverse_rms(middle)
-    normed_b = middle * inverse_b
-    hidden_b = gather_rows((normed_b * (1.0 + scale_b) + shift_b).astype(BF16))
-    gate_in = matmul(hidden_b, gate_cols)
-    up_in = matmul(hidden_b, up_cols)
-    activated = jax.nn.silu(gate_in)
-    inner = (activated * up_in).astype(BF16)
-    branch_b = scatter_rows(matmul(inner, w_down))
-    block_out = (middle + gate_b * branch_b).astype(BF16)
-
-    grad_gate_b = grad_out * branch_b
-    grad_inner = times_transpose(grad_branch_b, w_down)
-    grad_gate_in = (grad_inner * up_in * silu_slope(gate_in)).astype(BF16)
-    grad_up_in = (grad_inner * activated).astype(BF16)
-    grad_hidden_b = scatter_rows(
-        times_transpose(grad_gate_in, gate_cols) + times_transpose(grad_up_in, up_cols)
-    )
-    grad_middle = grad_out + rms_back(grad_hidden_b * (1.0 + scale_b), normed_b, inverse_b)
-    grad_gate_a = grad_middle * branch_a
-    own_branch_a = (grad_middle * gate_a).astype(BF16)
-    grad_mod_b = jnp.concatenate(
-        [grad_hidden_b, grad_hidden_b * normed_b, grad_gate_b], axis=-1
-    ).astype(BF16)
-    wide = grad_mod_b.shape[1]
-    ff, heads_wide, own_rows = gate_cols.shape[1], local_heads * HD, width // 8
-    mod_cols = -(-wide // (4 * TILE)) * TILE
-    pieces = lax.axis_size("dp") == 8
-    parts_b, arrays_b, shared_b, shapes_b = [], {}, [], []
+    given = [rows_lanes, projected_lanes, w_qkv_lanes, w_out_lanes, *tables, *gain_lanes]
     if pieces:
+        tiles_b, tiles_a = grad_mod_b.shape[1] // TILE, 2 * width // TILE
+        mod_b, mod_a = -(-tiles_b // 4) * TILE, -(-tiles_a // 4) * TILE
+        third = mod_b // 3
+        late_a = mod_a // 2 // TILE * TILE
+        ups = split_part("hidden_b", "grad_up_in", own_rows, ff, 2, 0)
+        lasts = split_part("hidden_a", "grad_project", own_rows, 3 * heads_wide, 1, 1, leave=True)
+        mods = [
+            Part("lifted", k, own_rows, (0, third), 0, 0, at=k * third, bias=True, leave=True)
+            for k in range(3)
+        ]
+        downs, gates = handed_mlp[0::2], handed_mlp[1::2]
         parts_b = [
-            *split_part("inner", "grad_branch_b", ff // 8, width, 0, 0, by_rows=True),
-            *split_part("hidden_b", "grad_gate_in", own_rows, ff, 1, 1),
-            *split_part("hidden_b", "grad_up_in", own_rows, ff, 2, 0),
-            *split_part("lifted", 0, own_rows, mod_cols, 3, 0, bias=True),
-        ]
-        parts_b = [parts_b[k] for k in (0, 2, 1, 3, 4, 5, 6, 7)]
+            again(downs[0]),
+            again(gates[0]),
+            ups[0],
+            again(downs[1]),
+            again(gates[1]),
+            ups[1],
+            *split_part("attended", "grad_branch_a", heads_wide // 8, width, 3, 1, by_rows=True, in_lanes=True),
+            *mods,
+            *lasts,
+        ]
         arrays_b = {
-            "inner": inner,
-            "grad_branch_b": grad_branch_b,
             "hidden_b": hidden_b,
-            "grad_gate_in": grad_gate_in,
             "grad_up_in": grad_up_in,
+            "attended": attended_lanes,
+            "hidden_a": hidden_a,
+            "lifted": lifted_full,
         }
-        shared_b = [(grad_mod_b, False)]
         shapes_b = [
             (ff // 8, width),
             (own_rows // 4, 4 * ff),
             (own_rows // 4, 4 * ff),
-            (own_rows // 4, wide),
-        ]
-    given = [rows_lanes, projected_lanes, w_qkv_lanes, w_out_lanes, *tables, *gain_lanes]
-    empty = jnp.zeros((16, TILE), F32)
-    if pieces:
-        (*sums_b, small_b, lifted_full, grad_branch_a, grad_lanes, grad_hidden_a, gain_sums) = (
-            attention_back(own_branch_a, lifted_low, given, parts_b, arrays_b, shared_b, empty, shapes_b)
+            (heads_wide // 8, width),
+        ]
+        own = [own_branch_a, *given, grad_middle, tokens[0], scale_a]
+        (
+            grad_w_down,
+            grad_w_gate,
+            grad_w_up,
+            grad_w_out,
+            *handed,
+            small_b,
+            grad_tokens,
+            grad_mod_a,
+            gain_sums,
+        ) = attention_back(
+            own,
+            parts_b,
+            arrays_b,
+            [(grad_mod_b, k * third, third) for k in range(3)],
+            (16, LANES),
+            [handed[k] for k in (0, 1, 2, 3)],
+            shapes_b,
         )
-        grad_branch_a = grad_branch_a.reshape(patches, width)
-        lifted_full = lifted_full.reshape(patches, width)
-    else:
-        grad_branch_a = gather_rows(own_branch_a)
-        grad_lanes, partial, gain_sums = plain_back(grad_branch_a, given)
-        grad_hidden_a = scatter_rows(partial)
-    grad_tokens = grad_middle + rms_back(grad_hidden_a * (1.0 + scale_a), normed_a, inverse_a)
-    grad_mod_a = jnp.concatenate(
-        [grad_hidden_a, grad_hidden_a * normed_a, grad_gate_a], axis=-1
-    ).astype(BF16)
-    first = mod_first.shape[1]
-    grad_condition = (
-        times_transpose(grad_mod_a[:, :first], mod_first)
-        + times_transpose(
-            jnp.concatenate([grad_mod_a[:, first:], grad_mod_b], axis=1), mod_rest
+        parts_a = [again(part) for part in mods + lasts]
+        spans = ((0, mod_a - late_a), (mod_a - late_a, mod_a))
+        parts_a += [
+            Part("lifted", k, own_rows, (0, span[1] - span[0]), 2, 0, at=span[0], bias=True)
+            for k, span in enumerate(spans)
+        ]
+        shapes_a = [
+            (own_rows // 4, tiles_b * TILE),
+            (4, own_rows // 4, 3 * heads_wide),
+            (own_rows // 4, tiles_a * TILE),
+        ]
+        sum_b, qkv_sum, sum_a, small_a, grad_condition = last_grads(
+            parts_a,
+            {"lifted": lifted_full},
+            [(grad_mod_a, span[0], span[1] - span[0]) for span in spans],
+            padded_small(gain_sums[:2]),
+            handed,
+            shapes_a,
+            condition[0],
+            embed,
+            grad_mod_a,
+            grad_mod_b,
+            [mod_first, mod_rest],
         )
-    ) * silu_slope(condition_in)
-    grad_project = out_of_lanes(grad_lanes).reshape(patches, 3 * heads_wide)
-    gain_sums = gain_sums[:2, :HD]
-    if pieces:
-        parts_a = [
-            *split_part("hidden_a", "grad_project", own_rows, 3 * heads_wide, 0, 0),
-            Part(
-                "attended", "grad_branch_a", heads_wide // 8, (0, width), 1, 1, by_rows=True, in_lanes=True
-            ),
-            *split_part("lifted", 0, own_rows, mod_cols, 2, 0, bias=True),
-        ]
-        parts_a = [parts_a[k] for k in (0, 2, 1, 3, 4)]
-        arrays_a = {
-            "hidden_a": hidden_a,
-            "grad_project": grad_project,
-            "attended": attended_lanes,
-            "grad_branch_a": grad_branch_a,
-            "lifted": lifted_full,
-        }
-        shapes_a = [
-            (4, own_rows // 4, 3 * heads_wide),
-            (heads_wide // 8, width),
-            (own_rows // 4, wide),
-        ]
-        qkv_sum, grad_w_out, mod_a, small_a = weight_grads(
-            parts_a, arrays_a, [(grad_mod_a, False)], padded_small(gain_sums), shapes_a
-        )
-        grad_w_down, grad_w_gate, grad_w_up, mod_b = sums_b
         grad_w_qkv = jnp.transpose(
             qkv_sum.reshape(4, own_rows // 4, 3, heads_wide), (1, 2, 0, 3)
         ).reshape(own_rows // 4, 3 * width)
-        grad_w_mod = jnp.concatenate([mod_a, mod_b], axis=1)
-        tiles = wide // TILE
-        bias = jnp.concatenate(bias_columns(small_a, tiles) + bias_columns(small_b, tiles))
+        grad_w_mod = jnp.concatenate([sum_a, sum_b], axis=1)
+        bias = jnp.concatenate(bias_columns(small_a, tiles_a) + bias_columns(small_b, tiles_b))
         own_bias = bias.shape[0] // (8 * ways)
         sum_bias = lax.dynamic_slice(
             bias, ((item * ways + lax.axis_index("seq")) * own_bias,), (own_bias,)
         )
         gains = jnp.sum(small_a[:, 8:10, :HD], axis=0)
     else:
+        tokens_f = tokens[0].astype(F32)
+        inverse_a = inverse_rms(tokens_f)
+        normed_a = tokens_f * inverse_a
+        grad_branch_a = gather_rows(own_branch_a)
+        grad_lanes, partial, gain_sums = plain_back(grad_branch_a, given)
+        grad_hidden_a = scatter_rows(partial)
+        grad_tokens = grad_middle + rms_back(grad_hidden_a * (1.0 + scale_a), normed_a, inverse_a)
+        grad_mod_a = jnp.concatenate([grad_hidden_a, grad_hidden_a * normed_a], axis=-1).astype(BF16)
+        grad_mod_first = jnp.concatenate([grad_mod_a, grad_mod_b[:, :width], grad_mod_b[:, 3 * width :]], axis=1)
+        grad_condition = (
+            times_transpose(grad_mod_first, mod_first)
+            + times_transpose(grad_mod_b[:, width : 3 * width], mod_rest)
+        ) * silu_slope(condition[0].astype(F32) + embed)
+        grad_project = out_of_lanes(grad_lanes).reshape(patches, 3 * heads_wide)
+        gain_sums = gain_sums[:2, :HD]
         mod_rows = jnp.concatenate([grad_mod_a, grad_mod_b], axis=1)
         grad_w_down = plain_sums(inner, grad_branch_b, 0)
         grad_w_gate = plain_sums(hidden_b, grad_gate_in, 1)
@@ -1583,7 +1986,7 @@
         grad_w_qkv = plain_sums(hidden_a, grad_project, 3)
         attended = out_of_lanes(attended_lanes).reshape(patches, heads_wide)
         grad_w_out = plain_sums(attended, grad_branch_a, 0)
-        grad_w_mod = plain_sums(gather_rows(lifted_low), rows_to_columns(mod_rows, 6), 6)
+        grad_w_mod = plain_sums(lifted_full, rows_to_columns(mod_rows, 6), 6)
         bias_rows = jnp.sum(mod_rows, axis=0, dtype=F32)
         sum_bias = lax.psum_scatter(bias_rows, ("dp", "seq"), scatter_dimension=0, tiled=True)
         gains = lax.psum(gain_sums, ("dp", "seq"))

time: 485 us -> 399 us (0.82)
  matrix products: 33.3 us -> 0 us
  Pallas kernels: 392 us -> 361 us
  other arithmetic: 25.1 us -> 11.4 us
  local copies, waits for them, and re-layouts: 26.4 us -> 18.1 us
    dot_general x8 -> x0, matrix products: 33.3 us -> none  [the longest x5 23.4 us: times_transpose(): return jnp.einsum('rb,ab->ra', left, right, preferred_element_type=F32)]
    pallas_call x6 -> x3, Pallas kernels: 202 us -> 187 us  [the longest x1 66 us: first_stage(): pl.pallas_call(kernel, out_shape=[jax.ShapeDtypeStruct((4, depth, 4 * wid...]
    pallas_call x1, Pallas kernels: 68.4 us -> 56.7 us  [attend(): pl.pallas_call(kernel, out_shape=[jax.ShapeDtypeStruct((patches, wide * 2...]
where the time goes in v4:
time: 399 us; the launch traced here: 393 us
  Pallas kernels  361 us (90%)
  local copies, waits for them, and re-layouts  18.1 us (5%)
  other arithmetic  11.4 us (3%)
    pallas_call x1, Pallas kernels, attention_back(): pl.pallas_call(kernel, out_shape=[jax.ShapeDtypeStruct(shape, F32) for sh...  117 us
    pallas_call x1, Pallas kernels, first_stage(): pl.pallas_call(kernel, out_shape=[jax.ShapeDtypeStruct((4, depth, 4 * wid...  66 us
    pallas_call x1, Pallas kernels, last_grads(): pl.pallas_call(kernel, out_shape=[jax.ShapeDtypeStruct(shape, F32) for sh...  63.7 us
    pallas_call x1, Pallas kernels, mlp(): pl.pallas_call(kernel, out_shape=[jax.ShapeDtypeStruct((4, rows, width),...  57.1 us
    pallas_call x1, Pallas kernels, attend(): pl.pallas_call(kernel, out_shape=[jax.ShapeDtypeStruct((patches, wide * 2...  56.7 us
    unnamed x43, local copies, waits for them, and re-layouts  8.08 us

profile of v4, /device:TPU:0, one launch (start us, length us, event | category | flops | bytes accessed | tf_op | source)
XLA Modules:
  0.0 392.8 jit_solution(8474027535246752541)
XLA Ops:
  1.3 0.1 fusion.2
  1.4 0.7 pad_maximum_fusion.2.refs_5_.refs_12_
  2.1 0.8 reduce-window.9
  2.9 0.6 fusion.4
  3.5 1.9 fusion.5
  6.2 0.6 broadcast_in_dim.56.refs_6_.refs_11_
  6.8 1.4 broadcast_in_dim.57.refs_7_.refs_12_
  8.1 1.3 copy.39
  9.4 66.0 %first_stage.1 = (bf16[4,288,4608]{2,1,0:T(8,128)(2,1)}, bf16[4,288,1536]{2,1,0:T(8,128)(2,1)}, f32[256,1152]{1,0:T(8,128)}, f32[256,1152]{1,0:T(8,128)}, f32[25...) custom-call(bf16[288,6912]{1,0:T(8,128)(2,1)} %refs_8_.1, ...), custom_call_target="tpu_custom_call" | custom-call | tf_op jit(solution)/shard_map/first_stage/pallas_call | solution.py:572
  75.4 0.8 slice_convert_fusion.1
  76.2 0.3 broadcast_multiply_fusion.1
  76.6 2.3 broadcast_select_fusion
  78.9 0.0 copy-start.11
  78.9 0.0 copy-start.12
  79.0 0.0 copy-start.2
  79.0 0.8 pad.27.refs_3_.refs_17_
  79.8 0.8 pad.28.refs_4_.refs_18_
  80.6 0.8 pad.29.refs_5_.refs_19_
  81.5 0.0 copy-done.12
  81.5 0.5 pad_bitcast_fusion
  82.0 1.1 pad.26
  83.1 56.7 %attend.1 = (f32[1024,1024]{1,0:T(8,128)}, bf16[1024,1536]{1,0:T(8,128)(2,1)}, bf16[1024,512]{1,0:T(8,128)(2,1)}, f32[256,1152]{1,0:T(8,128)}, bf16[4,288,2304]{...) custom-call(bf16[1024,1152]{1,0:T(8,128)(2,1)} %bitcast.50, ...), custom_call_target="tpu_custom_call" | custom-call | tf_op jit(solution)/shard_map/attend/pallas_call | solution.py:801
  139.8 57.1 %mlp.1 = (bf16[4,256,1152]{2,1,0:T(8,128)(2,1)}, bf16[1024,768]{1,0:T(8,128)(2,1)}, bf16[1024,768]{1,0:T(8,128)(2,1)}, bf16[1024,768]{1,0:T(8,128)(2,1)}, bf16[2...) custom-call(bf16[256,1152]{1,0:T(8,128)(2,1)} %get-tuple-element.67., ...), custom_call_target="tpu_custom_call" | custom-call | tf_op jit(solution)/shard_map/mlp/pallas_call | solution.py:966
  196.9 0.0 copy-start.10
  196.9 117.4 %attention_back.1 = (f32[96,1152]{1,0:T(8,128)}, f32[36,3072]{1,0:T(8,128)}, f32[36,3072]{1,0:T(8,128)}, f32[36,1152]{1,0:T(8,128)}, bf16[2,2,144,384]{3,2,1,0:T...) custom-call(bf16[1024,1152]{1,0:T(8,128)(2,1)} %bitcast.57, ...), custom_call_target="tpu_custom_call" | custom-call | tf_op jit(solution)/shard_map/attention_back/pallas_call | solution.py:1676
  314.3 0.8 broadcast_select_fusion.1
  315.1 0.6 concatenate.17.refs_10_
  315.7 63.7 %last_grads.1 = (f32[36,4608]{1,0:T(8,128)}, f32[4,36,864]{2,1,0:T(8,128)}, f32[36,2304]{1,0:T(8,128)}, f32[4,16,128]{2,1,0:T(8,128)}, f32[256,1152]{1,0:T(8,128)}) custom-call(bf16[1024,1152]{1,0:T(8,128)(2,1)} %bitcast.49, bf16[256,2304]{1,0:T(8,128)(2,1)} %get-tuple-element.91.refs_1_.refs_2_.refs_13_, ...), custom_call_target="tpu_custom_call" | custom-call | tf_op jit(solution)/shard_map/last_grads/pallas_call | solution.py:1482
  379.4 0.8 copy.38
  380.3 0.1 slice_reduce_fusion
  380.5 0.6 dynamic_slice.3
  381.1 2.3 pad_maximum_fusion
  383.4 0.0 copy-done.4
  383.4 0.1 copy.29
  383.5 0.6 reshape.169
  384.1 0.2 copy.30
  384.3 1.2 reshape.170
  385.5 0.7 slice_reduce_fusion.4
  386.2 0.5 slice_bitcast_fusion
  386.7 0.8 copy.56
  387.5 0.0 copy-done
  387.5 1.0 copy.57
  388.6 1.0 copy.58
  389.6 0.0 copy-done.8
  389.6 0.7 copy.59
  390.3 0.8 copy.60
  391.1 0.8 copy.61
  391.9 0.8 copy.62
  (32 shorter events, 0.2 us)
Async XLA Ops:
  78.9 2.5 copy-start.11
  78.9 2.5 copy-start.12
  79.0 3.0 copy-start.2
  196.9 117.4 %copy-start.10 = (pred[8]{0:T(512)(128)(4,1)S(1)}, pred[8]{0:T(512)(128)(4,1)}, u32[]{:S(2)}) copy-start(pred[8]{0:T(512)(128)(4,1)} %constant.60.clone.1) | copy-start | bytes 28
  315.7 64.6 %copy-start.9 = (f32[4,16,128]{2,1,0:T(8,128)S(1)}, f32[4,16,128]{2,1,0:T(8,128)}, u32[]{:S(2)}) copy-start(f32[4,16,128]{2,1,0:T(8,128)} %get-tuple-element.109) | copy-start | bytes 98308
  379.4 4.0 %copy-start.4 = (f32[4,36,864]{2,1,0:T(8,128)S(1)}, f32[4,36,864]{2,1,0:T(8,128)}, u32[]{:S(2)}) copy-start(f32[4,36,864]{2,1,0:T(8,128)} %get-tuple-element.101) | copy-start | bytes 1492996
  384.1 2.6 copy-start.3
  384.3 3.3 copy-start
  386.7 1.8 copy-start.1
  388.5 1.1 copy-start.8
  388.5 1.7 copy-start.6
  388.5 2.5 copy-start.5
  389.6 2.2 copy-start.7

commit v5 on v4

--- a/solution.py
+++ b/solution.py
@@ -609,11 +609,13 @@
 
 
 def lane_tables(positions):
-    cosine, sine = rope_tables(positions, HD)
-    cosine, sine = cosine[:, 0], sine[:, 0]
-    takes_ahead = (jnp.arange(HD) // QUARTER % 2 == 0)[None, :]
-    tables = (cosine, jnp.where(takes_ahead, -sine, 0.0), jnp.where(takes_ahead, 0.0, sine))
-    return [jnp.pad(table, ((0, 0), (0, LANES - HD))) for table in tables]
+    lane = jnp.arange(LANES)[None, :]
+    frequency = jnp.exp(-math.log(10000.0) * (lane % QUARTER).astype(F32) / QUARTER)
+    places = jnp.where(lane < 2 * QUARTER, positions[0][:, None], positions[1][:, None])
+    angles = places.astype(F32) * frequency
+    valid, takes_ahead = lane < HD, lane // QUARTER % 2 == 0
+    cosine, sine = jnp.where(valid, jnp.cos(angles), 0.0), jnp.where(valid, jnp.sin(angles), 0.0)
+    return [cosine, jnp.where(takes_ahead, -sine, 0.0), jnp.where(takes_ahead, 0.0, sine)]
 
 
 def head_inverse(values):
@@ -1426,11 +1428,11 @@
 
 LAST_STEPS = (
     ("b0", "b1", "b2", "b3", "b4"),
-    ("s0", "s3", "s1"),
-    ("b5", "s4", "t0", "s2"),
-    ("t3", "b6", "t1", "f5"),
-    ("t4", "l0", "l3", "t2", "x0", "l1"),
-    ("f6", "x1", "l4", "s5", "l2", "x2", "t5", "x3", "s6", "l5", "t6", "x4", "l6"),
+    ("s0", "b5"),
+    ("s1",),
+    ("b6", "f3", "s2", "t0", "t1"),
+    ("f4", "t2", "s3", "x0", "l0", "l1"),
+    ("l2", "s4", "x1", "f5", "t3", "x2", "t4", "f6", "l3", "s5", "x3", "l4", "s6", "t5", "t6", "x4", "l5", "l6"),
 )
 
 
@@ -1509,15 +1511,14 @@
 
 
 BACK_STEPS = {
-    "start": ("b0", "b1", "b2", "b3", "b4", "b5", "r3", "s1", "s0", "s3", "t1"),
-    "gathered": ("b6", "b7"),
-    "head0": ("f2", "l1", "t0", "t3"),
-    "head1": ("s2", "s4", "f5", "f6", "l0", "l3"),
-    "head2": ("f7", "t4", "b8", "s5"),
-    "head3": ("b11", "b12", "t2", "l4", "b9"),
-    "put1": ("b10", "s6", "s7", "x0"),
-    "put3": ("t5", "f8", "l2", "x1", "t6", "t7", "l5", "f11", "x2"),
-    "end": ("f9", "x3", "l6", "l7", "f12", "f10", "x4"),
+    "start": ("b0", "b1", "b2", "b3", "b4", "b5"),
+    "gathered": ("b6", "b7", "s1", "s0", "s3"),
+    "head0": ("b8", "s4", "f2"),
+    "head1": ("b9", "f5", "f6", "f7", "s2", "t1", "t0", "t3"),
+    "head2": ("b10", "s5", "f8", "t4"),
+    "head3": ("s6", "s7", "f9", "t2", "x0"),
+    "put3": ("t5", "x1", "t6", "t7", "f10", "x2", "l0", "l1", "l3", "l4"),
+    "end": ("x3", "l2", "l5", "l6", "l7", "x4"),
 }
 
 
@@ -1538,8 +1539,8 @@
 def back_kernel(sums, own, outs, refs):
     grad_in, rows_in, heads_in, w_qkv_in, w_out_in, cosine, ahead, behind, q_gain, k_gain = own[:10]
     grad_middle, tokens, scale = own[10:]
-    tokens_out, mod_out, gains_out = outs
-    (branch_all, rows, heads, w_qkv, w_out, grad_heads, packed, load_sem), refs = refs[:8], refs[8:]
+    tokens_out, mod_out, gains_out, packed = outs
+    (branch_all, rows, heads, w_qkv, w_out, grad_heads, load_sem), refs = refs[:7], refs[7:]
     gather = RowGather(grad_in, branch_all, *refs[:3])
     row_sums = RowSums(*refs[3:])
     local_rows = grad_in.shape[0]
@@ -1571,7 +1572,6 @@
     sums.share()
     sums.small[0] = jnp.zeros_like(sums.small[0])
     sums.others["grad_branch_a"] = (branch_all, lambda: None)
-    sums.others["grad_project"] = (packed, lambda: None)
     sums.do(*BACK_STEPS["start"])
     gather.pass_on()
     gather.end()
@@ -1638,7 +1638,7 @@
 def attention_back(own, parts, arrays, shared, small_shape, handed, out_shapes):
     names = tuple(arrays)
     shapes = [value.shape + (first, columns) for value, first, columns in shared]
-    sums = GradSums(parts, names, shapes, small_shape, {"hidden_a": "hidden_b"})
+    sums = GradSums(parts, names, shapes, small_shape)
     count = len(out_shapes)
     rows, width = own[0].shape
     kept, heads, w_qkv, w_out = own[1:5]
@@ -1651,7 +1651,6 @@
         pltpu.VMEM(w_qkv.shape, BF16),
         pltpu.VMEM(w_out.shape, BF16),
         pltpu.VMEM((4 * rows, w_out.shape[0]), BF16),
-        pltpu.VMEM((4 * rows, -(-3 * width // 4 // LANES) * LANES), BF16),
         pltpu.SemaphoreType.DMA((7,)),
         *RowGather.scratch(),
         *RowSums.scratch(rows, width),
@@ -1667,7 +1666,7 @@
             count,
             len(leaving),
             1,
-            3,
+            4,
             len(own_scratch),
         )
         sums.bind(ins, exchanged, None, outs, small_out, handed_in, handed_out, scratch)
@@ -1682,12 +1681,13 @@
             jax.ShapeDtypeStruct((rows, width), F32),
             jax.ShapeDtypeStruct((rows, 2 * width), BF16),
             jax.ShapeDtypeStruct((8, LANES), F32),
+            jax.ShapeDtypeStruct((4 * rows, -(-3 * width // 4 // LANES) * LANES), BF16),
         ],
         in_specs=[anywhere] * (len(names) + len(shared) + len(handed))
         + [vmem]
         + [anywhere] * 4
         + [vmem] * 8,
-        out_specs=[vmem] * count + [anywhere] * len(leaving) + [vmem] * 4,
+        out_specs=[vmem] * count + [anywhere] * len(leaving) + [vmem] * 5,
         scratch_shapes=own_scratch + sums.scratch([value.shape for value in arrays.values()]),
         compiler_params=pltpu.CompilerParams(
             collective_id=BACK_ID, has_side_effects=True, vmem_limit_bytes=63 * 2**20
@@ -1798,7 +1798,8 @@
     patches = local_rows * ways
     local_heads = HEADS // ways
     item = lax.axis_index("dp")
-    running = jnp.cumsum(noise_counts)
+    image = jnp.arange(noise_counts.shape[0], dtype=jnp.int32)
+    running = jnp.sum(jnp.where(image[None, :] <= image[:, None], noise_counts[None, :], 0), axis=1)
     image_id = jnp.sum((running <= item).astype(jnp.int32))
     chosen = jnp.arange(noise_counts.shape[0], dtype=jnp.int32) == image_id
     share = 1.0 / jnp.sum(jnp.where(chosen, noise_counts, 0)).astype(F32)
@@ -1879,7 +1880,7 @@
         third = mod_b // 3
         late_a = mod_a // 2 // TILE * TILE
         ups = split_part("hidden_b", "grad_up_in", own_rows, ff, 2, 0)
-        lasts = split_part("hidden_a", "grad_project", own_rows, 3 * heads_wide, 1, 1, leave=True)
+        lasts = split_part("hidden_a", "grad_project", own_rows, 3 * heads_wide, 1, 0)
         mods = [
             Part("lifted", k, own_rows, (0, third), 0, 0, at=k * third, bias=True, leave=True)
             for k in range(3)
@@ -1894,13 +1895,11 @@
             ups[1],
             *split_part("attended", "grad_branch_a", heads_wide // 8, width, 3, 1, by_rows=True, in_lanes=True),
             *mods,
-            *lasts,
         ]
         arrays_b = {
             "hidden_b": hidden_b,
             "grad_up_in": grad_up_in,
             "attended": attended_lanes,
-            "hidden_a": hidden_a,
             "lifted": lifted_full,
         }
         shapes_b = [
@@ -1920,6 +1919,7 @@
             grad_tokens,
             grad_mod_a,
             gain_sums,
+            grad_project,
         ) = attention_back(
             own,
             parts_b,
@@ -1929,7 +1929,7 @@
             [handed[k] for k in (0, 1, 2, 3)],
             shapes_b,
         )
-        parts_a = [again(part) for part in mods + lasts]
+        parts_a = [again(part) for part in mods] + lasts
         spans = ((0, mod_a - late_a), (mod_a - late_a, mod_a))
         parts_a += [
             Part("lifted", k, own_rows, (0, span[1] - span[0]), 2, 0, at=span[0], bias=True)
@@ -1942,7 +1942,7 @@
         ]
         sum_b, qkv_sum, sum_a, small_a, grad_condition = last_grads(
             parts_a,
-            {"lifted": lifted_full},
+            {"hidden_a": hidden_a, "grad_project": grad_project, "lifted": lifted_full},
             [(grad_mod_a, span[0], span[1] - span[0]) for span in spans],
             padded_small(gain_sums[:2]),
             handed,

time: 399 us -> 383 us (0.960)
  Pallas kernels: 361 us -> 347 us
    pallas_call x1, Pallas kernels: 117 us -> 95.3 us  [attention_back(): pl.pallas_call(kernel, out_shape=[jax.ShapeDtypeStruct(shape, F32) for sh...]
    pallas_call x1, Pallas kernels: 63.7 us -> 71.9 us  [last_grads(): pl.pallas_call(kernel, out_shape=[jax.ShapeDtypeStruct(shape, F32) for sh...]
where the time goes in v5:
time: 383 us; the launch traced here: 377 us
  Pallas kernels  347 us (91%)
  local copies, waits for them, and re-layouts  16.4 us (4%)
  other arithmetic  11.1 us (3%)
    pallas_call x1, Pallas kernels, attention_back(): pl.pallas_call(kernel, out_shape=[jax.ShapeDtypeStruct(shape, F32) for sh...  95.3 us
    pallas_call x1, Pallas kernels, last_grads(): pl.pallas_call(kernel, out_shape=[jax.ShapeDtypeStruct(shape, F32) for sh...  71.9 us
    pallas_call x1, Pallas kernels, first_stage(): pl.pallas_call(kernel, out_shape=[jax.ShapeDtypeStruct((4, depth, 4 * wid...  66 us
    pallas_call x1, Pallas kernels, mlp(): pl.pallas_call(kernel, out_shape=[jax.ShapeDtypeStruct((4, rows, width),...  57.1 us
    pallas_call x1, Pallas kernels, attend(): pl.pallas_call(kernel, out_shape=[jax.ShapeDtypeStruct((patches, wide * 2...  56.7 us
    unnamed x43, local copies, waits for them, and re-layouts  8.08 us

profile of v5, /device:TPU:0, one launch (start us, length us, event | category | flops | bytes accessed | tf_op | source)
XLA Modules:
  0.0 377.2 jit_solution(3788814655507882209)
XLA Ops:
  1.3 0.1 fusion.1
  1.4 0.7 pad_maximum_fusion.1.refs_5_.refs_12_
  2.1 0.8 select_reduce_fusion
  2.8 0.6 fusion.3
  3.5 1.9 fusion.4
  6.1 0.6 broadcast_in_dim.109.refs_6_.refs_11_
  6.7 1.4 broadcast_in_dim.110.refs_7_.refs_12_
  8.1 1.3 copy.41
  9.3 66.0 %first_stage.1 = (bf16[4,288,4608]{2,1,0:T(8,128)(2,1)}, bf16[4,288,1536]{2,1,0:T(8,128)(2,1)}, f32[256,1152]{1,0:T(8,128)}, f32[256,1152]{1,0:T(8,128)}, f32[25...) custom-call(bf16[288,6912]{1,0:T(8,128)(2,1)} %refs_8_.1, ...), custom_call_target="tpu_custom_call" | custom-call | tf_op jit(solution)/shard_map/first_stage/pallas_call | solution.py:572
  75.4 0.0 copy-start.11
  75.4 0.0 copy-start.12
  75.4 0.0 copy-start.2
  75.4 0.8 fusion.11
  76.3 3.2 fusion
  79.5 0.0 copy-done.11
  79.5 0.0 copy-done.12
  79.5 0.5 pad_bitcast_fusion
  80.0 0.0 copy-done.2
  80.0 1.1 pad.16
  81.1 56.7 %attend.1 = (f32[1024,1024]{1,0:T(8,128)}, bf16[1024,1536]{1,0:T(8,128)(2,1)}, bf16[1024,512]{1,0:T(8,128)(2,1)}, f32[256,1152]{1,0:T(8,128)}, bf16[4,288,2304]{...) custom-call(bf16[1024,1152]{1,0:T(8,128)(2,1)} %bitcast.47, ...), custom_call_target="tpu_custom_call" | custom-call | tf_op jit(solution)/shard_map/attend/pallas_call | solution.py:803
  137.8 57.1 %mlp.1 = (bf16[4,256,1152]{2,1,0:T(8,128)(2,1)}, bf16[1024,768]{1,0:T(8,128)(2,1)}, bf16[1024,768]{1,0:T(8,128)(2,1)}, bf16[1024,768]{1,0:T(8,128)(2,1)}, bf16[2...) custom-call(bf16[256,1152]{1,0:T(8,128)(2,1)} %get-tuple-element.66., ...), custom_call_target="tpu_custom_call" | custom-call | tf_op jit(solution)/shard_map/mlp/pallas_call | solution.py:968
  194.9 0.0 copy-start.10
  195.0 95.3 %attention_back.1 = (f32[96,1152]{1,0:T(8,128)}, f32[36,3072]{1,0:T(8,128)}, f32[36,3072]{1,0:T(8,128)}, f32[36,1152]{1,0:T(8,128)}, bf16[2,2,144,384]{3,2,1,0:T...) custom-call(bf16[1024,1152]{1,0:T(8,128)(2,1)} %bitcast.56, ...), custom_call_target="tpu_custom_call" | custom-call | tf_op jit(solution)/shard_map/attention_back/pallas_call | solution.py:1675
  290.3 0.0 copy-done.10
  290.3 0.8 broadcast_select_fusion
  291.0 0.6 concatenate.13.refs_10_
  291.6 71.9 %last_grads.1 = (f32[36,4608]{1,0:T(8,128)}, f32[4,36,864]{2,1,0:T(8,128)}, f32[36,2304]{1,0:T(8,128)}, f32[4,16,128]{2,1,0:T(8,128)}, f32[256,1152]{1,0:T(8,128)}) custom-call(bf16[1024,1152]{1,0:T(8,128)(2,1)} %bitcast.48, bf16[1024,896]{1,0:T(8,128)(2,1)} %get-tuple-element.90.refs_1_, bf16[1024,1152]{1,0:T(8,128)(2,1)} %bitcast.50, ...), custom_call_target="tpu_custom_call" | custom-call | tf_op jit(solution)/shard_map/last_grads/pallas_call | solution.py:1484
  363.5 0.0 copy-start.4
  363.5 0.8 copy.40
  364.5 0.0 copy-done.9
  364.5 0.1 slice_reduce_fusion
  364.6 0.6 dynamic_slice.3
  365.3 2.3 pad_maximum_fusion
  367.6 0.1 copy.31
  367.7 0.6 reshape.173
  368.3 0.2 copy.32
  368.4 0.0 copy-start
  368.4 1.2 reshape.174
  369.6 0.7 slice_reduce_fusion.4
  370.3 0.5 slice_bitcast_fusion
  370.9 0.8 copy.58
  371.7 1.0 copy.59
  372.7 1.0 copy.60
  373.7 0.0 copy-done.8
  373.8 0.7 copy.61
  374.4 0.8 copy.62
  375.2 0.8 copy.63
  376.0 0.8 copy.64
  (29 shorter events, 0.2 us)
Async XLA Ops:
  75.4 4.1 %copy-start.11 = (f32[72]{0:T(128)S(1)}, f32[72]{0:T(128)}, u32[]{:S(2)}) copy-start(f32[72]{0:T(128)} %param.26) | copy-start | bytes 868
  75.4 4.1 %copy-start.12 = (f32[72]{0:T(128)S(1)}, f32[72]{0:T(128)}, u32[]{:S(2)}) copy-start(f32[72]{0:T(128)} %param.25) | copy-start | bytes 868
  75.4 4.6 %copy-start.2 = (bf16[288,1152]{1,0:T(8,128)(2,1)S(1)}, bf16[288,1152]{1,0:T(8,128)(2,1)}, u32[]{:S(2)}) copy-start(bf16[288,1152]{1,0:T(8,128)(2,1)} %param.19) | copy-start | bytes 1990660
  194.9 95.3 %copy-start.10 = (pred[8]{0:T(512)(128)(4,1)S(1)}, pred[8]{0:T(512)(128)(4,1)}, u32[]{:S(2)}) copy-start(pred[8]{0:T(512)(128)(4,1)} %constant.67.clone.1) | copy-start | bytes 28
  291.6 72.8 %copy-start.9 = (f32[4,16,128]{2,1,0:T(8,128)S(1)}, f32[4,16,128]{2,1,0:T(8,128)}, u32[]{:S(2)}) copy-start(f32[4,16,128]{2,1,0:T(8,128)} %get-tuple-element.107) | copy-start | bytes 98308
  363.5 4.0 %copy-start.4 = (f32[4,36,864]{2,1,0:T(8,128)S(1)}, f32[4,36,864]{2,1,0:T(8,128)}, u32[]{:S(2)}) copy-start(f32[4,36,864]{2,1,0:T(8,128)} %get-tuple-element.99) | copy-start | bytes 1492996
  368.2 2.6 copy-start.3
  368.4 3.3 copy-start
  370.9 1.8 copy-start.1
  372.7 1.1 copy-start.8
  372.7 1.7 copy-start.6
  372.7 2.5 copy-start.5
  373.8 2.2 copy-start.7

commit v6 on v5

--- a/solution.py
+++ b/solution.py
@@ -337,17 +337,10 @@
             for k, (source, target) in enumerate(self.spans(array, self.column))
         ]
 
-    def steps(self):
-        count = len(self.blocks)
-        todo = []
-        for step in range(count + 3):
-            if step < count:
-                todo.append(lambda step=step: self.arrive(step))
-            if 0 <= step - 1 < count:
-                todo.append(lambda step=step: self.pass_on(step - 1))
-            if 0 <= step - 2 < count:
-                todo.append(lambda step=step: self.complete(step - 2))
-        return todo
+    def do(self, *steps):
+        kinds = {"a": self.arrive, "p": self.pass_on, "c": self.complete}
+        for step in steps:
+            kinds[step[0]](int(step[1:]))
 
     def arrive(self, step):
         self.over(step).wait_recv()
@@ -473,14 +466,18 @@
         copy.wait()
 
 
+def row_of(ref, start, columns):
+    rows = range(start // LANES, (start + columns) // LANES)
+    return jnp.concatenate([ref[row : row + 1, :] for row in rows], axis=1)
+
+
 def first_kernel(imports, *refs):
     (w_mod, w_qkv, condition, tokens, cotangent, embed, share, bias, positions), refs = refs[:9], refs[9:]
     (mod_out, qkv_out, scale_a, gate_a, gate_b), refs = refs[:5], refs[5:]
-    (hidden_all, lifted_all, grads, lifted, positions_all), refs = refs[:5], refs[5:]
+    (hidden_all, grads, lifted, positions_all), refs = refs[:4], refs[4:]
     (mod_all, lanes, hidden, mod_sem, spot_send, spot_recv), refs = refs[:6], refs[6:]
     imports.bind({0: w_mod, 1: lanes}, {0: mod_all, 1: qkv_out}, refs[:3])
     gather = RowGather(hidden, hidden_all, *refs[3:6])
-    gather_lifted = RowGather(lifted, lifted_all, *refs[6:9])
     item, column = lax.axis_index("dp"), lax.axis_index("seq")
     width = tokens.shape[1]
     greet(imports.partners())
@@ -523,7 +520,7 @@
         modulation = jnp.dot(lifted[...], weights, preferred_element_type=F32)
         return [
             modulation[:, k * width : (k + 1) * width]
-            + bias[:, pl.ds(imports.source_column(start + k * width), width)]
+            + row_of(bias, imports.source_column(start + k * width), width)
             for k in range(2)
         ]
 
@@ -533,7 +530,6 @@
     normed = values * inverse_rms(values)
     hidden[...] = (normed * (1.0 + scale) + shift).astype(BF16)
     gather.start()
-    gather_lifted.start()
     imports.pass_on(1)
     imports.arrive(2)
     imports.complete(1)
@@ -548,14 +544,12 @@
     gather.pass_on()
     imports.complete(2)
     imports.complete(3)
-    gather_lifted.pass_on()
     imports.end()
     for copy in imports.beside(0):
         copy.wait_send()
     wait_all(imports.beside(1))
     wait_all(imports.own(1))
     gather.end()
-    gather_lifted.end()
     wait_all(spot_copies)
     store.wait()
 
@@ -578,13 +572,12 @@
             jax.ShapeDtypeStruct((rows, width), F32),
             jax.ShapeDtypeStruct((rows, width), F32),
             jax.ShapeDtypeStruct((4, rows, width), BF16),
-            jax.ShapeDtypeStruct((4, rows, width), BF16),
             jax.ShapeDtypeStruct((rows, width), BF16),
             jax.ShapeDtypeStruct((rows, width), BF16),
             jax.ShapeDtypeStruct((4,) + positions.shape, jnp.int32),
         ],
         in_specs=[anywhere] + [vmem] * 8,
-        out_specs=[anywhere, anywhere] + [vmem] * 8,
+        out_specs=[anywhere, anywhere] + [vmem] * 7,
         scratch_shapes=[
             pltpu.VMEM((4, depth, 4 * width), BF16),
             pltpu.VMEM((4, depth, lanes), BF16),
@@ -594,7 +587,7 @@
             pltpu.SemaphoreType.DMA((3,)),
         ]
         + imports.scratch()
-        + RowGather.scratch() * 2,
+        + RowGather.scratch(),
         compiler_params=pltpu.CompilerParams(
             collective_id=WEIGHT_ID, has_side_effects=True, vmem_limit_bytes=60 * 2**20
         ),
@@ -691,6 +684,15 @@
             pltpu.SemaphoreType.DMA((3,)),
             pltpu.SemaphoreType.DMA((3,)),
         ]
+
+
+IMPORT_STEPS = (
+    ("a0",),
+    ("a1", "a2", "p0"),
+    ("a3", "a4", "c0", "p1"),
+    ("p2", "p3", "c1"),
+    ("p4", "c2", "c3", "c4"),
+)
 
 
 def attend_kernel(imports, *refs):
@@ -719,12 +721,6 @@
     for array in imports.arrays:
         start_all(imports.beside(array))
     gather.start()
-    todo = imports.steps()
-
-    def aside(number):
-        for _ in range(min(number, len(todo))):
-            todo.pop(0)()
-
     factor = HD ** (-0.5)
     rows = branch_out.shape[0]
     heads = attended_out.shape[1] // LANES
@@ -742,7 +738,7 @@
             values = values * head_inverse(values) * gain
             start = pair * 2 * LANES + half * LANES
             rows_out[:, start : start + LANES] = rotated(values, tables, 1).astype(BF16)
-    aside(1)
+    imports.do(*IMPORT_STEPS[0])
     for copy in loads:
         copy.wait()
     for copy in stores:
@@ -760,7 +756,7 @@
             )
             attended_out[block, spans[0]] = mixed.astype(BF16)
         sums.put(index, jnp.dot(attended_out[block, :], w_out[...], preferred_element_type=F32))
-        aside((1, 3, 4, len(todo))[index])
+        imports.do(*IMPORT_STEPS[1 + index])
     gather.pass_on()
     wait_all(imports.own(0))
     for copy in imports.beside(0):
@@ -771,7 +767,7 @@
     width = tokens.shape[1]
     weights = mod_all[...].reshape(-1, 2 * width)
     modulation = jnp.dot(lifted[...], weights, preferred_element_type=F32)
-    modulation = modulation + bias[:, pl.ds(imports.source_column(0), 2 * width)]
+    modulation = modulation + row_of(bias, imports.source_column(0), 2 * width)
     scale = modulation[:, width:]
     scale_out[...] = scale
     branch = sums.sums()
@@ -1428,11 +1424,11 @@
 
 LAST_STEPS = (
     ("b0", "b1", "b2", "b3", "b4"),
-    ("s0", "b5"),
-    ("s1",),
-    ("b6", "f3", "s2", "t0", "t1"),
-    ("f4", "t2", "s3", "x0", "l0", "l1"),
-    ("l2", "s4", "x1", "f5", "t3", "x2", "t4", "f6", "l3", "s5", "x3", "l4", "s6", "t5", "t6", "x4", "l5", "l6"),
+    ("b5",),
+    ("b6", "s0", "s1"),
+    ("s2", "f3"),
+    ("f4", "s3", "x0", "t0", "t1", "t2"),
+    ("s4", "f5", "x1", "f6", "s5", "x2", "t3", "s6", "x3", "t4", "l0", "l1", "l2", "t5", "t6", "l3", "l4", "l5", "l6", "x4"),
 )
 
 
@@ -1513,12 +1509,12 @@
 BACK_STEPS = {
     "start": ("b0", "b1", "b2", "b3", "b4", "b5"),
     "gathered": ("b6", "b7", "s1", "s0", "s3"),
-    "head0": ("b8", "s4", "f2"),
-    "head1": ("b9", "f5", "f6", "f7", "s2", "t1", "t0", "t3"),
-    "head2": ("b10", "s5", "f8", "t4"),
-    "head3": ("s6", "s7", "f9", "t2", "x0"),
-    "put3": ("t5", "x1", "t6", "t7", "f10", "x2", "l0", "l1", "l3", "l4"),
-    "end": ("x3", "l2", "l5", "l6", "l7", "x4"),
+    "head0": ("s4", "f2"),
+    "head1": ("b8", "f5", "f6", "f7", "s2", "t1", "t0", "t3"),
+    "head2": ("b9", "s5", "t4"),
+    "head3": ("b10", "s6", "s7", "f8", "t2", "x0"),
+    "put3": ("t5", "x1", "t6", "t7", "f9", "x2", "l0", "l1", "l3", "l4"),
+    "end": ("f10", "x3", "l2", "l5", "l6", "l7", "x4"),
 }
 
 
@@ -1538,11 +1534,12 @@
 
 def back_kernel(sums, own, outs, refs):
     grad_in, rows_in, heads_in, w_qkv_in, w_out_in, cosine, ahead, behind, q_gain, k_gain = own[:10]
-    grad_middle, tokens, scale = own[10:]
-    tokens_out, mod_out, gains_out, packed = outs
+    grad_middle, tokens, scale, lifted = own[10:]
+    tokens_out, mod_out, gains_out, packed, lifted_all = outs
     (branch_all, rows, heads, w_qkv, w_out, grad_heads, load_sem), refs = refs[:7], refs[7:]
     gather = RowGather(grad_in, branch_all, *refs[:3])
-    row_sums = RowSums(*refs[3:])
+    gather_lifted = RowGather(lifted, lifted_all, *refs[3:6])
+    row_sums = RowSums(*refs[6:])
     local_rows = grad_in.shape[0]
     count = grad_heads.shape[1] // LANES
     factor = HD ** (-0.5)
@@ -1569,9 +1566,11 @@
     sums.load()
     sums.greet()
     gather.start()
+    gather_lifted.start()
     sums.share()
     sums.small[0] = jnp.zeros_like(sums.small[0])
     sums.others["grad_branch_a"] = (branch_all, lambda: None)
+    sums.others["lifted"] = (lifted_all, gather_lifted.end)
     sums.do(*BACK_STEPS["start"])
     gather.pass_on()
     gather.end()
@@ -1616,6 +1615,8 @@
             rows[:, spans[k]] = (inverse * (back - normed * mean)).astype(BF16)
         if head == count - 1:
             pack_heads(rows, packed)
+        if head == 0:
+            gather_lifted.pass_on()
         sums.do(*BACK_STEPS["head%d" % head])
     gains_out[...] = jnp.concatenate(gain_sums + [jnp.zeros((6, LANES), F32)], axis=0)
     loads[2].wait()
@@ -1653,6 +1654,7 @@
         pltpu.VMEM((4 * rows, w_out.shape[0]), BF16),
         pltpu.SemaphoreType.DMA((7,)),
         *RowGather.scratch(),
+        *RowGather.scratch(),
         *RowSums.scratch(rows, width),
     ]
 
@@ -1666,7 +1668,7 @@
             count,
             len(leaving),
             1,
-            4,
+            5,
             len(own_scratch),
         )
         sums.bind(ins, exchanged, None, outs, small_out, handed_in, handed_out, scratch)
@@ -1682,12 +1684,13 @@
             jax.ShapeDtypeStruct((rows, 2 * width), BF16),
             jax.ShapeDtypeStruct((8, LANES), F32),
             jax.ShapeDtypeStruct((4 * rows, -(-3 * width // 4 // LANES) * LANES), BF16),
+            jax.ShapeDtypeStruct((4, rows, width), BF16),
         ],
         in_specs=[anywhere] * (len(names) + len(shared) + len(handed))
         + [vmem]
         + [anywhere] * 4
-        + [vmem] * 8,
-        out_specs=[vmem] * count + [anywhere] * len(leaving) + [vmem] * 5,
+        + [vmem] * 9,
+        out_specs=[vmem] * count + [anywhere] * len(leaving) + [vmem] * 6,
         scratch_shapes=own_scratch + sums.scratch([value.shape for value in arrays.values()]),
         compiler_params=pltpu.CompilerParams(
             collective_id=BACK_ID, has_side_effects=True, vmem_limit_bytes=63 * 2**20
@@ -1805,7 +1808,7 @@
     share = 1.0 / jnp.sum(jnp.where(chosen, noise_counts, 0)).astype(F32)
 
     embed = time_embed(time_steps, width)
-    bias_row = b_mod[None]
+    bias_row = b_mod.reshape(-1, LANES)
     share_row = jnp.full((1, width), share)
     (
         mod_first,
@@ -1814,17 +1817,15 @@
         gate_a,
         gate_b,
         hidden_a,
-        lifted_full,
         own_branch_b,
         lifted_low,
         all_positions,
     ) = first_stage(
-        w_mod, w_qkv, condition[0], tokens[0], cotangent[0], embed, share_row, bias_row, positions[:, 0]
+        w_mod, w_qkv, condition[0], tokens[0], cotangent[0], embed, share_row, bias_row, positions
     )
     hidden_a = hidden_a.reshape(patches, width)
-    lifted_full = lifted_full.reshape(patches, width)
     w_qkv_lanes = w_qkv_lanes.reshape(width, w_qkv_lanes.shape[2])
-    tables = lane_tables(jnp.transpose(all_positions, (1, 0, 2)).reshape(2, patches))
+    tables = lane_tables(jnp.transpose(all_positions[:, :, 0], (1, 0, 2)).reshape(2, patches))
     w_out_lanes = in_lanes(w_out, 0)
     gain_lanes = [jnp.pad(gain, (0, LANES - HD))[None] for gain in (q_gain, k_gain)]
     (
@@ -1900,7 +1901,6 @@
             "hidden_b": hidden_b,
             "grad_up_in": grad_up_in,
             "attended": attended_lanes,
-            "lifted": lifted_full,
         }
         shapes_b = [
             (ff // 8, width),
@@ -1908,7 +1908,7 @@
             (own_rows // 4, 4 * ff),
             (heads_wide // 8, width),
         ]
-        own = [own_branch_a, *given, grad_middle, tokens[0], scale_a]
+        own = [own_branch_a, *given, grad_middle, tokens[0], scale_a, lifted_low]
         (
             grad_w_down,
             grad_w_gate,
@@ -1920,6 +1920,7 @@
             grad_mod_a,
             gain_sums,
             grad_project,
+            lifted_full,
         ) = attention_back(
             own,
             parts_b,
@@ -1929,6 +1930,7 @@
             [handed[k] for k in (0, 1, 2, 3)],
             shapes_b,
         )
+        lifted_full = lifted_full.reshape(patches, width)
         parts_a = [again(part) for part in mods] + lasts
         spans = ((0, mod_a - late_a), (mod_a - late_a, mod_a))
         parts_a += [
@@ -1986,7 +1988,7 @@
         grad_w_qkv = plain_sums(hidden_a, grad_project, 3)
         attended = out_of_lanes(attended_lanes).reshape(patches, heads_wide)
         grad_w_out = plain_sums(attended, grad_branch_a, 0)
-        grad_w_mod = plain_sums(lifted_full, rows_to_columns(mod_rows, 6), 6)
+        grad_w_mod = plain_sums(gather_rows(lifted_low), rows_to_columns(mod_rows, 6), 6)
         bias_rows = jnp.sum(mod_rows, axis=0, dtype=F32)
         sum_bias = lax.psum_scatter(bias_rows, ("dp", "seq"), scatter_dimension=0, tiled=True)
         gains = lax.psum(gain_sums, ("dp", "seq"))

time: 383 us -> 377 us (0.984)
    pallas_call x1, Pallas kernels: 66 us -> 58.8 us  [first_stage(): pl.pallas_call(kernel, out_shape=[jax.ShapeDtypeStruct((4, depth, 4 * wid...]
where the time goes in v6:
time: 377 us; the launch traced here: 371 us
  Pallas kernels  344 us (91%)
  local copies, waits for them, and re-layouts  13.7 us (4%)
  other arithmetic  11.1 us (3%)
    pallas_call x1, Pallas kernels, attention_back(): pl.pallas_call(kernel, out_shape=[jax.ShapeDtypeStruct(shape, F32) for sh...  98 us
    pallas_call x1, Pallas kernels, last_grads(): pl.pallas_call(kernel, out_shape=[jax.ShapeDtypeStruct(shape, F32) for sh...  72.9 us
    pallas_call x1, Pallas kernels, first_stage(): pl.pallas_call(kernel, out_shape=[jax.ShapeDtypeStruct((4, depth, 4 * wid...  58.8 us
    pallas_call x1, Pallas kernels, mlp(): pl.pallas_call(kernel, out_shape=[jax.ShapeDtypeStruct((4, rows, width),...  57.4 us
    pallas_call x1, Pallas kernels, attend(): pl.pallas_call(kernel, out_shape=[jax.ShapeDtypeStruct((patches, wide * 2...  57 us
    unnamed x43, local copies, waits for them, and re-layouts  7.59 us

profile of v6, /device:TPU:0, one launch (start us, length us, event | category | flops | bytes accessed | tf_op | source)
XLA Modules:
  0.0 371.5 jit_solution(5772628118929501156)
XLA Ops:
  1.3 0.1 fusion.1
  1.4 0.7 pad_maximum_fusion.1.refs_5_.refs_12_
  2.1 0.8 select_reduce_fusion
  2.8 0.6 fusion.3
  3.5 1.9 fusion.4
  6.1 0.6 broadcast_in_dim.106.refs_6_.refs_11_
  6.7 58.8 %first_stage.1 = (bf16[4,288,4608]{2,1,0:T(8,128)(2,1)}, bf16[4,288,1536]{2,1,0:T(8,128)(2,1)}, f32[256,1152]{1,0:T(8,128)}, f32[256,1152]{1,0:T(8,128)}, f32[25...) custom-call(bf16[288,6912]{1,0:T(8,128)(2,1)} %refs_8_.3, ...), custom_call_target="tpu_custom_call" | custom-call | tf_op jit(solution)/shard_map/first_stage/pallas_call | solution.py:566
  65.5 0.0 copy-start.11
  65.6 0.0 copy-start.12
  65.6 0.0 copy-start.2
  65.6 0.8 copy.41
  66.4 3.2 fusion
  69.6 0.0 copy-done.11
  69.6 0.0 copy-done.12
  69.6 0.5 pad_bitcast_fusion
  70.1 0.0 copy-done.2
  70.1 1.1 pad.16
  71.2 57.0 %attend.1 = (f32[1024,1024]{1,0:T(8,128)}, bf16[1024,1536]{1,0:T(8,128)(2,1)}, bf16[1024,512]{1,0:T(8,128)(2,1)}, f32[256,1152]{1,0:T(8,128)}, bf16[4,288,2304]{...) custom-call(bf16[1024,1152]{1,0:T(8,128)(2,1)} %bitcast.49, ...), custom_call_target="tpu_custom_call" | custom-call | tf_op jit(solution)/shard_map/attend/pallas_call | solution.py:799
  128.2 57.4 %mlp.1 = (bf16[4,256,1152]{2,1,0:T(8,128)(2,1)}, bf16[1024,768]{1,0:T(8,128)(2,1)}, bf16[1024,768]{1,0:T(8,128)(2,1)}, bf16[1024,768]{1,0:T(8,128)(2,1)}, bf16[2...) custom-call(bf16[256,1152]{1,0:T(8,128)(2,1)} %get-tuple-element.66., ...), custom_call_target="tpu_custom_call" | custom-call | tf_op jit(solution)/shard_map/mlp/pallas_call | solution.py:964
  185.7 0.0 copy-start.10
  185.7 98.0 %attention_back.1 = (f32[96,1152]{1,0:T(8,128)}, f32[36,3072]{1,0:T(8,128)}, f32[36,3072]{1,0:T(8,128)}, f32[36,1152]{1,0:T(8,128)}, bf16[2,2,144,384]{3,2,1,0:T...) custom-call(bf16[1024,1152]{1,0:T(8,128)(2,1)} %bitcast.57, ...), custom_call_target="tpu_custom_call" | custom-call | tf_op jit(solution)/shard_map/attention_back/pallas_call | solution.py:1677
  283.7 0.0 copy-done.10
  283.7 0.8 broadcast_select_fusion
  284.5 0.6 concatenate.13.refs_10_
  285.1 72.9 %last_grads.1 = (f32[36,4608]{1,0:T(8,128)}, f32[4,36,864]{2,1,0:T(8,128)}, f32[36,2304]{1,0:T(8,128)}, f32[4,16,128]{2,1,0:T(8,128)}, f32[256,1152]{1,0:T(8,128)}) custom-call(bf16[1024,1152]{1,0:T(8,128)(2,1)} %bitcast.50, bf16[1024,896]{1,0:T(8,128)(2,1)} %get-tuple-element.89.refs_1_, bf16[1024,1152]{1,0:T(8,128)(2,1)} %bitcast.56, ...), custom_call_target="tpu_custom_call" | custom-call | tf_op jit(solution)/shard_map/last_grads/pallas_call | solution.py:1480
  358.0 0.0 copy-start.4
  358.0 0.8 copy.40
  358.9 0.0 copy-done.9
  359.0 0.1 slice_reduce_fusion
  359.1 0.6 dynamic_slice.3
  359.7 2.3 pad_maximum_fusion
  362.0 0.0 copy-done.4
  362.0 0.1 copy.31
  362.2 0.6 reshape.177
  362.7 0.2 copy.32
  362.9 0.0 copy-start
  362.9 1.2 reshape.178
  364.1 0.7 slice_reduce_fusion.4
  364.8 0.5 slice_bitcast_fusion
  365.3 0.0 copy-done.3
  365.3 0.8 copy.58
  366.2 1.0 copy.59
  367.2 1.0 copy.60
  368.2 0.0 copy-done.8
  368.2 0.7 copy.61
  368.9 0.8 copy.62
  369.7 0.8 copy.63
  370.5 0.8 copy.64
  (28 shorter events, 0.2 us)
Async XLA Ops:
  65.5 4.1 %copy-start.11 = (f32[72]{0:T(128)S(1)}, f32[72]{0:T(128)}, u32[]{:S(2)}) copy-start(f32[72]{0:T(128)} %param.26) | copy-start | bytes 868
  65.6 4.1 %copy-start.12 = (f32[72]{0:T(128)S(1)}, f32[72]{0:T(128)}, u32[]{:S(2)}) copy-start(f32[72]{0:T(128)} %param.25) | copy-start | bytes 868
  65.6 4.6 %copy-start.2 = (bf16[288,1152]{1,0:T(8,128)(2,1)S(1)}, bf16[288,1152]{1,0:T(8,128)(2,1)}, u32[]{:S(2)}) copy-start(bf16[288,1152]{1,0:T(8,128)(2,1)} %param.19) | copy-start | bytes 1990660
  185.7 98.1 %copy-start.10 = (pred[8]{0:T(512)(128)(4,1)S(1)}, pred[8]{0:T(512)(128)(4,1)}, u32[]{:S(2)}) copy-start(pred[8]{0:T(512)(128)(4,1)} %constant.67.clone.1) | copy-start | bytes 28
  285.1 73.9 %copy-start.9 = (f32[4,16,128]{2,1,0:T(8,128)S(1)}, f32[4,16,128]{2,1,0:T(8,128)}, u32[]{:S(2)}) copy-start(f32[4,16,128]{2,1,0:T(8,128)} %get-tuple-element.107) | copy-start | bytes 98308
  358.0 4.0 %copy-start.4 = (f32[4,36,864]{2,1,0:T(8,128)S(1)}, f32[4,36,864]{2,1,0:T(8,128)}, u32[]{:S(2)}) copy-start(f32[4,36,864]{2,1,0:T(8,128)} %get-tuple-element.99) | copy-start | bytes 1492996
  362.7 2.6 copy-start.3
  362.9 3.3 copy-start
  365.3 1.8 copy-start.1
  367.2 1.1 copy-start.8
  367.2 1.7 copy-start.6
  367.2 2.5 copy-start.5
  368.2 2.2 copy-start.7

commit v7 on v6

--- a/solution.py
+++ b/solution.py
@@ -1023,6 +1023,7 @@
         self.order = order
         for kind in ("by_rows", "in_lanes", "bias", "enter", "leave"):
             setattr(self, kind, kinds.get(kind, False))
+        self.region = kinds.get("region")
         self.slab = padded_rows(rows)
 
     def handed(self):
@@ -1354,13 +1355,13 @@
         for copy in self.last(index):
             copy.wait()
         rows = part.rows // 4
-        wide = out.shape[-1]
+        base, wide = part.region or (0, out.shape[-1])
         for k in range(4):
             values = self.slab_in[index][k].astype(F32)[:rows]
             if len(out.shape) == 3:
                 out[k, :, part.at : stop] = values
             else:
-                start = first_tile(k, wide // TILE) * TILE
+                start = base + first_tile(k, wide // TILE) * TILE
                 out[:, start + part.at : start + stop] = values
 
     def small_step(self, step):
@@ -1718,9 +1719,9 @@
     return jnp.concatenate([jnp.zeros((8, TILE), F32), values])
 
 
-def again(part):
+def again(part, region=None):
     span = (part.start, part.start + part.columns)
-    kinds = {"by_rows": part.by_rows, "enter": True}
+    kinds = {"by_rows": part.by_rows, "enter": True, "region": region}
     return Part(None, None, part.rows, span, part.out, part.order, at=part.at, **kinds)
 
 
@@ -1931,18 +1932,18 @@
             shapes_b,
         )
         lifted_full = lifted_full.reshape(patches, width)
-        parts_a = [again(part) for part in mods] + lasts
+        wide_a, wide_b = tiles_a * TILE, tiles_b * TILE
+        parts_a = [again(part, (wide_a, wide_b)) for part in mods] + lasts
         spans = ((0, mod_a - late_a), (mod_a - late_a, mod_a))
         parts_a += [
-            Part("lifted", k, own_rows, (0, span[1] - span[0]), 2, 0, at=span[0], bias=True)
+            Part("lifted", k, own_rows, (0, span[1] - span[0]), 0, 0, at=span[0], bias=True, region=(0, wide_a))
             for k, span in enumerate(spans)
         ]
         shapes_a = [
-            (own_rows // 4, tiles_b * TILE),
+            (own_rows // 4, wide_a + wide_b),
             (4, own_rows // 4, 3 * heads_wide),
-            (own_rows // 4, tiles_a * TILE),
-        ]
-        sum_b, qkv_sum, sum_a, small_a, grad_condition = last_grads(
+        ]
+        grad_w_mod, qkv_sum, small_a, grad_condition = last_grads(
             parts_a,
             {"hidden_a": hidden_a, "grad_project": grad_project, "lifted": lifted_full},
             [(grad_mod_a, span[0], span[1] - span[0]) for span in spans],
@@ -1958,7 +1959,6 @@
         grad_w_qkv = jnp.transpose(
             qkv_sum.reshape(4, own_rows // 4, 3, heads_wide), (1, 2, 0, 3)
         ).reshape(own_rows // 4, 3 * width)
-        grad_w_mod = jnp.concatenate([sum_a, sum_b], axis=1)
         bias = jnp.concatenate(bias_columns(small_a, tiles_a) + bias_columns(small_b, tiles_b))
         own_bias = bias.shape[0] // (8 * ways)
         sum_bias = lax.dynamic_slice(

time: 377 us -> 377 us (level)
    unnamed x43 -> x44, local copies, waits for them, and re-layouts: 7.59 us -> 8.48 us
where the time goes in v7:
time: 377 us; the launch traced here: 371 us
  Pallas kernels  344 us (91%)
  local copies, waits for them, and re-layouts  15.7 us (4%)
  other arithmetic  8.83 us (2%)
    pallas_call x1, Pallas kernels, attention_back(): pl.pallas_call(kernel, out_shape=[jax.ShapeDtypeStruct(shape, F32) for sh...  98 us
    pallas_call x1, Pallas kernels, last_grads(): pl.pallas_call(kernel, out_shape=[jax.ShapeDtypeStruct(shape, F32) for sh...  72.9 us
    pallas_call x1, Pallas kernels, first_stage(): pl.pallas_call(kernel, out_shape=[jax.ShapeDtypeStruct((4, depth, 4 * wid...  58.9 us
    pallas_call x1, Pallas kernels, mlp(): pl.pallas_call(kernel, out_shape=[jax.ShapeDtypeStruct((4, rows, width),...  57.4 us
    pallas_call x1, Pallas kernels, attend(): pl.pallas_call(kernel, out_shape=[jax.ShapeDtypeStruct((patches, wide * 2...  57 us
    unnamed x44, local copies, waits for them, and re-layouts  8.48 us

profile of v7, /device:TPU:0, one launch (start us, length us, event | category | flops | bytes accessed | tf_op | source)
XLA Modules:
  0.0 371.1 jit_solution(6842390191961879538)
XLA Ops:
  1.3 0.1 fusion.1
  1.4 0.7 pad_maximum_fusion.refs_5_.refs_12_
  2.1 0.8 select_reduce_fusion
  2.8 0.6 fusion.3
  3.5 1.9 fusion.4
  6.1 0.6 broadcast_in_dim.106.refs_6_.refs_11_
  6.7 58.9 %first_stage.1 = (bf16[4,288,4608]{2,1,0:T(8,128)(2,1)}, bf16[4,288,1536]{2,1,0:T(8,128)(2,1)}, f32[256,1152]{1,0:T(8,128)}, f32[256,1152]{1,0:T(8,128)}, f32[25...) custom-call(bf16[288,6912]{1,0:T(8,128)(2,1)} %refs_8_.3, ...), custom_call_target="tpu_custom_call" | custom-call | tf_op jit(solution)/shard_map/first_stage/pallas_call | solution.py:566
  65.6 0.0 copy-start.3
  65.6 0.8 copy.41
  66.4 3.2 fusion
  69.6 0.0 copy-done.11
  69.6 0.0 copy-done.12
  69.6 0.5 pad_bitcast_fusion
  70.1 0.0 copy-done.3
  70.1 1.1 pad.16
  71.2 57.0 %attend.1 = (f32[1024,1024]{1,0:T(8,128)}, bf16[1024,1536]{1,0:T(8,128)(2,1)}, bf16[1024,512]{1,0:T(8,128)(2,1)}, f32[256,1152]{1,0:T(8,128)}, bf16[4,288,2304]{...) custom-call(bf16[1024,1152]{1,0:T(8,128)(2,1)} %bitcast.49, ...), custom_call_target="tpu_custom_call" | custom-call | tf_op jit(solution)/shard_map/attend/pallas_call | solution.py:799
  128.2 57.4 %mlp.1 = (bf16[4,256,1152]{2,1,0:T(8,128)(2,1)}, bf16[1024,768]{1,0:T(8,128)(2,1)}, bf16[1024,768]{1,0:T(8,128)(2,1)}, bf16[1024,768]{1,0:T(8,128)(2,1)}, bf16[2...) custom-call(bf16[256,1152]{1,0:T(8,128)(2,1)} %get-tuple-element.65., ...), custom_call_target="tpu_custom_call" | custom-call | tf_op jit(solution)/shard_map/mlp/pallas_call | solution.py:964
  185.6 0.0 copy-start.10
  185.7 98.0 %attention_back.1 = (f32[96,1152]{1,0:T(8,128)}, f32[36,3072]{1,0:T(8,128)}, f32[36,3072]{1,0:T(8,128)}, f32[36,1152]{1,0:T(8,128)}, bf16[2,2,144,384]{3,2,1,0:T...) custom-call(bf16[1024,1152]{1,0:T(8,128)(2,1)} %bitcast.57, ...), custom_call_target="tpu_custom_call" | custom-call | tf_op jit(solution)/shard_map/attention_back/pallas_call | solution.py:1678
  283.7 0.0 copy-done.10
  283.7 0.7 broadcast_select_fusion
  284.5 0.6 concatenate.10.refs_10_
  285.1 72.9 %last_grads.1 = (f32[36,6912]{1,0:T(8,128)}, f32[4,36,864]{2,1,0:T(8,128)}, f32[4,16,128]{2,1,0:T(8,128)}, f32[256,1152]{1,0:T(8,128)}) custom-call(bf16[1024,1152]{1,0:T(8,128)(2,1)} %bitcast.50, bf16[1024,896]{1,0:T(8,128)(2,1)} %get-tuple-element.88.refs_1_, bf16[1024,1152]{1,0:T(8,128)(2,1)} %bitcast.56, ...), custom_call_target="tpu_custom_call" | custom-call | tf_op jit(solution)/shard_map/last_grads/pallas_call | solution.py:1481
  358.0 0.8 copy.40
  358.9 0.0 copy-done.9
  358.9 0.1 slice_reduce_fusion
  359.0 0.6 dynamic_slice.3
  359.7 1.2 copy.31
  360.9 0.0 copy-start.4
  360.9 0.6 reshape.177
  361.4 0.2 copy.32
  361.6 1.2 reshape.178
  362.8 0.7 slice_reduce_fusion.4
  363.5 0.5 slice_bitcast_fusion
  364.0 0.0 copy-done.4
  364.0 0.8 copy.59
  364.9 0.0 copy-done
  364.9 1.0 copy.60
  365.9 0.0 copy-start.7
  365.9 1.0 copy.61
  366.9 0.0 copy-done.8
  366.9 0.7 copy.62
  367.6 0.8 copy.63
  368.4 0.0 copy-done.5
  368.4 0.8 copy.64
  369.2 0.0 copy-done.7
  369.2 0.8 copy.65
  369.9 1.0 copy.66
  (28 shorter events, 0.2 us)
Async XLA Ops:
  6.7 62.9 %copy-start.11 = (f32[72]{0:T(128)S(1)}, f32[72]{0:T(128)}, u32[]{:S(2)}) copy-start(f32[72]{0:T(128)} %param.26) | copy-start | bytes 868
  6.7 62.9 %copy-start.12 = (f32[72]{0:T(128)S(1)}, f32[72]{0:T(128)}, u32[]{:S(2)}) copy-start(f32[72]{0:T(128)} %param.25) | copy-start | bytes 868
  65.6 4.6 %copy-start.3 = (bf16[288,1152]{1,0:T(8,128)(2,1)S(1)}, bf16[288,1152]{1,0:T(8,128)(2,1)}, u32[]{:S(2)}) copy-start(bf16[288,1152]{1,0:T(8,128)(2,1)} %param.19) | copy-start | bytes 1990660
  185.6 98.1 %copy-start.10 = (pred[8]{0:T(512)(128)(4,1)S(1)}, pred[8]{0:T(512)(128)(4,1)}, u32[]{:S(2)}) copy-start(pred[8]{0:T(512)(128)(4,1)} %constant.67.clone.1) | copy-start | bytes 28
  285.1 73.8 %copy-start.9 = (f32[4,16,128]{2,1,0:T(8,128)S(1)}, f32[4,16,128]{2,1,0:T(8,128)}, u32[]{:S(2)}) copy-start(f32[4,16,128]{2,1,0:T(8,128)} %get-tuple-element.105) | copy-start | bytes 98308
  360.9 3.2 copy-start.4
  361.4 3.4 copy-start
  364.0 1.8 copy-start.1
  365.9 1.0 copy-start.8
  365.9 1.7 copy-start.6
  365.9 2.5 copy-start.5
  365.9 3.3 copy-start.7
  366.9 3.0 copy-start.2
